TPU v7x, 32 devices: a whole 2x2x4 slice. The times are simulated.
32 devices in a mesh: height: 8 (over z, x), cols: 4 (over y, core).
Axes of the slice: x: 2, y: 2, z: 4, core: 2. Of those that a mesh axis runs over, the one named last changes fastest.
Arguments:
- positions: float32 [3, 16, 32, 128], P(None, 'height', 'cols'), may hold values from -0.5 to 0.5
- velocities: float32 [3, 16, 32, 128], P(None, 'height', 'cols'), may hold values from -3 to 3
- contacts: int32 [9, 16, 32], P(None, 'height', 'cols'), may hold values 0 or 1
- exit_flags: int32 [16, 32], P('height', 'cols'), may hold values from 0 to 1, as said below
- inlet_slots: int32 [8, 32], P('height', 'cols'), may hold values from 0 to 7, as said below
- cell_blocks: int32 [16, 32], P('height', 'cols'), may hold values from 0 to 511
- cell_slots: int32 [16, 32, 128], P('height', 'cols'), may hold values from 0 to 127
- gas_source: float32 [16, 256, 512], P('height', 'cols'), may hold values from -12 to 12
- diagonal: float32 [16, 256, 512], P('height', 'cols'), may hold values from 0.25 to 2
Outputs:
- positions_out: float32 [3, 16, 32, 128], P(None, 'height', 'cols')
- velocities_out: float32 [3, 16, 32, 128], P(None, 'height', 'cols')
- pressure: float32 [16, 256, 512], P('height', 'cols')
- residual: float32 [16, 256, 512], P('height', 'cols')
Inputs may be any that keep to these rules, and one draw needn't show every extreme that they name: `exit_flags`: only the top tile row of each device's 2 tile rows holds ones; at most 8 ones on one device, exactly 8 on some device. `inlet_slots`: each device's 8 entries are a permutation of 0 to 7.
All inputs are finite; a program needn't handle non-finite values. No bound on the sum of `contacts` on one device may be relied on, other than what follows from the above.
Results may differ from a plain program's by a relative error of at most 0.0003.
Values sent between devices are 32-bit elements; how exact they have to be, the bound alone decides.
No kernel may reach another device: no remote copies, remote signals or barrier semaphores. Data moves between devices by JAX's collectives and lax.ppermute only.
A program may use at most 64 MiB of HBM per device.

v0:
```python
import jax
import jax.numpy as jnp
from jax import lax
from jax.sharding import PartitionSpec as P

ITERS = 2


spring = 0.05
cutoff_sq = 1.44
damping = 0.5
step_dt = 0.05
gravity = 1.0
deposit_gain = 2.0
highest = lax.Precision.HIGHEST


def padded_2(block, sides, width):
    for axis, dim in sides:
        count = lax.axis_size(axis)
        forward = [(i, i + 1) for i in range(count - 1)]
        backward = [(target, source) for source, target in forward]
        low = lax.ppermute(
            lax.slice_in_dim(block, block.shape[dim] - width, None, axis=dim), axis, forward
        )
        high = lax.ppermute(lax.slice_in_dim(block, 0, width, axis=dim), axis, backward)
        block = jnp.concatenate([low, block, high], axis=dim)
    return block


def shifted(value, axis, steps):
    count = lax.axis_size(axis)
    pairs = [(source, (source + steps) % count) for source in range(count)]
    return lax.ppermute(value, axis, pairs)


def row_forces(window, flags):
    width = flags.shape[1]
    centre = window[:, 1, 1 : width + 1, :]
    places = centre[0:3]
    moving = places - damping * centre[3:6]
    own_sq = jnp.sum(places * places, axis=0)
    total = jnp.zeros(places.shape, jnp.float32)
    for row_step in range(3):
        for col_step in range(3):
            other = window[:, row_step, col_step : col_step + width, :]
            offset = jnp.array([col_step - 1.0, 0.0, row_step - 1.0], jnp.float32)[:, None, None]
            other_places = other[0:3] + offset
            cross = jnp.einsum("cip,ciq->ipq", places, other_places, precision=highest)
            other_sq = jnp.sum(other_places * other_places, axis=0)
            dist_sq = own_sq[:, :, None] + other_sq[:, None, :] - 2.0 * cross
            active = flags[row_step * 3 + col_step].astype(jnp.float32)
            weight = spring * jnp.maximum(1.0 - dist_sq / cutoff_sq, 0.0) * active[:, None, None]
            pulled = jnp.einsum(
                "ipq,ciq->cip", weight, other_places - damping * other[3:6], precision=highest
            )
            total = total + moving * jnp.sum(weight, axis=2)[None] - pulled
    return total


def tile_forces(extended, flags):
    count = flags.shape[1]

    def one_row(index):
        window = lax.dynamic_slice_in_dim(extended, index, 3, 1)
        row_flags = lax.dynamic_slice_in_dim(flags, index, 1, 1)[:, 0]
        return row_forces(window, row_flags)

    stacked = lax.map(one_row, jnp.arange(count, dtype=jnp.int32))
    return jnp.transpose(stacked, (1, 0, 2, 3))


def advance(state, forces):
    upward = jnp.array([0.0, 0.0, 1.0], jnp.float32)[:, None, None, None]
    speeds = state[3:6] + step_dt * forces - step_dt * gravity * upward
    places = state[0:3] + step_dt * speeds
    return jnp.concatenate([places, speeds], axis=0)


def operate(field, diagonal):
    padded = padded_2(field, (("height", 0), ("cols", 1)), 1)
    padded = jnp.pad(padded, ((0, 0), (0, 0), (1, 1)))
    beside_all = padded[2:, 1:-1, 1:-1] + padded[:-2, 1:-1, 1:-1]
    beside_all = beside_all + padded[1:-1, 2:, 1:-1] + padded[1:-1, :-2, 1:-1]
    beside_all = beside_all + padded[1:-1, 1:-1, 2:] + padded[1:-1, 1:-1, :-2]
    return (6.0 + diagonal) * field - beside_all


def paired_sums(residual, precond, image):
    return lax.psum((jnp.sum(residual * precond), jnp.sum(precond * image)), ("height", "cols"))


def on_device(
    positions,
    velocities,
    contacts,
    exit_flags,
    inlet_slots,
    cell_blocks,
    cell_slots,
    gas_source,
    diagonal,
):
    state = jnp.concatenate([positions, velocities], axis=0)
    tile_rows = state.shape[1]
    tile_cols = state.shape[2]
    parts = state.shape[3]
    for repeat in range(2):
        extended = padded_2(state, (("height", 1), ("cols", 2)), 1)
        state = advance(state, tile_forces(extended, contacts))
    settled = state
    flat_flags = exit_flags.reshape(-1)
    tiles = settled.reshape(6, tile_rows * tile_cols, parts)
    ranks = jnp.cumsum(flat_flags) - 1
    buffer_ids = jnp.arange(tile_cols, dtype=jnp.int32)
    picker = ((ranks[None, :] == buffer_ids[:, None]) & (flat_flags[None, :] > 0)).astype(
        jnp.float32
    )
    outgoing = jnp.einsum("kt,ctp->ckp", picker, tiles, precision=highest)
    kept = tiles * (1 - flat_flags).astype(jnp.float32)[None, :, None]
    arrived = shifted(outgoing, "height", 1)
    placing = (inlet_slots[0][None, :] == buffer_ids[:, None]).astype(jnp.float32)
    bottom = jnp.einsum("jk,ckp->cjp", placing, arrived, precision=highest)
    tiles = jnp.concatenate([bottom, kept[:, tile_cols:, :]], axis=1)
    state = tiles.reshape(6, tile_rows, tile_cols, parts)
    lifting = deposit_gain * settled[5].reshape(tile_rows * tile_cols, parts)
    slot_table = (
        cell_slots.reshape(tile_rows * tile_cols, parts)[:, :, None]
        == jnp.arange(parts, dtype=jnp.int32)[None, None, :]
    ).astype(jnp.float32)
    per_tile = jnp.einsum("tp,tpc->tc", lifting, slot_table, precision=highest)
    blocks = gas_source.size // parts
    block_table = (
        jnp.arange(blocks, dtype=jnp.int32)[:, None] == cell_blocks.reshape(-1)[None, :]
    ).astype(jnp.float32)
    deposited = jnp.dot(block_table, per_tile, precision=highest).reshape(gas_source.shape)
    right_side = gas_source - deposited
    scaling = 1.0 / (6.0 + diagonal)
    solution = jnp.zeros_like(right_side)
    residual = right_side
    precond = residual * scaling
    image = operate(precond, diagonal)
    weighted, curvature = paired_sums(residual, precond, image)
    alpha = weighted / curvature
    direction = precond
    along = image
    for step in range(ITERS):
        solution = solution + alpha * direction
        residual = residual - alpha * along
        if step + 1 < ITERS:
            precond = residual * scaling
            image = operate(precond, diagonal)
            renewed, curvature = paired_sums(residual, precond, image)
            ratio = renewed / weighted
            alpha = renewed / (curvature - ratio * renewed / alpha)
            direction = precond + ratio * direction
            along = image + ratio * along
            weighted = renewed
    return (state[0:3], state[3:6], solution, residual)


def solution(mesh):
    in_specs = (
        P(None, "height", "cols", None),
        P(None, "height", "cols", None),
        P(None, "height", "cols"),
        P("height", "cols"),
        P("height", "cols"),
        P("height", "cols"),
        P("height", "cols", None),
        P("height", "cols", None),
        P("height", "cols", None),
    )
    out_specs = (
        P(None, "height", "cols", None),
        P(None, "height", "cols", None),
        P("height", "cols", None),
        P("height", "cols", None),
    )
    return jax.shard_map(
        on_device, mesh=mesh, in_specs=in_specs, out_specs=out_specs, check_vma=False
    )
```

profile of v0, /device:TPU:0, one launch (start us, length us, event | category | flops | bytes accessed | tf_op | source)
XLA Modules:
  0.0 243.5 jit_solution(3225536009246568072)
XLA Ops:
  1.5 1.3 collective-permute-start.1
  2.8 5.5 %collective-permute-start = (f32[6,1,8,128]{3,0,2,1:T(8,128)S(1)}, f32[6,1,8,128]{3,0,2,1:T(8,128)S(1)}, u32[]{:S(2)}, u32[]{:S(2)}) collective-permute-start(f32[6,1,8,128]{3,0,2,1:T(8,128)S(1)} %get-tuple-element.370), channel_id=1, source_target_pairs={{0,4},{4,8},{8,12},{12,16},{16,20},{20,24},{24,28},{1,5},{5,9},{9,... | collective-permute-start | bytes 73736 | tf_op jit(solution)/shard_map/ppermute | solution.py:23
  8.2 1.6 collective-permute-done
  9.8 1.3 collective-permute-start.3
  11.1 3.0 %collective-permute-start.2 = (f32[6,4,1,128]{3,0,2,1:T(8,128)S(1)}, f32[6,4,1,128]{3,0,2,1:T(8,128)S(1)}, u32[]{:S(2)}, u32[]{:S(2)}) collective-permute-start(f32[6,4,1,128]{3,0,2,1:T(8,128)S(1)} %get-tuple-element.366), channel_id=1, source_target_pairs={{0,1},{1,2},{2,3},{4,5},{5,6},{6,7},{8,9},{9,10},{10,11},{12,13},{... | collective-permute-start | bytes 36872 | tf_op jit(solution)/shard_map/ppermute | solution.py:23
  15.8 38.9 %while.22 = (s32[]{:T(128)}, f32[2,3,8,128]{3,2,0,1:T(8,128)S(1)}, s32[2]{0:T(128)S(1)}, f32[6,4,10,128]{3,0,2,1:T(8,128)S(1)}, s32[9,2,8]{2,1,0:T(2,128)S(1)}, ...) while((s32[]{:T(128)}, f32[2,3,8,128]{3,2,0,1:T(8,128)S(1)}, ...), condition=%wide.region_20.21_spmd.clone, body=%wide.region_0.20_spmd.sunk.clone.sunk | while | flops 94617760 | bytes 10712344 | solution.py:69
  22.7 1.1 fusion.519
  24.4 1.1 fusion.521
  27.8 1.1 fusion.525
  31.2 1.1 fusion.529
  32.9 1.1 fusion.531
  42.2 1.1 fusion.519
  43.9 1.1 fusion.521
  47.3 1.1 fusion.525
  49.0 1.1 fusion.527
  50.7 1.1 fusion.529
  52.4 1.1 fusion.531
  55.5 1.3 collective-permute-start.5
  56.8 5.4 %collective-permute-start.4 = (f32[6,1,8,128]{3,2,1,0:T(8,128)S(1)}, f32[6,1,8,128]{3,2,1,0:T(8,128)S(1)}, u32[]{:S(2)}, u32[]{:S(2)}) collective-permute-start(f32[6,1,8,128]{3,2,1,0:T(8,128)S(1)} %get-tuple-element.374), channel_id=1, source_target_pairs={{0,4},{4,8},{8,12},{12,16},{16,20},{20,24},{24,28},{1,5},{5,9},{9,... | collective-permute-start | bytes 73736 | tf_op jit(solution)/shard_map/ppermute | solution.py:23
  62.4 1.4 collective-permute-done.4
  63.7 1.3 collective-permute-start.7
  65.0 3.0 %collective-permute-start.6 = (f32[6,4,1,128]{3,2,1,0:T(1,128)S(1)}, f32[6,4,1,128]{3,2,1,0:T(1,128)S(1)}, u32[]{:S(2)}, u32[]{:S(2)}) collective-permute-start(f32[6,4,1,128]{3,2,1,0:T(1,128)S(1)} %get-tuple-element.368), channel_id=1, source_target_pairs={{0,1},{1,2},{2,3},{4,5},{5,6},{6,7},{8,9},{9,10},{10,11},{12,13},{... | collective-permute-start | bytes 36872 | tf_op jit(solution)/shard_map/ppermute | solution.py:23
  69.3 39.3 %while.23 = (s32[]{:T(128)}, f32[2,3,8,128]{3,2,0,1:T(8,128)S(1)}, s32[2]{0:T(128)S(1)}, f32[6,4,10,128]{3,0,2,1:T(8,128)S(1)}, s32[9,2,8]{2,1,0:T(2,128)S(1)}, ...) while((s32[]{:T(128)}, f32[2,3,8,128]{3,2,0,1:T(8,128)S(1)}, ...), condition=%wide.region_41.42_spmd.clone, body=%wide.region_21.41_spmd.sunk.clone.sunk | while | flops 94617760 | bytes 10712344 | solution.py:69
  76.4 1.1 fusion.556
  78.1 1.1 fusion.558
  81.5 1.1 fusion.562
  83.2 1.1 fusion.564
  84.9 1.1 fusion.566
  86.6 1.1 fusion.568
  95.8 1.1 fusion.556
  97.5 1.1 fusion.558
  100.9 1.1 fusion.562
  102.6 1.1 fusion.564
  104.3 1.1 fusion.566
  106.1 1.1 fusion.568
  111.5 1.3 collective-permute-start.9
  112.8 5.8 %collective-permute-start.10 = (f32[1,64,512]{2,1,0:T(8,128)S(1)}, f32[1,64,512]{2,1,0:T(8,128)S(1)}, u32[]{:S(2)}, u32[]{:S(2)}) collective-permute-start(f32[1,64,512]{2,1,0:T(8,128)S(1)} %get-tuple-element.364), channel_id=1, source_target_pairs={{0,4},{4,8},{8,12},{12,16},{16,20},{20,24},{24,28},{1,5},{5,9},{9,... | collective-permute-start | bytes 393224 | tf_op jit(solution)/shard_map/ppermute | solution.py:23
  118.7 3.3 %collective-permute-start.8 = (f32[6,8,128]{2,1,0:T(8,128)S(1)}, f32[6,8,128]{2,1,0:T(8,128)S(1)}, u32[]{:S(2)}, u32[]{:S(2)}) collective-permute-start(f32[6,8,128]{2,1,0:T(8,128)S(1)} %convolution_bitcast_fusion.19), channel_id=1, source_target_pairs={{0,4},{4,8},{8,12},{12,16},{16,20},{20,24},{24,28},{28,0},{1,5},{5... | collective-permute-start | bytes 73736 | tf_op jit(solution)/shard_map/ppermute | solution.py:34
  122.0 1.6 collective-permute-done.10
  123.6 1.3 collective-permute-start.11
  124.9 3.9 %collective-permute-start.12 = (f32[4,1,512]{2,1,0:T(1,128)S(1)}, f32[4,1,512]{2,1,0:T(1,128)S(1)}, u32[]{:S(2)}, u32[]{:S(2)}) collective-permute-start(f32[4,1,512]{2,1,0:T(1,128)S(1)} %get-tuple-element.360), channel_id=1, source_target_pairs={{0,1},{1,2},{2,3},{4,5},{5,6},{6,7},{8,9},{9,10},{10,11},{12,13},{... | collective-permute-start | bytes 24584 | tf_op jit(solution)/shard_map/ppermute | solution.py:23
  130.7 46.0 %all-reduce.3 = (f32[]{:T(128)}, f32[]{:T(128)}) all-reduce(f32[]{:T(128)} %get-tuple-element.269, f32[]{:T(128)} %get-tuple-element.268), channel_id=1, replica_groups=mesh['height'=8,'cols'=4] {'height','cols'}, use_global_device_ids=true, to_apply=%region_44.45 | all-reduce | flops 2 | bytes 16 | tf_op jit(solution)/shard_map/psum | solution.py:90
  178.1 1.3 collective-permute-start.13
  179.5 4.8 %collective-permute-start.14 = (f32[1,64,512]{2,1,0:T(8,128)S(1)}, f32[1,64,512]{2,1,0:T(8,128)S(1)}, u32[]{:S(2)}, u32[]{:S(2)}) collective-permute-start(f32[1,64,512]{2,1,0:T(8,128)S(1)} %get-tuple-element.362), channel_id=1, source_target_pairs={{0,4},{4,8},{8,12},{12,16},{16,20},{20,24},{24,28},{1,5},{5,9},{9,... | collective-permute-start | bytes 393224 | tf_op jit(solution)/shard_map/ppermute | solution.py:23
  185.3 3.0 %collective-permute-done.14 = f32[1,64,512]{2,1,0:T(8,128)S(1)} collective-permute-done((f32[1,64,512]{2,1,0:T(8,128)S(1)}, f32[1,64,512]{2,1,0:T(8,128)S(1)}, u32[]{:S(2)}, u32[]{:S(2)}) %collective-permute-start.14) | collective-permute-done | bytes 131104 | tf_op jit(solution)/shard_map/ppermute | solution.py:23
  188.3 1.3 collective-permute-start.15
  189.6 3.0 %collective-permute-start.16 = (f32[4,1,512]{2,1,0:T(1,128)S(1)}, f32[4,1,512]{2,1,0:T(1,128)S(1)}, u32[]{:S(2)}, u32[]{:S(2)}) collective-permute-start(f32[4,1,512]{2,1,0:T(1,128)S(1)} %get-tuple-element.358), channel_id=1, source_target_pairs={{0,1},{1,2},{2,3},{4,5},{5,6},{6,7},{8,9},{9,10},{10,11},{12,13},{... | collective-permute-start | bytes 24584 | tf_op jit(solution)/shard_map/ppermute | solution.py:23
  194.7 43.3 %all-reduce.2 = (f32[]{:T(128)}, f32[]{:T(128)}) all-reduce(f32[]{:T(128)} %get-tuple-element.267, f32[]{:T(128)} %get-tuple-element.266), channel_id=1, replica_groups=mesh['height'=8,'cols'=4] {'height','cols'}, use_global_device_ids=true, to_apply=%region_48.49 | all-reduce | flops 2 | bytes 16 | tf_op jit(solution)/shard_map/psum | solution.py:90
  (159 shorter events, 51.8 us)
Async XLA Ops:
  0.6 0.8 copy-start.11
  1.5 6.8 %collective-permute-start.1 = (f32[6,1,8,128]{3,0,2,1:T(8,128)S(1)}, f32[6,1,8,128]{3,0,2,1:T(8,128)S(1)}, u32[]{:S(2)}, u32[]{:S(2)}) collective-permute-start(f32[6,1,8,128]{3,0,2,1:T(8,128)S(1)} %get-tuple-element.371), channel_id=1, source_target_pairs={{4,0},{8,4},{12,8},{16,12},{20,16},{24,20},{28,24},{5,1},{9,5},{13... | collective-permute-start | bytes 73736 | tf_op jit(solution)/shard_map/ppermute | solution.py:26
  2.8 7.1 %collective-permute-start = (f32[6,1,8,128]{3,0,2,1:T(8,128)S(1)}, f32[6,1,8,128]{3,0,2,1:T(8,128)S(1)}, u32[]{:S(2)}, u32[]{:S(2)}) collective-permute-start(f32[6,1,8,128]{3,0,2,1:T(8,128)S(1)} %get-tuple-element.370), channel_id=1, source_target_pairs={{0,4},{4,8},{8,12},{12,16},{16,20},{20,24},{24,28},{1,5},{5,9},{9,... | collective-permute-start | bytes 73736 | tf_op jit(solution)/shard_map/ppermute | solution.py:23
  9.8 4.4 %copy-start.12 = (s32[9,2,8]{0,2,1:T(8,128)S(1)}, s32[9,2,8]{0,2,1:T(8,128)}, u32[]{:S(2)}) copy-start(s32[9,2,8]{0,2,1:T(8,128)} %param.35) | copy-start | bytes 1732
  9.8 4.4 %copy-start.13 = (s32[2,8]{1,0:T(2,128)S(1)}, s32[2,8]{1,0:T(2,128)}, u32[]{:S(2)}) copy-start(s32[2,8]{1,0:T(2,128)} %param.36) | copy-start | bytes 196
  9.8 4.5 %collective-permute-start.3 = (f32[6,4,1,128]{3,0,2,1:T(8,128)S(1)}, f32[6,4,1,128]{3,0,2,1:T(8,128)S(1)}, u32[]{:S(2)}, u32[]{:S(2)}) collective-permute-start(f32[6,4,1,128]{3,0,2,1:T(8,128)S(1)} %get-tuple-element.367), channel_id=1, source_target_pairs={{1,0},{2,1},{3,2},{5,4},{6,5},{7,6},{9,8},{10,9},{11,10},{13,12},{... | collective-permute-start | bytes 36872 | tf_op jit(solution)/shard_map/ppermute | solution.py:26
  11.1 3.9 %collective-permute-start.2 = (f32[6,4,1,128]{3,0,2,1:T(8,128)S(1)}, f32[6,4,1,128]{3,0,2,1:T(8,128)S(1)}, u32[]{:S(2)}, u32[]{:S(2)}) collective-permute-start(f32[6,4,1,128]{3,0,2,1:T(8,128)S(1)} %get-tuple-element.366), channel_id=1, source_target_pairs={{0,1},{1,2},{2,3},{4,5},{5,6},{6,7},{8,9},{9,10},{10,11},{12,13},{... | collective-permute-start | bytes 36872 | tf_op jit(solution)/shard_map/ppermute | solution.py:23
  15.0 0.7 copy-start.2
  15.1 0.7 copy-start.3
  15.1 0.7 copy-start.4
  15.1 0.7 copy-start.5
  15.1 0.7 copy-start.6
  15.1 0.7 copy-start.7
  15.1 0.7 copy-start.8
  15.1 0.7 copy-start.9
  15.8 38.9 %copy-start.10 = (f32[3,2,8,128]{3,2,1,0:T(8,128)S(1)}, f32[3,2,8,128]{3,2,1,0:T(8,128)}, u32[]{:S(2)}) copy-start(f32[3,2,8,128]{3,2,1,0:T(8,128)} %param.33) | copy-start | bytes 73732
  54.7 0.7 copy-start.14
  55.5 6.9 %collective-permute-start.5 = (f32[6,1,8,128]{3,2,1,0:T(8,128)S(1)}, f32[6,1,8,128]{3,2,1,0:T(8,128)S(1)}, u32[]{:S(2)}, u32[]{:S(2)}) collective-permute-start(f32[6,1,8,128]{3,2,1,0:T(8,128)S(1)} %get-tuple-element.375), channel_id=1, source_target_pairs={{4,0},{8,4},{12,8},{16,12},{20,16},{24,20},{28,24},{5,1},{9,5},{13... | collective-permute-start | bytes 73736 | tf_op jit(solution)/shard_map/ppermute | solution.py:26
  56.8 7.0 %collective-permute-start.4 = (f32[6,1,8,128]{3,2,1,0:T(8,128)S(1)}, f32[6,1,8,128]{3,2,1,0:T(8,128)S(1)}, u32[]{:S(2)}, u32[]{:S(2)}) collective-permute-start(f32[6,1,8,128]{3,2,1,0:T(8,128)S(1)} %get-tuple-element.374), channel_id=1, source_target_pairs={{0,4},{4,8},{8,12},{12,16},{16,20},{20,24},{24,28},{1,5},{5,9},{9,... | collective-permute-start | bytes 73736 | tf_op jit(solution)/shard_map/ppermute | solution.py:23
  63.7 5.4 %collective-permute-start.7 = (f32[6,4,1,128]{3,2,1,0:T(1,128)S(1)}, f32[6,4,1,128]{3,2,1,0:T(1,128)S(1)}, u32[]{:S(2)}, u32[]{:S(2)}) collective-permute-start(f32[6,4,1,128]{3,2,1,0:T(1,128)S(1)} %get-tuple-element.369), channel_id=1, source_target_pairs={{1,0},{2,1},{3,2},{5,4},{6,5},{7,6},{9,8},{10,9},{11,10},{13,12},{... | collective-permute-start | bytes 36872 | tf_op jit(solution)/shard_map/ppermute | solution.py:26
  65.0 4.1 %collective-permute-start.6 = (f32[6,4,1,128]{3,2,1,0:T(1,128)S(1)}, f32[6,4,1,128]{3,2,1,0:T(1,128)S(1)}, u32[]{:S(2)}, u32[]{:S(2)}) collective-permute-start(f32[6,4,1,128]{3,2,1,0:T(1,128)S(1)} %get-tuple-element.368), channel_id=1, source_target_pairs={{0,1},{1,2},{2,3},{4,5},{5,6},{6,7},{8,9},{9,10},{10,11},{12,13},{... | collective-permute-start | bytes 36872 | tf_op jit(solution)/shard_map/ppermute | solution.py:23
  68.4 0.7 copy-start.17
  108.7 0.7 copy-start.16
  110.3 1.0 copy-start
  110.3 1.0 copy-start.1
  111.5 10.5 %collective-permute-start.9 = (f32[1,64,512]{2,1,0:T(8,128)S(1)}, f32[1,64,512]{2,1,0:T(8,128)S(1)}, u32[]{:S(2)}, u32[]{:S(2)}) collective-permute-start(f32[1,64,512]{2,1,0:T(8,128)S(1)} %get-tuple-element.365), channel_id=1, source_target_pairs={{4,0},{8,4},{12,8},{16,12},{20,16},{24,20},{28,24},{5,1},{9,5},{13... | collective-permute-start | bytes 393224 | tf_op jit(solution)/shard_map/ppermute | solution.py:26
  112.8 10.8 %collective-permute-start.10 = (f32[1,64,512]{2,1,0:T(8,128)S(1)}, f32[1,64,512]{2,1,0:T(8,128)S(1)}, u32[]{:S(2)}, u32[]{:S(2)}) collective-permute-start(f32[1,64,512]{2,1,0:T(8,128)S(1)} %get-tuple-element.364), channel_id=1, source_target_pairs={{0,4},{4,8},{8,12},{12,16},{16,20},{20,24},{24,28},{1,5},{5,9},{9,... | collective-permute-start | bytes 393224 | tf_op jit(solution)/shard_map/ppermute | solution.py:23
  118.7 65.6 %collective-permute-start.8 = (f32[6,8,128]{2,1,0:T(8,128)S(1)}, f32[6,8,128]{2,1,0:T(8,128)S(1)}, u32[]{:S(2)}, u32[]{:S(2)}) collective-permute-start(f32[6,8,128]{2,1,0:T(8,128)S(1)} %convolution_bitcast_fusion.19), channel_id=1, source_target_pairs={{0,4},{4,8},{8,12},{12,16},{16,20},{20,24},{24,28},{28,0},{1,5},{5... | collective-permute-start | bytes 73736 | tf_op jit(solution)/shard_map/ppermute | solution.py:34
  123.6 5.3 %collective-permute-start.11 = (f32[4,1,512]{2,1,0:T(1,128)S(1)}, f32[4,1,512]{2,1,0:T(1,128)S(1)}, u32[]{:S(2)}, u32[]{:S(2)}) collective-permute-start(f32[4,1,512]{2,1,0:T(1,128)S(1)} %get-tuple-element.361), channel_id=1, source_target_pairs={{1,0},{2,1},{3,2},{5,4},{6,5},{7,6},{9,8},{10,9},{11,10},{13,12},{... | collective-permute-start | bytes 24584 | tf_op jit(solution)/shard_map/ppermute | solution.py:26
  124.9 4.7 %collective-permute-start.12 = (f32[4,1,512]{2,1,0:T(1,128)S(1)}, f32[4,1,512]{2,1,0:T(1,128)S(1)}, u32[]{:S(2)}, u32[]{:S(2)}) collective-permute-start(f32[4,1,512]{2,1,0:T(1,128)S(1)} %get-tuple-element.360), channel_id=1, source_target_pairs={{0,1},{1,2},{2,3},{4,5},{5,6},{6,7},{8,9},{9,10},{10,11},{12,13},{... | collective-permute-start | bytes 24584 | tf_op jit(solution)/shard_map/ppermute | solution.py:23
  178.1 7.2 %collective-permute-start.13 = (f32[1,64,512]{2,1,0:T(8,128)S(1)}, f32[1,64,512]{2,1,0:T(8,128)S(1)}, u32[]{:S(2)}, u32[]{:S(2)}) collective-permute-start(f32[1,64,512]{2,1,0:T(8,128)S(1)} %get-tuple-element.363), channel_id=1, source_target_pairs={{4,0},{8,4},{12,8},{16,12},{20,16},{24,20},{28,24},{5,1},{9,5},{13... | collective-permute-start | bytes 393224 | tf_op jit(solution)/shard_map/ppermute | solution.py:26
  179.4 4.8 %copy-start.15 = (s32[1,8]{1,0:T(1,128)S(1)}, s32[1,8]{1,0:T(1,128)}, u32[]{:S(2)}) copy-start(s32[1,8]{1,0:T(1,128)} %param.37) | copy-start | bytes 100
  179.5 8.8 %collective-permute-start.14 = (f32[1,64,512]{2,1,0:T(8,128)S(1)}, f32[1,64,512]{2,1,0:T(8,128)S(1)}, u32[]{:S(2)}, u32[]{:S(2)}) collective-permute-start(f32[1,64,512]{2,1,0:T(8,128)S(1)} %get-tuple-element.362), channel_id=1, source_target_pairs={{0,4},{4,8},{8,12},{12,16},{16,20},{20,24},{24,28},{1,5},{5,9},{9,... | collective-permute-start | bytes 393224 | tf_op jit(solution)/shard_map/ppermute | solution.py:23
  188.3 5.0 %collective-permute-start.15 = (f32[4,1,512]{2,1,0:T(1,128)S(1)}, f32[4,1,512]{2,1,0:T(1,128)S(1)}, u32[]{:S(2)}, u32[]{:S(2)}) collective-permute-start(f32[4,1,512]{2,1,0:T(1,128)S(1)} %get-tuple-element.359), channel_id=1, source_target_pairs={{1,0},{2,1},{3,2},{5,4},{6,5},{7,6},{9,8},{10,9},{11,10},{13,12},{... | collective-permute-start | bytes 24584 | tf_op jit(solution)/shard_map/ppermute | solution.py:26
  189.6 3.8 %collective-permute-start.16 = (f32[4,1,512]{2,1,0:T(1,128)S(1)}, f32[4,1,512]{2,1,0:T(1,128)S(1)}, u32[]{:S(2)}, u32[]{:S(2)}) collective-permute-start(f32[4,1,512]{2,1,0:T(1,128)S(1)} %get-tuple-element.358), channel_id=1, source_target_pairs={{0,1},{1,2},{2,3},{4,5},{5,6},{6,7},{8,9},{9,10},{10,11},{12,13},{... | collective-permute-start | bytes 24584 | tf_op jit(solution)/shard_map/ppermute | solution.py:23
where the time goes:
time: 245 us; the launch traced here: 244 us
  blocking collectives  89.3 us (36%)
  matrix products  62.7 us (26%)
  starting transfers between devices  48.1 us (20%)
  loops' own time  13.5 us (6%)
  waiting for transfers between devices  10.1 us (4%)
  local copies, waits for them, and re-layouts  7.45 us (3%)
  between operations  7 us (3%)
  other arithmetic  5.43 us (2%)
    psum x2, blocking collectives, paired_sums(): lax.psum((jnp.sum(residual * precond), jnp.sum(precond * image)), ('heigh...  89.3 us
    dot_general x36, matrix products, row_forces(): cross = jnp.einsum('cip,ciq->ipq', places, other_places, precision=highest)  41 us
    ppermute x8, starting transfers between devices, padded_2(): lax.ppermute(lax.slice_in_dim(block, block.shape[dim] - width, None, axis...  34.5 us
    dot_general x36, matrix products, row_forces(): jnp.einsum('ipq,ciq->cip', weight, other_places - damping * other[3:6], p...  20.5 us
    another operation x2, loops' own time, tile_forces(): stacked = lax.map(one_row, jnp.arange(count, dtype=jnp.int32))  13.5 us
    ppermute x8, starting transfers between devices, padded_2(): lax.ppermute(lax.slice_in_dim(block, 0, width, axis=dim), axis, backward)  10.3 us
    ppermute x8, waiting for transfers between devices, padded_2(): lax.ppermute(lax.slice_in_dim(block, block.shape[dim] - width, None, axis...  9.12 us
  transfers between devices with their start and end apart: 17, of which 8 were waited for; matrix products, arithmetic and copies ran while one was open for 1% of the time, Pallas kernels for 0%

commit v1 on v0

v1 whole, which is shorter than its diff:
```python
import functools
import jax
import jax.numpy as jnp
from jax import lax
from jax.experimental import pallas as pl
from jax.experimental.pallas import tpu as pltpu
from jax.sharding import PartitionSpec as P

f32, bf16, i32 = jnp.float32, jnp.bfloat16, jnp.int32
spring = 0.05
cutoff_sq = 1.44
damping = 0.5
step_dt = 0.05
gravity = 1.0
deposit_gain = 2.0
LANES = 128
COMPS = 8
DEPTH = 2
ROWS_OUT = 24


def rounded(value):
    return value.astype(bf16).astype(f32)


def rounded_pair(value):
    high = rounded(value)
    return high, rounded(value - high)


def split(value):
    high = rounded(value)
    mid = rounded(value - high)
    return high, mid, value - high - mid


def centred(tile, r, c, rows, wide):
    row = lax.broadcasted_iota(i32, (COMPS, LANES), 0)
    side = jnp.float32(c - wide // 2)
    up = (r - rows // 2).astype(f32)
    return tile + jnp.where(row == 0, side, jnp.where(row == 2, up, 0.0))


def place_parts(tile, r, c, rows, wide):
    row = lax.broadcasted_iota(i32, (COMPS, LANES), 0)
    place = jnp.where(row < 3, centred(tile, r, c, rows, wide), 0.0)
    high, mid = rounded_pair(place)
    place = high + mid
    return high, mid, -jnp.sum(place * place, axis=0, keepdims=True)


def source_features(tile, r, c, rows, wide):
    row = lax.broadcasted_iota(i32, (COMPS, LANES), 0)
    row32 = lax.broadcasted_iota(i32, (32, LANES), 0)
    high, mid, size = place_parts(tile, r, c, rows, wide)
    size_high, size_mid, size_low = split(size)
    first = jnp.where(row < 3, high, 1.0)
    first = jnp.where(row == 3, size_high, jnp.where(row == 4, size_mid, jnp.where(row == 5, size_low, first)))
    second = jnp.where(row < 3, high, jnp.where(row == 3, 1.0, 0.0))
    kind = lax.rem(r, 3) * 4 + c % 4
    kind = kind + jnp.where(kind < 4, 12, jnp.where(kind < 9, 15, 18))
    near = jnp.concatenate([first, second, mid, mid], axis=0) + jnp.where(row32 == kind, 1.0, 0.0)
    high, mid, low = split(centred(tile, r, c, rows, wide) - damping * pltpu.roll(tile, 5, 0))
    first = jnp.where(row < 3, high, jnp.where(row == 3, 1.0, 0.0))
    second = jnp.where(row < 3, mid, jnp.where(row < 4, 0.0, pltpu.roll(low, 4, 0)))
    return near, jnp.concatenate([first, second], axis=0).astype(bf16)


def target_features(tile, r, c, rows, wide):
    row = lax.broadcasted_iota(i32, (COMPS, LANES), 0)
    row32 = lax.broadcasted_iota(i32, (32, LANES), 0)
    lane32 = lax.broadcasted_iota(i32, (32, LANES), 1)
    high, mid, size = place_parts(tile, r, c, rows, wide)
    own_high, own_mid, own_low = split(cutoff_sq + size)
    first = jnp.where(row < 3, 2.0 * high, jnp.where(row < 6, 1.0, jnp.where(row == 6, own_high, own_mid)))
    second = jnp.where(row < 3, 2.0 * mid, jnp.where(row == 3, own_low, 0.0))
    third = jnp.where(row < 3, 2.0 * high, 0.0)
    fourth = jnp.where(row < 3, 2.0 * mid, 0.0)
    kind = jnp.where(row32 < 16, row32 - 12, jnp.where(row32 < 24, row32 - 15, row32 - 18))
    is_kind = ((row32 >= 12) & (row32 < 16)) | ((row32 >= 19) & (row32 < 24)) | ((row32 >= 27) & (row32 < 30))
    kind_row = jnp.where(kind < 4, 0, jnp.where(kind < 8, 1, 2))
    up = kind_row + lax.rem(4 - lax.rem(r, 3), 3)
    up = jnp.where(up > 2, up - 3, up)
    side = kind - 4 * kind_row + (5 - c % 4) % 4
    side = jnp.where(side > 3, side - 4, side)
    wanted = jnp.where(side < 3, 3 * up + side, LANES)
    flags = jnp.sum(jnp.where(lane32 == wanted, tile[6:7, :], 0.0), axis=1, keepdims=True)
    barred = jnp.where(is_kind, -1024.0 * (1.0 - flags), 0.0)
    return jnp.concatenate([first, second, third, fourth], axis=0) + barred


def forces_on(tiles, r, c, rows, wide, turned, pulled):
    features = [target_features(tile, r, c + k, rows, wide) for k, tile in enumerate(tiles)]
    target = jnp.concatenate(features, axis=1).astype(bf16)
    weights = []
    for k in range(4):
        spread = [jnp.zeros((32, 2 * LANES), bf16)] * 4
        spread[k] = target
        weights.append(jnp.concatenate(spread, axis=0))
    total = jnp.zeros((16, 2 * LANES), f32)
    for i in range(3):
        for half in range(2):
            parts = []
            pulls = []
            for j in (2 * half, 2 * half + 1):
                s = c - 1 + j
                near = jnp.dot(turned[r + i - 1, s // 4], weights[s % 4], preferred_element_type=f32)
                parts.append(jnp.maximum(near, 0.0))
                pulls.append(pulled[r + i - 1, s])
            pulls = jnp.concatenate(pulls, axis=1)
            weight = jnp.concatenate(parts, axis=0)
            high = weight.astype(bf16)
            total = total + jnp.dot(pulls, high, preferred_element_type=f32)
            low = (weight - high.astype(f32)).astype(bf16)
            total = total + jnp.dot(pulls, low, preferred_element_type=f32)
    forces = []
    for k, tile in enumerate(tiles):
        first, second = total[0:8, k * LANES : (k + 1) * LANES], total[8:16, k * LANES : (k + 1) * LANES]
        moving = centred(tile, r, c + k, rows, wide) - damping * pltpu.roll(tile, 5, 0)
        forces.append((spring / cutoff_sq) * (moving * first[3:4, :] - first - second - pltpu.roll(second, 4, 0)))
    return forces


def stepped(tile, force):
    row = lax.broadcasted_iota(i32, (COMPS, LANES), 0)
    change = step_dt * force - jnp.where(row == 2, step_dt * gravity, 0.0)
    speeds = tile + pltpu.roll(change, 3, 0)
    places = tile + step_dt * pltpu.roll(speeds, 5, 0)
    return jnp.where(row < 3, places, jnp.where(row < 6, speeds, tile))


def particles_kernel(
    where_ref, exits_ref, owners_ref, own_ref, first_ref, second_ref, slots_ref,
    sums_ref, settled_ref, leaving_ref, state, turned, pulled, begun,
    *, rows, cols,
):
    wide = cols + 2 * DEPTH
    high = rows + 2 * DEPTH
    left, right = where_ref[0], where_ref[1]
    even, below, above = where_ref[2], where_ref[3], where_ref[4]
    for r in range(rows):
        for c in range(wide):
            one, two = first_ref[r, c], second_ref[r, c]
            low = jnp.where(even > 0, two, one)
            top = jnp.where(even > 0, one, two)
            state[r, c] = jnp.where(below > 0, low, 0.0)
            state[rows + DEPTH + r, c] = jnp.where(above > 0, top, 0.0)
            state[DEPTH + r, c] = own_ref[r, c]

    def fill(source, first, last):
        def one_row(r, carry):
            for block in range(wide // 4):
                near = []
                for c in range(4 * block, 4 * block + 4):
                    places, moving = source_features(source[r, c], r, c, high, wide)
                    near.append(places)
                    pulled[r, c] = moving
                turned[r, block] = jnp.concatenate(near, axis=0).T.astype(bf16)
            return carry

        lax.fori_loop(first, last, one_row, 0)

    fill(state, 0, high)

    def first_step(r, carry):
        begun[r, 0] = jnp.zeros((COMPS, LANES), f32)
        begun[r, wide - 1] = jnp.zeros((COMPS, LANES), f32)
        for c in range(1, wide - 1, 2):
            tiles = [state[r, c], state[r, c + 1]]
            forces = forces_on(tiles, r, c, high, wide, turned, pulled)
            for k in range(2):
                inside = ((r >= DEPTH) | (below > 0)) & ((r < rows + DEPTH) | (above > 0))
                if c + k < DEPTH:
                    inside = inside & (left > 0)
                if c + k >= cols + DEPTH:
                    inside = inside & (right > 0)
                begun[r, c + k] = jnp.where(inside, stepped(tiles[k], forces[k]), 0.0)
        return carry

    lax.fori_loop(1, high - 1, first_step, 0)
    fill(begun, 1, high - 1)

    def second_step(r, carry):
        for c in range(DEPTH, DEPTH + cols, 2):
            tiles = [begun[r, c], begun[r, c + 1]]
            forces = forces_on(tiles, r, c, high, wide, turned, pulled)
            for k in range(2):
                done = stepped(tiles[k], forces[k])
                settled_ref[r - DEPTH, c + k - DEPTH] = done
                lift = deposit_gain * done[5:6, :]
                lift_high, lift_mid, lift_low = split(lift)
                row = lax.broadcasted_iota(i32, (16, LANES), 0)
                parts = jnp.where(
                    row == 0, lift_high, jnp.where(row == 1, lift_mid, jnp.where(row == 2, lift_low, 0.0))
                ).astype(bf16)
                cell = lax.broadcasted_iota(i32, (LANES, LANES), 0)
                slots = slots_ref[r - DEPTH, c + k - DEPTH : c + k - DEPTH + 1, :]
                table = jnp.where(cell == slots, 1.0, 0.0).astype(bf16)
                gathered = lax.dot_general(parts, table, (((1,), (1,)), ((), ())), preferred_element_type=f32)
                sums_ref[pl.ds((r - DEPTH) * cols + c + k - DEPTH, 1), :] = jnp.sum(gathered, axis=0, keepdims=True)
        return carry

    lax.fori_loop(DEPTH, DEPTH + rows, second_step, 0)

    lane = lax.broadcasted_iota(i32, (1, LANES), 1)
    owner_row = jnp.zeros((1, LANES), i32)
    for t in range(rows * cols):
        owner_row = jnp.where(lax.rem(lane, rows * cols) == t, owners_ref[t // cols, t % cols], owner_row)
    row = lax.broadcasted_iota(i32, (ROWS_OUT - rows * cols, LANES), 0)
    sums_ref[rows * cols :, :] = jnp.where(row == 0, owner_row.astype(f32), 0.0)

    leaving_ref[...] = jnp.zeros_like(leaving_ref)
    count = jnp.int32(0)
    for t in range(rows * cols):
        flag = exits_ref[t // cols, t % cols]

        @pl.when((flag > 0) & (count < cols))
        def _(t=t, count=count):
            leaving_ref[count] = settled_ref[t // cols, t % cols]

        count = count + flag


def particles(where, exits, owners, own, first, second, slots):
    rows, cols = slots.shape[:2]
    wide, high = cols + 2 * DEPTH, rows + 2 * DEPTH
    smem = pl.BlockSpec(memory_space=pltpu.SMEM)
    vmem = pl.BlockSpec(memory_space=pltpu.VMEM)
    return pl.pallas_call(
        functools.partial(particles_kernel, rows=rows, cols=cols),
        out_shape=(
            jax.ShapeDtypeStruct((ROWS_OUT, LANES), f32),
            jax.ShapeDtypeStruct((rows, cols, COMPS, LANES), f32),
            jax.ShapeDtypeStruct((cols, COMPS, LANES), f32),
        ),
        in_specs=[smem, smem, smem, vmem, vmem, vmem, vmem],
        out_specs=(vmem, vmem, vmem),
        scratch_shapes=[
            pltpu.VMEM((high, wide, COMPS, LANES), f32),
            pltpu.VMEM((high, wide // 4, LANES, LANES), bf16),
            pltpu.VMEM((high, wide, 16, LANES), bf16),
            pltpu.VMEM((high, wide, COMPS, LANES), f32),
        ],
        compiler_params=pltpu.CompilerParams(vmem_limit_bytes=40 * 1024 * 1024),
        name="particles",
    )(where, exits, owners, own, first, second, slots)


def matching(heights, groups, axis, odd, wrap):
    size = heights if axis == "height" else groups
    pairs = []
    for h in range(heights):
        for c in range(groups):
            i = h if axis == "height" else c
            j = i ^ 1 if not odd else (i + 1 if i % 2 else i - 1)
            if 0 <= j < size or wrap:
                j = j % size
                target = (j, c) if axis == "height" else (h, j)
            else:
                target = (h, c ^ 1) if axis == "height" else (h ^ 1, c)
            pairs.append((h * groups + c, target[0] * groups + target[1]))
    return pairs


def exchanged(value, axis, wrap):
    heights, groups = lax.axis_size("height"), lax.axis_size("cols")
    return [
        lax.ppermute(value, ("height", "cols"), matching(heights, groups, axis, odd, wrap)) for odd in (False, True)
    ]


def right_side_kernel(
    where_ref, sums_ref, side_a, side_b, height_a, height_b, gas_ref, diagonal_ref, line_a, line_b,
    corner_a, corner_b, gas_a, gas_b, rhs_ref, near_ref, far_ref, dots_ref, scaling, rhs, first, second,
    *, cols,
):
    levels, across, along = gas_ref.shape
    edge = 8
    wide = across + 2 * edge
    quarters = along // LANES
    left, right, even_c = where_ref[0], where_ref[1], where_ref[5]
    even, below, above = where_ref[2], where_ref[3], where_ref[4]

    def low_of(is_even, one, two):
        return jnp.where(is_even > 0, two, one)

    def high_of(is_even, one, two):
        return jnp.where(is_even > 0, one, two)

    for ref in (scaling, rhs):
        ref[:, 0:edge, :] = jnp.zeros((3 * levels, edge, along), f32)
        ref[:, edge + across :, :] = jnp.zeros((3 * levels, edge, along), f32)
    scaling[levels : 2 * levels, edge : edge + across] = 1.0 / (6.0 + diagonal_ref[...])
    rhs[levels : 2 * levels, edge : edge + across] = gas_ref[...]
    for level, choose, present in ((0, low_of, below), (2 * levels, high_of, above)):
        for z in range(levels):
            rhs[level + z, edge : edge + across] = choose(even, gas_a[0, z], gas_b[0, z])
            m = 1.0 / (6.0 + choose(even, gas_a[1, z], gas_b[1, z]))
            scaling[level + z, edge : edge + across] = jnp.where(present > 0, m, 0.0)

    def put_line(z, x, lines, present):
        m = jnp.where(present, 1.0 / (6.0 + lines), 0.0)
        for k in range(quarters):
            rhs[z, x : x + 1, k * LANES : (k + 1) * LANES] = lines[k : k + 1]
            scaling[z, x : x + 1, k * LANES : (k + 1) * LANES] = m[quarters + k : quarters + k + 1]

    for z in range(levels):
        for x in range(2):
            put_line(levels + z, edge - 2 + x, low_of(even_c, line_a[z, x, 8:16], line_b[z, x, 8:16]), left > 0)
            put_line(levels + z, edge + across + x, high_of(even_c, line_a[z, x, 8:16], line_b[z, x, 8:16]), right > 0)
        for level, choose, present in ((0, low_of, below), (2 * levels, high_of, above)):
            lines = [choose(even, corner_a[z, cols + 4 + x], corner_b[z, cols + 4 + x]) for x in range(2)]
            put_line(level + z, edge - 1, lines[0], (present > 0) & (left > 0))
            put_line(level + z, edge + across, lines[1], (present > 0) & (right > 0))

    lane = lax.broadcasted_iota(i32, (1, LANES), 1)
    tiles = 16
    shift_q, shift_x = quarters.bit_length() - 1, across.bit_length() - 1
    groups = []
    for name, choose, present in (("below", low_of, below), ("own", None, None), ("above", high_of, above)):
        if choose is None:
            parts = [low_of(even_c, side_a[...], side_b[...]), sums_ref[...], high_of(even_c, side_a[...], side_b[...])]
        else:
            block = [choose(even, height_a[k * ROWS_OUT : (k + 1) * ROWS_OUT], height_b[k * ROWS_OUT : (k + 1) * ROWS_OUT]) for k in range(3)]
            parts = [low_of(even_c, block[1], block[2]), block[0], high_of(even_c, block[1], block[2])]
        level = 0 if name == "below" else levels if name == "own" else 2 * levels
        code = jnp.full((1, LANES), -1, i32)
        for n, part in enumerate(parts):
            owner = part[tiles : tiles + 1].astype(i32)
            x = ((owner >> shift_q) & (across - 1)) + (edge + (n - 1) * across)
            z = owner >> (shift_q + shift_x)
            here = ((lane >> 4) == n) | ((lane >> 4) == n + 3)
            here = here & (x >= edge - 2) & (x < edge + across + 2)
            if n == 0:
                here = here & (left > 0)
            if n == 2:
                here = here & (right > 0)
            if present is not None:
                here = here & (present > 0)
            code = jnp.where(here, (z * wide + x) * quarters + (owner & (quarters - 1)), code)
        values = jnp.concatenate([part[0:tiles] for part in parts], axis=0)
        high = values.astype(bf16)
        low = (values - high.astype(f32)).astype(bf16)
        values = jnp.concatenate([high, low, jnp.zeros((LANES - 6 * tiles, LANES), bf16)], axis=0)
        spot = lax.broadcasted_iota(i32, (levels * wide, LANES), 0) * quarters
        for k in range(quarters):
            table = jnp.where(code == spot + k, 1.0, 0.0).astype(bf16)
            added = jnp.dot(table, values, preferred_element_type=f32)
            for z in range(levels):
                rhs[level + z, :, k * LANES : (k + 1) * LANES] -= added[z * wide : (z + 1) * wide]

    for z in range(3 * levels):
        first[z] = scaling[z] * rhs[z]
    place = lax.broadcasted_iota(i32, (wide, along), 1)

    def beside(ref, z):
        mid = ref[z]
        total = ref[z - 1] + ref[z + 1] + pltpu.roll(mid, 1, 0) + pltpu.roll(mid, wide - 1, 0)
        total = total + jnp.where(place > 0, pltpu.roll(mid, 1, 1), 0.0)
        return total + jnp.where(place < along - 1, pltpu.roll(mid, along - 1, 1), 0.0)

    dots = [jnp.zeros((8, LANES), f32)] * 4

    def folded(value):
        value = jnp.sum(value.reshape(across // 8, 8, along), axis=0)
        return sum(value[:, k * LANES : (k + 1) * LANES] for k in range(quarters))

    inner = slice(edge, edge + across)
    for z in range(levels - 1, 2 * levels + 1):
        near = beside(first, z)
        second[z] = scaling[z] * near
        if levels <= z < 2 * levels:
            near = near[inner]
            near_ref[z - levels] = near
            rhs_ref[z - levels] = rhs[z, inner]
            z0 = first[z, inner]
            dots[0] = dots[0] + folded(z0 * rhs[z, inner])
            dots[1] = dots[1] + folded(z0 * near)
            dots[2] = dots[2] + folded(second[z, inner] * near)
    for z in range(levels, 2 * levels):
        far = beside(second, z)[inner]
        far_ref[z - levels] = far
        dots[3] = dots[3] + folded(second[z, inner] * far)
    row = lax.broadcasted_iota(i32, (8, LANES), 0)
    lane8 = lax.broadcasted_iota(i32, (8, LANES), 1)
    line = jnp.zeros((1, LANES), f32)
    for k in range(4):
        total = jnp.sum(jnp.sum(dots[k], axis=0, keepdims=True), axis=1, keepdims=True)
        line = jnp.where(lane == k, total, line)
    dots_ref[...] = jnp.broadcast_to(line, dots_ref.shape)


def right_side_of(where, sums, side, height, gas, diagonal, lines, corners, gases, devices, cols):
    levels, across, along = gas.shape
    smem = pl.BlockSpec(memory_space=pltpu.SMEM)
    vmem = pl.BlockSpec(memory_space=pltpu.VMEM)
    whole = pltpu.VMEM((3 * levels, across + 16, along), f32)
    return pl.pallas_call(
        functools.partial(right_side_kernel, cols=cols),
        out_shape=(jax.ShapeDtypeStruct(gas.shape, f32),) * 3 + (jax.ShapeDtypeStruct((devices, LANES), f32),),
        in_specs=[smem] + [vmem] * 13,
        out_specs=(vmem,) * 4,
        scratch_shapes=[whole] * 4,
        compiler_params=pltpu.CompilerParams(vmem_limit_bytes=40 * 1024 * 1024),
        name="right_side",
    )(where, sums, *side, *height, gas, diagonal, *lines, *corners, *gases)


def results_kernel(
    where_ref, exits_ref, inlets_ref, dots_ref, rhs_ref, near_ref, far_ref, diagonal_ref, settled_ref,
    height_a, height_b, positions_ref, velocities_ref, pressure_ref, residual_ref,
):
    rows, cols = settled_ref.shape[:2]
    even = where_ref[2]
    totals = jnp.sum(dots_ref[...], axis=0, keepdims=True)
    g00, g01, g11, g12 = [totals[:, k : k + 1] for k in range(4)]
    ratio = g01 / g00
    alpha = g00 / (g00 - g01)
    square = alpha * alpha
    renewed = square * (g11 - ratio * g01)
    beta = renewed / g00
    crossed = square * (ratio * ratio * g01 - 2.0 * ratio * g11 + g12)
    curvature = renewed - crossed - beta * renewed / alpha
    later = renewed / curvature
    one = alpha + later * (1.0 - alpha + beta)
    two = later * alpha
    for z in range(rhs_ref.shape[0]):
        m = 1.0 / (6.0 + diagonal_ref[z])
        rhs, near = rhs_ref[z], near_ref[z]
        pressure_ref[z] = m * (one * rhs + two * near)
        residual_ref[z] = (1.0 - one) * rhs + (one - two) * near + two * far_ref[z]
    for r in range(rows):
        for c in range(cols):
            kept = jnp.where(exits_ref[r, c] > 0, 0.0, settled_ref[r, c])
            if r > 0:
                for d in range(3):
                    positions_ref[d, r, c : c + 1] = kept[d : d + 1]
                    velocities_ref[d, r, c : c + 1] = kept[d + 3 : d + 4]
    start = 3 * ROWS_OUT
    for k in range(cols):
        slot = slice(start + k * COMPS, start + (k + 1) * COMPS)
        tile = jnp.where(even > 0, height_b[slot], height_a[slot])
        c = inlets_ref[0, k]
        for d in range(3):
            positions_ref[d, 0, pl.ds(c, 1)] = tile[d : d + 1]
            velocities_ref[d, 0, pl.ds(c, 1)] = tile[d + 3 : d + 4]


def results_of(where, exits, inlets, dots, rhs, near, far, diagonal, settled, height):
    rows, cols = settled.shape[:2]
    smem = pl.BlockSpec(memory_space=pltpu.SMEM)
    vmem = pl.BlockSpec(memory_space=pltpu.VMEM)
    particle = jax.ShapeDtypeStruct((3, rows, cols, LANES), f32)
    cells = jax.ShapeDtypeStruct(rhs.shape, f32)
    return pl.pallas_call(
        results_kernel,
        out_shape=(particle, particle, cells, cells),
        in_specs=[smem] * 3 + [vmem] * 8,
        out_specs=(vmem,) * 4,
        compiler_params=pltpu.CompilerParams(vmem_limit_bytes=40 * 1024 * 1024),
        name="results",
    )(where, exits, inlets, dots, rhs, near, far, diagonal, settled, *height)


def on_device(
    positions, velocities, contacts, exit_flags, inlet_slots, cell_blocks, cell_slots, gas_source, diagonal
):
    heights, groups = lax.axis_size("height"), lax.axis_size("cols")
    h, c = lax.axis_index("height"), lax.axis_index("cols")
    rows, cols = positions.shape[1:3]
    levels, across, along = gas_source.shape
    where = jnp.stack([c > 0, c < groups - 1, h % 2 == 0, h > 0, h < heights - 1, c % 2 == 0, c < 0, c < 0])
    where = where.astype(jnp.int32)
    flags = jnp.pad(contacts.astype(f32).transpose(1, 2, 0), ((0, 0), (0, 0), (0, LANES - contacts.shape[0])))
    tiles = jnp.concatenate(
        [
            positions.transpose(1, 2, 0, 3),
            velocities.transpose(1, 2, 0, 3),
            flags[:, :, None, :],
            jnp.zeros((rows, cols, 1, LANES), f32),
        ],
        axis=2,
    )

    def edge_lines(lines):
        return lines.reshape(levels, 2, along // LANES, LANES)

    def side(first, last):
        cells = slice(0, 2) if first else slice(across - 2, across)
        return jnp.concatenate(
            [
                tiles[:, :DEPTH] if first else tiles[:, cols - DEPTH :],
                edge_lines(gas_source[:, cells]),
                edge_lines(diagonal[:, cells]),
            ],
            axis=2,
        )

    at_left, at_right = side(True, False), side(False, True)
    even = c % 2 == 0
    shared = [jnp.where(even, at_right, at_left), jnp.where(even, at_left, at_right)]
    lines = [
        lax.ppermute(value, ("height", "cols"), matching(heights, groups, "cols", odd, True))
        for value, odd in zip(shared, (False, True))
    ]
    low = jnp.where(c > 0, jnp.where(even, lines[1], lines[0]), 0.0)
    high = jnp.where(c < groups - 1, jnp.where(even, lines[0], lines[1]), 0.0)
    window = jnp.concatenate(
        [low[:, :, :COMPS], tiles, high[:, :, :COMPS], low[:, 1:2, COMPS:], high[:, 0:1, COMPS:]], axis=1
    )
    beside = exchanged(window, "height", False)
    gases = exchanged(jnp.stack([gas_source, diagonal]), "height", False)
    sums, settled, leaving = particles(where, exit_flags, cell_blocks, window, *beside, cell_slots)
    sides = exchanged(sums, "cols", True)
    parcel = jnp.concatenate([sums, *sides, leaving.reshape(cols * COMPS, LANES)], axis=0)
    parcels = exchanged(parcel, "height", True)
    rhs, near, far, dots = right_side_of(
        where, sums, sides, parcels, gas_source, diagonal, lines, beside, gases, heights * groups, cols
    )
    dots = lax.all_to_all(dots, ("height", "cols"), 0, 0, tiled=True)
    return results_of(where, exit_flags, inlet_slots, dots, rhs, near, far, diagonal, settled, parcels)


def solution(mesh):
    in_specs = (
        P(None, "height", "cols", None),
        P(None, "height", "cols", None),
        P(None, "height", "cols"),
        P("height", "cols"),
        P("height", "cols"),
        P("height", "cols"),
        P("height", "cols", None),
        P("height", "cols", None),
        P("height", "cols", None),
    )
    out_specs = (
        P(None, "height", "cols", None),
        P(None, "height", "cols", None),
        P("height", "cols", None),
        P("height", "cols", None),
    )
    return jax.shard_map(
        on_device, mesh=mesh, in_specs=in_specs, out_specs=out_specs, check_vma=False
    )
```

time: 245 us -> 82.6 us (0.34)
  blocking collectives: 89.3 us -> 10.2 us
  matrix products: 62.7 us -> 0 us
  starting transfers between devices: 48.1 us -> 14.2 us
  Pallas kernels: 0 us -> 23.3 us
  waiting for transfers between devices: 10.1 us -> 30.5 us
  loops' own time: 13.5 us -> 0 us
  between operations: 7 us -> 0.8 us
  other arithmetic: 5.43 us -> 0.15 us
  local copies, waits for them, and re-layouts: 7.45 us -> 3.25 us
    psum x2 -> x0, blocking collectives: 89.3 us -> none  [paired_sums(): lax.psum((jnp.sum(residual * precond), jnp.sum(precond * image)), ('heigh...]
    dot_general x76 -> x0, matrix products: 62.7 us -> none  [the longest x36 41 us: row_forces(): cross = jnp.einsum('cip,ciq->ipq', places, other_places, precision=highest)]
    ppermute x17 -> x10, starting transfers between devices: 48.1 us -> 14.2 us  [the longest x8 11 us: exchanged(): lax.ppermute(value, ('height', 'cols'), matching(heights, groups, axis, o...]
    pallas_call x0 -> x3, Pallas kernels: none -> 23.3 us  [the longest x1 20.1 us: particles(): pl.pallas_call(functools.partial(particles_kernel, rows=rows, cols=cols),...]
    ppermute x17 -> x10, waiting for transfers between devices: 10.1 us -> 30.5 us  [the longest x8 30.4 us: exchanged(): lax.ppermute(value, ('height', 'cols'), matching(heights, groups, axis, o...]
    another operation x2 -> x0, loops' own time: 13.5 us -> none  [tile_forces(): stacked = lax.map(one_row, jnp.arange(count, dtype=jnp.int32))]
    all_to_all x0 -> x1, blocking collectives: none -> 10.2 us  [on_device(): dots = lax.all_to_all(dots, ('height', 'cols'), 0, 0, tiled=True)]
    unnamed x40 -> x22, local copies, waits for them, and re-layouts: 4.57 us -> 1.39 us
  transfers between devices with their start and end apart: 17 -> 10, of which waited for: 8 -> 4; matrix products, arithmetic and copies ran while one was open for 1% -> 0% of each run, Pallas kernels for 0% -> 24%
where the time goes in v1:
time: 82.6 us; the launch traced here: 82.3 us
  waiting for transfers between devices  30.5 us (37%)
  Pallas kernels  23.3 us (28%)
  starting transfers between devices  14.2 us (17%)
  blocking collectives  10.2 us (12%)
  local copies, waits for them, and re-layouts  3.25 us (4%)
    ppermute x8, waiting for transfers between devices, exchanged(): lax.ppermute(value, ('height', 'cols'), matching(heights, groups, axis, o...  30.4 us
    pallas_call x1, Pallas kernels, particles(): pl.pallas_call(functools.partial(particles_kernel, rows=rows, cols=cols),...  20.1 us
    ppermute x8, starting transfers between devices, exchanged(): lax.ppermute(value, ('height', 'cols'), matching(heights, groups, axis, o...  11 us
    all_to_all x1, blocking collectives, on_device(): dots = lax.all_to_all(dots, ('height', 'cols'), 0, 0, tiled=True)  10.2 us
    ppermute x2, starting transfers between devices, on_device(): lax.ppermute(value, ('height', 'cols'), matching(heights, groups, 'cols',...  3.16 us
    pallas_call x1, Pallas kernels, results_of(): pl.pallas_call(results_kernel, out_shape=(particle, particle, cells, cell...  1.68 us
  transfers between devices with their start and end apart: 10, of which 4 were waited for; matrix products, arithmetic and copies ran while one was open for 0% of the time, Pallas kernels for 24%

profile of v1, /device:TPU:0, one launch (start us, length us, event | category | flops | bytes accessed | tf_op | source)
XLA Modules:
  0.0 82.3 jit_solution(11882854315761666729)
XLA Ops:
  0.6 0.0 copy-start.8
  0.7 0.7 copy-done.8
  1.3 0.8 fusion.2
  2.1 0.0 copy-start.7
  2.2 0.0 copy-start.6
  2.2 0.8 fusion.3
  3.0 0.0 copy-start
  3.0 0.0 copy-start.1
  3.0 0.1 pad.24.clone
  3.1 0.0 copy-done.7
  3.1 0.0 copy-done.6
  3.1 0.1 maximum_maximum_fusion
  3.2 0.5 collective-permute-start.1
  3.8 2.6 %collective-permute-start = (f32[2,2,16,128]{3,2,1,0:T(8,128)S(1)}, f32[2,2,16,128]{3,2,1,0:T(8,128)S(1)}, u32[]{:S(2)}, u32[]{:S(2)}) collective-permute-start(f32[2,2,16,128]{3,2,1,0:T(8,128)S(1)} %get-tuple-element.25), channel_id=1, source_target_pairs={{0,3},{1,2},{2,1},{3,0},{4,7},{5,6},{6,5},{7,4},{8,11},{9,10},{10,... | collective-permute-start | bytes 98312 | tf_op jit(solution)/shard_map/ppermute | solution.py:503
  6.4 0.0 copy-done
  6.4 0.0 copy-done.1
  6.5 0.1 collective-permute-start.9
  6.6 3.0 %collective-permute-start.8 = (f32[2,2,64,512]{3,2,1,0:T(8,128)S(1)}, f32[2,2,64,512]{3,2,1,0:T(8,128)S(1)}, u32[]{:S(2)}, u32[]{:S(2)}) collective-permute-start(f32[2,2,64,512]{3,2,1,0:T(8,128)S(1)} %pad_maximum_fusion), channel_id=1, source_target_pairs={{0,4},{1,5},{2,6},{3,7},{4,0},{5,1},{6,2},{7,3},{8,12},{9,13},{10,... | collective-permute-start | bytes 1572872 | tf_op jit(solution)/shard_map/ppermute | solution.py:268
  9.6 0.0 collective-permute-done.1.line_a
  9.6 0.0 collective-permute-done.line_b
  9.6 0.1 collective-permute-start.3
  9.7 3.0 %collective-permute-start.2 = (f32[2,14,8,128]{3,2,1,0:T(8,128)S(1)}, f32[2,14,8,128]{3,2,1,0:T(8,128)S(1)}, u32[]{:S(2)}, u32[]{:S(2)}) collective-permute-start(f32[2,14,8,128]{3,2,1,0:T(8,128)S(1)} %constant_dynamic-update-slice_fusion.own_ref), channel_id=1, source_target_pairs={{0,4},{1,5},{2,6},{3,7},{4,0},{5,1},{6,2},{7,3},{8,12},{9,13},{10,... | collective-permute-start | bytes 344072 | tf_op jit(solution)/shard_map/ppermute | solution.py:268
  12.7 0.0 copy-start.4
  12.7 0.0 copy-start.2
  12.7 0.1 stack.41
  12.9 0.0 copy-start.3
  12.9 0.0 collective-permute-done.3.second_ref.corner_b
  12.9 23.6 %collective-permute-done.2.first_ref.corner_a = f32[2,14,8,128]{3,2,1,0:T(8,128)S(1)} collective-permute-done((f32[2,14,8,128]{3,2,1,0:T(8,128)S(1)}, f32[2,14,8,128]{3,2,1,0:T(8,128)S(1)}, u32[]{:S(2)}, u32[]{:S(2)}) %collective-permute-start.2) | collective-permute-done | bytes 114720 | tf_op jit(solution)/shard_map/ppermute | solution.py:268
  36.5 0.0 copy-done.4
  36.5 0.0 copy-done.2
  36.5 0.0 copy-done.3
  36.5 20.1 %particles.1 = (f32[24,128]{1,0:T(8,128)S(1)}, f32[2,8,8,128]{3,2,1,0:T(8,128)S(1)}, f32[8,8,128]{2,1,0:T(8,128)S(1)}) custom-call(s32[8]{0:T(128)S(1)} %convert_element_type.8.where_ref, s32[2,8]{1,0:T(2,128)S(1)} %copy-done.3, s32[2,8]{1,0:T(2,128)S(1)} %copy-done.4, f32[2,14,8,128]{3,2,1,0:T(8,128)S(1)} %constant_dynamic-update-slice_fusion.own_ref, ...), custom_call_target="tpu_custom_call" | custom-call | tf_op jit(solution)/shard_map/particles/pallas_call | solution.py:229
  56.6 0.2 collective-permute-start.5
  56.8 0.5 collective-permute-start.4
  57.3 2.5 %collective-permute-done.5.side_b = f32[24,128]{1,0:T(8,128)S(1)} collective-permute-done((f32[24,128]{1,0:T(8,128)S(1)}, f32[24,128]{1,0:T(8,128)S(1)}, u32[]{:S(2)}, u32[]{:S(2)}) %collective-permute-start.5) | collective-permute-done | bytes 12320 | tf_op jit(solution)/shard_map/ppermute | solution.py:268
  59.7 0.0 collective-permute-done.4.side_a
  59.8 3.6 %collective-permute-start.7 = (f32[136,128]{1,0:T(8,128)S(1)}, f32[136,128]{1,0:T(8,128)S(1)}, u32[]{:S(2)}, u32[]{:S(2)}) collective-permute-start(f32[136,128]{1,0:T(8,128)S(1)} %pad_maximum_fusion.1), channel_id=1, source_target_pairs={{0,28},{1,29},{2,30},{3,31},{4,8},{5,9},{6,10},{7,11},{8,4},{9,5},... | collective-permute-start | bytes 208904 | tf_op jit(solution)/shard_map/ppermute | solution.py:268
  63.4 0.5 collective-permute-start.6
  63.9 3.0 %collective-permute-done.7.height_b = f32[136,128]{1,0:T(8,128)S(1)} collective-permute-done((f32[136,128]{1,0:T(8,128)S(1)}, f32[136,128]{1,0:T(8,128)S(1)}, u32[]{:S(2)}, u32[]{:S(2)}) %collective-permute-start.7) | collective-permute-done | bytes 69664 | tf_op jit(solution)/shard_map/ppermute | solution.py:268
  66.9 1.3 %collective-permute-done.6.height_a = f32[136,128]{1,0:T(8,128)S(1)} collective-permute-done((f32[136,128]{1,0:T(8,128)S(1)}, f32[136,128]{1,0:T(8,128)S(1)}, u32[]{:S(2)}, u32[]{:S(2)}) %collective-permute-start.6) | collective-permute-done | bytes 69664 | tf_op jit(solution)/shard_map/ppermute | solution.py:268
  68.2 0.0 collective-permute-done.9.gas_b
  68.2 0.0 collective-permute-done.8.gas_a
  68.2 1.6 %right_side.1 = (f32[2,64,512]{2,1,0:T(8,128)S(1)}, f32[2,64,512]{2,1,0:T(8,128)S(1)}, f32[2,64,512]{2,1,0:T(8,128)S(1)}, f32[32,128]{1,0:T(8,128)S(1)}) custom-call(s32[8]{0:T(128)S(1)} %convert_element_type.8.where_ref, f32[24,128]{1,0:T(8,128)S(1)} %get-tuple-element.11.sums_ref, f32[24,128]{1,0:T(8,128)S(1)} %collective-permute-done.4.side_a, ...), custom_call_target="tpu_custom_call" | custom-call | tf_op jit(solution)/shard_map/right_side/pallas_call | solution.py:398
  69.8 10.2 %all_to_all.11 = f32[32,1,128]{2,1,0:T(1,128)S(1)} all-to-all(f32[32,1,128]{2,1,0:T(1,128)S(1)} %bitcast.26), channel_id=1, replica_groups=mesh['height'=8,'cols'=4] {'height','cols'}, dimensions={0} | all-to-all | bytes 32768 | tf_op jit(solution)/shard_map/all_to_all | solution.py:520
  79.9 0.0 copy-start.5
  79.9 0.7 copy-done.5
  80.6 1.7 %results.1 = (f32[3,2,8,128]{3,2,1,0:T(8,128)}, f32[3,2,8,128]{3,2,1,0:T(8,128)}, f32[2,64,512]{2,1,0:T(8,128)}, f32[2,64,512]{2,1,0:T(8,128)}) custom-call(s32[8]{0:T(128)S(1)} %convert_element_type.8.where_ref, s32[2,8]{1,0:T(2,128)S(1)} %copy-done.3, s32[1,8]{1,0:T(1,128)S(1)} %copy-done.5, f32[32,128]{1,0:T(8,128)S(1)} %bitcast.24, ...), custom_call_target="tpu_custom_call" | custom-call | tf_op jit(solution)/shard_map/results/pallas_call | solution.py:455
  (18 shorter events, 0.2 us)
Async XLA Ops:
  0.6 0.7 copy-start.8
  2.1 1.0 %copy-start.7 = (f32[3,2,8,128]{3,2,1,0:T(8,128)S(1)}, f32[3,2,8,128]{3,2,1,0:T(8,128)}, u32[]{:S(2)}) copy-start(f32[3,2,8,128]{3,2,1,0:T(8,128)} %param.9) | copy-start | bytes 73732
  2.2 0.9 %copy-start.6 = (f32[3,2,8,128]{3,2,1,0:T(8,128)S(1)}, f32[3,2,8,128]{3,2,1,0:T(8,128)}, u32[]{:S(2)}) copy-start(f32[3,2,8,128]{3,2,1,0:T(8,128)} %param.10) | copy-start | bytes 73732
  3.0 3.4 %copy-start = (f32[2,64,512]{2,1,0:T(8,128)S(1)}, f32[2,64,512]{2,1,0:T(8,128)}, u32[]{:S(2)}) copy-start(f32[2,64,512]{2,1,0:T(8,128)} %diagonal_ref.3) | copy-start | bytes 786436
  3.0 3.4 %copy-start.1 = (f32[2,64,512]{2,1,0:T(8,128)S(1)}, f32[2,64,512]{2,1,0:T(8,128)}, u32[]{:S(2)}) copy-start(f32[2,64,512]{2,1,0:T(8,128)} %gas_ref.1) | copy-start | bytes 786436
  3.2 6.3 %collective-permute-start.1 = (f32[2,2,16,128]{3,2,1,0:T(8,128)S(1)}, f32[2,2,16,128]{3,2,1,0:T(8,128)S(1)}, u32[]{:S(2)}, u32[]{:S(2)}) collective-permute-start(f32[2,2,16,128]{3,2,1,0:T(8,128)S(1)} %get-tuple-element.24), channel_id=1, source_target_pairs={{0,1},{1,0},{2,3},{3,2},{4,5},{5,4},{6,7},{7,6},{8,9},{9,8},{10,11... | collective-permute-start | bytes 98312 | tf_op jit(solution)/shard_map/ppermute | solution.py:503
  3.8 5.8 %collective-permute-start = (f32[2,2,16,128]{3,2,1,0:T(8,128)S(1)}, f32[2,2,16,128]{3,2,1,0:T(8,128)S(1)}, u32[]{:S(2)}, u32[]{:S(2)}) collective-permute-start(f32[2,2,16,128]{3,2,1,0:T(8,128)S(1)} %get-tuple-element.25), channel_id=1, source_target_pairs={{0,3},{1,2},{2,1},{3,0},{4,7},{5,6},{6,5},{7,4},{8,11},{9,10},{10,... | collective-permute-start | bytes 98312 | tf_op jit(solution)/shard_map/ppermute | solution.py:503
  6.5 61.8 %collective-permute-start.9 = (f32[2,2,64,512]{3,2,1,0:T(8,128)S(1)}, f32[2,2,64,512]{3,2,1,0:T(8,128)S(1)}, u32[]{:S(2)}, u32[]{:S(2)}) collective-permute-start(f32[2,2,64,512]{3,2,1,0:T(8,128)S(1)} %pad_maximum_fusion), channel_id=1, source_target_pairs={{0,1},{1,0},{2,3},{3,2},{4,8},{5,9},{6,10},{7,11},{8,4},{9,5},{10,... | collective-permute-start | bytes 1572872 | tf_op jit(solution)/shard_map/ppermute | solution.py:268
  6.6 61.6 %collective-permute-start.8 = (f32[2,2,64,512]{3,2,1,0:T(8,128)S(1)}, f32[2,2,64,512]{3,2,1,0:T(8,128)S(1)}, u32[]{:S(2)}, u32[]{:S(2)}) collective-permute-start(f32[2,2,64,512]{3,2,1,0:T(8,128)S(1)} %pad_maximum_fusion), channel_id=1, source_target_pairs={{0,4},{1,5},{2,6},{3,7},{4,0},{5,1},{6,2},{7,3},{8,12},{9,13},{10,... | collective-permute-start | bytes 1572872 | tf_op jit(solution)/shard_map/ppermute | solution.py:268
  9.6 3.2 %collective-permute-start.3 = (f32[2,14,8,128]{3,2,1,0:T(8,128)S(1)}, f32[2,14,8,128]{3,2,1,0:T(8,128)S(1)}, u32[]{:S(2)}, u32[]{:S(2)}) collective-permute-start(f32[2,14,8,128]{3,2,1,0:T(8,128)S(1)} %constant_dynamic-update-slice_fusion.own_ref), channel_id=1, source_target_pairs={{0,1},{1,0},{2,3},{3,2},{4,8},{5,9},{6,10},{7,11},{8,4},{9,5},{10,... | collective-permute-start | bytes 344072 | tf_op jit(solution)/shard_map/ppermute | solution.py:268
  9.7 26.8 %collective-permute-start.2 = (f32[2,14,8,128]{3,2,1,0:T(8,128)S(1)}, f32[2,14,8,128]{3,2,1,0:T(8,128)S(1)}, u32[]{:S(2)}, u32[]{:S(2)}) collective-permute-start(f32[2,14,8,128]{3,2,1,0:T(8,128)S(1)} %constant_dynamic-update-slice_fusion.own_ref), channel_id=1, source_target_pairs={{0,4},{1,5},{2,6},{3,7},{4,0},{5,1},{6,2},{7,3},{8,12},{9,13},{10,... | collective-permute-start | bytes 344072 | tf_op jit(solution)/shard_map/ppermute | solution.py:268
  12.7 23.7 %copy-start.4 = (s32[2,8]{1,0:T(2,128)S(1)}, s32[2,8]{1,0:T(2,128)}, u32[]{:S(2)}) copy-start(s32[2,8]{1,0:T(2,128)} %owners_ref.1) | copy-start | bytes 196
  12.7 23.7 %copy-start.2 = (s32[2,8,128]{2,1,0:T(8,128)S(1)}, s32[2,8,128]{2,1,0:T(8,128)}, u32[]{:S(2)}) copy-start(s32[2,8,128]{2,1,0:T(8,128)} %slots_ref.1) | copy-start | bytes 24580
  12.9 23.6 %copy-start.3 = (s32[2,8]{1,0:T(2,128)S(1)}, s32[2,8]{1,0:T(2,128)}, u32[]{:S(2)}) copy-start(s32[2,8]{1,0:T(2,128)} %exits_ref.3) | copy-start | bytes 196
  56.6 3.2 %collective-permute-start.5 = (f32[24,128]{1,0:T(8,128)S(1)}, f32[24,128]{1,0:T(8,128)S(1)}, u32[]{:S(2)}, u32[]{:S(2)}) collective-permute-start(f32[24,128]{1,0:T(8,128)S(1)} %get-tuple-element.11.sums_ref), channel_id=1, source_target_pairs={{0,3},{1,2},{2,1},{3,0},{4,7},{5,6},{6,5},{7,4},{8,11},{9,10},{10,... | collective-permute-start | bytes 36872 | tf_op jit(solution)/shard_map/ppermute | solution.py:268
  56.8 3.0 %collective-permute-start.4 = (f32[24,128]{1,0:T(8,128)S(1)}, f32[24,128]{1,0:T(8,128)S(1)}, u32[]{:S(2)}, u32[]{:S(2)}) collective-permute-start(f32[24,128]{1,0:T(8,128)S(1)} %get-tuple-element.11.sums_ref), channel_id=1, source_target_pairs={{0,1},{1,0},{2,3},{3,2},{4,5},{5,4},{6,7},{7,6},{8,9},{9,8},{10,11... | collective-permute-start | bytes 36872 | tf_op jit(solution)/shard_map/ppermute | solution.py:268
  59.8 7.1 %collective-permute-start.7 = (f32[136,128]{1,0:T(8,128)S(1)}, f32[136,128]{1,0:T(8,128)S(1)}, u32[]{:S(2)}, u32[]{:S(2)}) collective-permute-start(f32[136,128]{1,0:T(8,128)S(1)} %pad_maximum_fusion.1), channel_id=1, source_target_pairs={{0,28},{1,29},{2,30},{3,31},{4,8},{5,9},{6,10},{7,11},{8,4},{9,5},... | collective-permute-start | bytes 208904 | tf_op jit(solution)/shard_map/ppermute | solution.py:268
  63.4 4.8 %collective-permute-start.6 = (f32[136,128]{1,0:T(8,128)S(1)}, f32[136,128]{1,0:T(8,128)S(1)}, u32[]{:S(2)}, u32[]{:S(2)}) collective-permute-start(f32[136,128]{1,0:T(8,128)S(1)} %pad_maximum_fusion.1), channel_id=1, source_target_pairs={{0,4},{1,5},{2,6},{3,7},{4,0},{5,1},{6,2},{7,3},{8,12},{9,13},{10,... | collective-permute-start | bytes 208904 | tf_op jit(solution)/shard_map/ppermute | solution.py:268
  79.9 0.7 copy-start.5

commit v2 on v1

--- a/solution.py
+++ b/solution.py
@@ -99,16 +99,11 @@
         weights.append(jnp.concatenate(spread, axis=0))
     total = jnp.zeros((16, 2 * LANES), f32)
     for i in range(3):
-        for half in range(2):
-            parts = []
-            pulls = []
-            for j in (2 * half, 2 * half + 1):
-                s = c - 1 + j
-                near = jnp.dot(turned[r + i - 1, s // 4], weights[s % 4], preferred_element_type=f32)
-                parts.append(jnp.maximum(near, 0.0))
-                pulls.append(pulled[r + i - 1, s])
-            pulls = jnp.concatenate(pulls, axis=1)
-            weight = jnp.concatenate(parts, axis=0)
+        for j in range(4):
+            s = c - 1 + j
+            near = jnp.dot(turned[r + i - 1, s // 4], weights[s % 4], preferred_element_type=f32)
+            weight = jnp.maximum(near, 0.0)
+            pulls = pulled[r + i - 1, s]
             high = weight.astype(bf16)
             total = total + jnp.dot(pulls, high, preferred_element_type=f32)
             low = (weight - high.astype(f32)).astype(bf16)
@@ -187,20 +182,24 @@
             for k in range(2):
                 done = stepped(tiles[k], forces[k])
                 settled_ref[r - DEPTH, c + k - DEPTH] = done
-                lift = deposit_gain * done[5:6, :]
-                lift_high, lift_mid, lift_low = split(lift)
-                row = lax.broadcasted_iota(i32, (16, LANES), 0)
-                parts = jnp.where(
-                    row == 0, lift_high, jnp.where(row == 1, lift_mid, jnp.where(row == 2, lift_low, 0.0))
-                ).astype(bf16)
-                cell = lax.broadcasted_iota(i32, (LANES, LANES), 0)
-                slots = slots_ref[r - DEPTH, c + k - DEPTH : c + k - DEPTH + 1, :]
-                table = jnp.where(cell == slots, 1.0, 0.0).astype(bf16)
-                gathered = lax.dot_general(parts, table, (((1,), (1,)), ((), ())), preferred_element_type=f32)
-                sums_ref[pl.ds((r - DEPTH) * cols + c + k - DEPTH, 1), :] = jnp.sum(gathered, axis=0, keepdims=True)
         return carry
 
     lax.fori_loop(DEPTH, DEPTH + rows, second_step, 0)
+
+    def deposit(r, carry):
+        row = lax.broadcasted_iota(i32, (16, LANES), 0)
+        cell = lax.broadcasted_iota(i32, (LANES, LANES), 0)
+        for c in range(cols):
+            lift_high, lift_mid, lift_low = split(deposit_gain * settled_ref[r, c, 5:6, :])
+            parts = jnp.where(row == 0, lift_high, jnp.where(row == 1, lift_mid, jnp.where(row == 2, lift_low, 0.0)))
+            table = jnp.where(cell == slots_ref[r, c : c + 1, :], 1.0, 0.0).astype(bf16)
+            gathered = lax.dot_general(
+                parts.astype(bf16), table, (((1,), (1,)), ((), ())), preferred_element_type=f32
+            )
+            sums_ref[pl.ds(r * cols + c, 1), :] = jnp.sum(gathered, axis=0, keepdims=True)
+        return carry
+
+    lax.fori_loop(0, rows, deposit, 0)
 
     lane = lax.broadcasted_iota(i32, (1, LANES), 1)
     owner_row = jnp.zeros((1, LANES), i32)
@@ -509,7 +508,8 @@
         [low[:, :, :COMPS], tiles, high[:, :, :COMPS], low[:, 1:2, COMPS:], high[:, 0:1, COMPS:]], axis=1
     )
     beside = exchanged(window, "height", False)
-    gases = exchanged(jnp.stack([gas_source, diagonal]), "height", False)
+    cells, beside = lax.optimization_barrier((jnp.stack([gas_source, diagonal]), beside))
+    gases = exchanged(cells, "height", False)
     sums, settled, leaving = particles(where, exit_flags, cell_blocks, window, *beside, cell_slots)
     sides = exchanged(sums, "cols", True)
     parcel = jnp.concatenate([sums, *sides, leaving.reshape(cols * COMPS, LANES)], axis=0)

time: 82.6 us -> 65 us (0.79)
  waiting for transfers between devices: 30.5 us -> 13 us
  Pallas kernels: 23.3 us -> 20.4 us
  starting transfers between devices: 14.2 us -> 15.6 us
  local copies, waits for them, and re-layouts: 3.25 us -> 4.51 us
    ppermute x8, waiting for transfers between devices: 30.4 us -> 11.3 us  [exchanged(): lax.ppermute(value, ('height', 'cols'), matching(heights, groups, axis, o...]
    pallas_call x1, Pallas kernels: 20.1 us -> 17.1 us  [particles(): pl.pallas_call(functools.partial(particles_kernel, rows=rows, cols=cols),...]
    ppermute x2, waiting for transfers between devices: 0.01 us -> 1.67 us  [on_device(): lax.ppermute(value, ('height', 'cols'), matching(heights, groups, 'cols',...]
    ppermute x8, starting transfers between devices: 11 us -> 12.4 us  [exchanged(): lax.ppermute(value, ('height', 'cols'), matching(heights, groups, axis, o...]
    unnamed x22, local copies, waits for them, and re-layouts: 1.39 us -> 2.66 us
  transfers between devices with their start and end apart: 10 -> 10, of which waited for: 4 -> 5; matrix products, arithmetic and copies ran while one was open for 0% -> 0% of each run, Pallas kernels for 24% -> 26%
where the time goes in v2:
time: 65 us; the launch traced here: 64.6 us
  Pallas kernels  20.4 us (31%)
  starting transfers between devices  15.6 us (24%)
  waiting for transfers between devices  13 us (20%)
  blocking collectives  10.3 us (16%)
  local copies, waits for them, and re-layouts  4.51 us (7%)
  between operations  0.79 us (1%)
    pallas_call x1, Pallas kernels, particles(): pl.pallas_call(functools.partial(particles_kernel, rows=rows, cols=cols),...  17.1 us
    ppermute x8, starting transfers between devices, exchanged(): lax.ppermute(value, ('height', 'cols'), matching(heights, groups, axis, o...  12.4 us
    ppermute x8, waiting for transfers between devices, exchanged(): lax.ppermute(value, ('height', 'cols'), matching(heights, groups, axis, o...  11.3 us
    all_to_all x1, blocking collectives, on_device(): dots = lax.all_to_all(dots, ('height', 'cols'), 0, 0, tiled=True)  10.3 us
    ppermute x2, starting transfers between devices, on_device(): lax.ppermute(value, ('height', 'cols'), matching(heights, groups, 'cols',...  3.16 us
    unnamed x22, local copies, waits for them, and re-layouts  2.66 us
    pallas_call x1, Pallas kernels, results_of(): pl.pallas_call(results_kernel, out_shape=(particle, particle, cells, cell...  1.68 us
    ppermute x2, waiting for transfers between devices, on_device(): lax.ppermute(value, ('height', 'cols'), matching(heights, groups, 'cols',...  1.67 us
  transfers between devices with their start and end apart: 10, of which 5 were waited for; matrix products, arithmetic and copies ran while one was open for 0% of the time, Pallas kernels for 26%

profile of v2, /device:TPU:0, one launch (start us, length us, event | category | flops | bytes accessed | tf_op | source)
XLA Modules:
  0.0 64.6 jit_solution(6302646050681699189)
XLA Ops:
  0.6 0.0 copy-start.8
  0.7 0.7 %copy-done.8 = s32[9,2,8]{0,2,1:T(8,128)S(1)} copy-done((s32[9,2,8]{0,2,1:T(8,128)S(1)}, s32[9,2,8]{0,2,1:T(8,128)}, u32[]{:S(2)}) %copy-start.8) | copy-done | bytes 600
  1.3 0.8 %fusion.2 = (f32[2,2,512]{2,1,0:T(2,128)S(1)}, f32[2,2,512]{2,1,0:T(2,128)S(1)}) fusion(f32[2,64,512]{2,1,0:T(8,128)} %gas_ref.1), kind=kLoop, calls=%fused_computation.17 | loop fusion | bytes 32768 | tf_op jit(solution)/shard_map/slice | solution.py:492
  2.2 0.8 %fusion.3 = (f32[2,2,512]{2,1,0:T(2,128)S(1)}, f32[2,2,512]{2,1,0:T(2,128)S(1)}) fusion(f32[2,64,512]{2,1,0:T(8,128)} %diagonal_ref.3), kind=kLoop, calls=%fused_computation.18 | loop fusion | bytes 32768 | tf_op jit(solution)/shard_map/slice | solution.py:493
  2.9 0.0 copy-start.6
  2.9 0.0 copy-start.7
  3.0 0.1 pad.24.clone
  3.1 0.6 copy-done.6
  3.7 0.0 copy-done.7
  3.7 0.1 maximum_maximum_fusion
  3.8 0.0 copy-start.1
  3.8 0.0 copy-start
  3.8 0.5 collective-permute-start.1
  4.4 2.6 %collective-permute-start = (f32[2,2,16,128]{3,2,1,0:T(8,128)S(1)}, f32[2,2,16,128]{3,2,1,0:T(8,128)S(1)}, u32[]{:S(2)}, u32[]{:S(2)}) collective-permute-start(f32[2,2,16,128]{3,2,1,0:T(8,128)S(1)} %get-tuple-element.31), channel_id=1, source_target_pairs={{0,3},{1,2},{2,1},{3,0},{4,7},{5,6},{6,5},{7,4},{8,11},{9,10},{10,... | collective-permute-start | bytes 98312 | tf_op jit(solution)/shard_map/ppermute | solution.py:502
  7.0 0.0 collective-permute-done.1.line_a
  7.0 1.7 %collective-permute-done.line_b = f32[2,2,16,128]{3,2,1,0:T(8,128)S(1)} collective-permute-done((f32[2,2,16,128]{3,2,1,0:T(8,128)S(1)}, f32[2,2,16,128]{3,2,1,0:T(8,128)S(1)}, u32[]{:S(2)}, u32[]{:S(2)}) %collective-permute-start) | collective-permute-done | bytes 32800 | tf_op jit(solution)/shard_map/ppermute | solution.py:502
  8.7 0.2 collective-permute-start.3
  8.9 3.0 %collective-permute-start.2 = (f32[2,14,8,128]{3,2,1,0:T(8,128)S(1)}, f32[2,14,8,128]{3,2,1,0:T(8,128)S(1)}, u32[]{:S(2)}, u32[]{:S(2)}) collective-permute-start(f32[2,14,8,128]{3,2,1,0:T(8,128)S(1)} %constant_dynamic-update-slice_fusion.own_ref), channel_id=1, source_target_pairs={{0,4},{1,5},{2,6},{3,7},{4,0},{5,1},{6,2},{7,3},{8,12},{9,13},{10,... | collective-permute-start | bytes 344072 | tf_op jit(solution)/shard_map/ppermute | solution.py:267
  12.0 0.0 copy-done.1
  12.0 0.0 copy-done
  12.0 0.0 collective-permute-done.3.second_ref.corner_b
  12.0 4.8 %collective-permute-done.2.first_ref.corner_a = f32[2,14,8,128]{3,2,1,0:T(8,128)S(1)} collective-permute-done((f32[2,14,8,128]{3,2,1,0:T(8,128)S(1)}, f32[2,14,8,128]{3,2,1,0:T(8,128)S(1)}, u32[]{:S(2)}, u32[]{:S(2)}) %collective-permute-start.2) | collective-permute-done | bytes 114720 | tf_op jit(solution)/shard_map/ppermute | solution.py:267
  16.8 0.0 collective-permute-start.9
  16.8 4.0 %collective-permute-start.8 = (f32[2,2,64,512]{3,2,1,0:T(8,128)S(1)}, f32[2,2,64,512]{3,2,1,0:T(8,128)S(1)}, u32[]{:S(2)}, u32[]{:S(2)}) collective-permute-start(f32[2,2,64,512]{3,2,1,0:T(8,128)S(1)} %pad_maximum_fusion), channel_id=1, source_target_pairs={{0,4},{1,5},{2,6},{3,7},{4,0},{5,1},{6,2},{7,3},{8,12},{9,13},{10,... | collective-permute-start | bytes 1572872 | tf_op jit(solution)/shard_map/ppermute | solution.py:267
  20.8 0.0 copy-start.4
  20.8 0.0 copy-start.2
  20.8 0.1 stack.41
  20.9 0.0 copy-start.3
  20.9 0.6 copy-done.4
  21.5 0.0 copy-done.2
  21.5 0.1 copy-done.3
  21.6 17.1 %particles.1 = (f32[24,128]{1,0:T(8,128)S(1)}, f32[2,8,8,128]{3,2,1,0:T(8,128)S(1)}, f32[8,8,128]{2,1,0:T(8,128)S(1)}) custom-call(s32[8]{0:T(128)S(1)} %convert_element_type.8.where_ref, s32[2,8]{1,0:T(2,128)S(1)} %copy-done.3, s32[2,8]{1,0:T(2,128)S(1)} %copy-done.4, f32[2,14,8,128]{3,2,1,0:T(8,128)S(1)} %constant_dynamic-update-slice_fusion.own_ref, ...), custom_call_target="tpu_custom_call" | custom-call | tf_op jit(solution)/shard_map/particles/pallas_call | solution.py:228
  38.7 0.7 %collective-permute-start.5 = (f32[24,128]{1,0:T(8,128)S(1)}, f32[24,128]{1,0:T(8,128)S(1)}, u32[]{:S(2)}, u32[]{:S(2)}) collective-permute-start(f32[24,128]{1,0:T(8,128)S(1)} %get-tuple-element.16.sums_ref), channel_id=1, source_target_pairs={{0,3},{1,2},{2,1},{3,0},{4,7},{5,6},{6,5},{7,4},{8,11},{9,10},{10,... | collective-permute-start | bytes 36872 | tf_op jit(solution)/shard_map/ppermute | solution.py:267
  39.4 1.0 %collective-permute-start.4 = (f32[24,128]{1,0:T(8,128)S(1)}, f32[24,128]{1,0:T(8,128)S(1)}, u32[]{:S(2)}, u32[]{:S(2)}) collective-permute-start(f32[24,128]{1,0:T(8,128)S(1)} %get-tuple-element.16.sums_ref), channel_id=1, source_target_pairs={{0,1},{1,0},{2,3},{3,2},{4,5},{5,4},{6,7},{7,6},{8,9},{9,8},{10,11... | collective-permute-start | bytes 36872 | tf_op jit(solution)/shard_map/ppermute | solution.py:267
  40.4 1.5 %collective-permute-done.5.side_b = f32[24,128]{1,0:T(8,128)S(1)} collective-permute-done((f32[24,128]{1,0:T(8,128)S(1)}, f32[24,128]{1,0:T(8,128)S(1)}, u32[]{:S(2)}, u32[]{:S(2)}) %collective-permute-start.5) | collective-permute-done | bytes 12320 | tf_op jit(solution)/shard_map/ppermute | solution.py:267
  42.0 0.0 collective-permute-done.4.side_a
  42.0 3.5 %collective-permute-start.7 = (f32[136,128]{1,0:T(8,128)S(1)}, f32[136,128]{1,0:T(8,128)S(1)}, u32[]{:S(2)}, u32[]{:S(2)}) collective-permute-start(f32[136,128]{1,0:T(8,128)S(1)} %pad_maximum_fusion.1), channel_id=1, source_target_pairs={{0,28},{1,29},{2,30},{3,31},{4,8},{5,9},{6,10},{7,11},{8,4},{9,5},... | collective-permute-start | bytes 208904 | tf_op jit(solution)/shard_map/ppermute | solution.py:267
  45.5 0.0 collective-permute-start.6
  45.5 3.7 %collective-permute-done.7.height_b = f32[136,128]{1,0:T(8,128)S(1)} collective-permute-done((f32[136,128]{1,0:T(8,128)S(1)}, f32[136,128]{1,0:T(8,128)S(1)}, u32[]{:S(2)}, u32[]{:S(2)}) %collective-permute-start.7) | collective-permute-done | bytes 69664 | tf_op jit(solution)/shard_map/ppermute | solution.py:267
  49.1 1.3 %collective-permute-done.6.height_a = f32[136,128]{1,0:T(8,128)S(1)} collective-permute-done((f32[136,128]{1,0:T(8,128)S(1)}, f32[136,128]{1,0:T(8,128)S(1)}, u32[]{:S(2)}, u32[]{:S(2)}) %collective-permute-start.6) | collective-permute-done | bytes 69664 | tf_op jit(solution)/shard_map/ppermute | solution.py:267
  50.4 0.0 collective-permute-done.9.gas_b
  50.4 0.0 collective-permute-done.8.gas_a
  50.4 1.6 %right_side.1 = (f32[2,64,512]{2,1,0:T(8,128)S(1)}, f32[2,64,512]{2,1,0:T(8,128)S(1)}, f32[2,64,512]{2,1,0:T(8,128)S(1)}, f32[32,128]{1,0:T(8,128)S(1)}) custom-call(s32[8]{0:T(128)S(1)} %convert_element_type.8.where_ref, f32[24,128]{1,0:T(8,128)S(1)} %get-tuple-element.16.sums_ref, f32[24,128]{1,0:T(8,128)S(1)} %collective-permute-done.4.side_a, ...), custom_call_target="tpu_custom_call" | custom-call | tf_op jit(solution)/shard_map/right_side/pallas_call | solution.py:397
  52.0 10.3 %all_to_all.11 = f32[32,1,128]{2,1,0:T(1,128)S(1)} all-to-all(f32[32,1,128]{2,1,0:T(1,128)S(1)} %bitcast.26), channel_id=1, replica_groups=mesh['height'=8,'cols'=4] {'height','cols'}, dimensions={0} | all-to-all | bytes 32768 | tf_op jit(solution)/shard_map/all_to_all | solution.py:520
  62.3 0.0 copy-start.5
  62.3 0.7 %copy-done.5 = s32[1,8]{1,0:T(1,128)S(1)} copy-done((s32[1,8]{1,0:T(1,128)S(1)}, s32[1,8]{1,0:T(1,128)}, u32[]{:S(2)}) %copy-start.5) | copy-done | bytes 56
  62.9 1.7 %results.1 = (f32[3,2,8,128]{3,2,1,0:T(8,128)}, f32[3,2,8,128]{3,2,1,0:T(8,128)}, f32[2,64,512]{2,1,0:T(8,128)}, f32[2,64,512]{2,1,0:T(8,128)}) custom-call(s32[8]{0:T(128)S(1)} %convert_element_type.8.where_ref, s32[2,8]{1,0:T(2,128)S(1)} %copy-done.3, s32[1,8]{1,0:T(1,128)S(1)} %copy-done.5, f32[32,128]{1,0:T(8,128)S(1)} %bitcast.24, ...), custom_call_target="tpu_custom_call" | custom-call | tf_op jit(solution)/shard_map/results/pallas_call | solution.py:454
  (18 shorter events, 0.2 us)
Async XLA Ops:
  0.6 0.7 %copy-start.8 = (s32[9,2,8]{0,2,1:T(8,128)S(1)}, s32[9,2,8]{0,2,1:T(8,128)}, u32[]{:S(2)}) copy-start(s32[9,2,8]{0,2,1:T(8,128)} %param.11) | copy-start | bytes 1732
  2.9 0.7 %copy-start.6 = (f32[3,2,8,128]{3,2,1,0:T(8,128)S(1)}, f32[3,2,8,128]{3,2,1,0:T(8,128)}, u32[]{:S(2)}) copy-start(f32[3,2,8,128]{3,2,1,0:T(8,128)} %param.10) | copy-start | bytes 73732
  2.9 0.8 %copy-start.7 = (f32[3,2,8,128]{3,2,1,0:T(8,128)S(1)}, f32[3,2,8,128]{3,2,1,0:T(8,128)}, u32[]{:S(2)}) copy-start(f32[3,2,8,128]{3,2,1,0:T(8,128)} %param.9) | copy-start | bytes 73732
  3.8 8.2 %copy-start.1 = (f32[2,64,512]{2,1,0:T(8,128)S(1)}, f32[2,64,512]{2,1,0:T(8,128)}, u32[]{:S(2)}) copy-start(f32[2,64,512]{2,1,0:T(8,128)} %gas_ref.1) | copy-start | bytes 786436
  3.8 8.2 %copy-start = (f32[2,64,512]{2,1,0:T(8,128)S(1)}, f32[2,64,512]{2,1,0:T(8,128)}, u32[]{:S(2)}) copy-start(f32[2,64,512]{2,1,0:T(8,128)} %diagonal_ref.3) | copy-start | bytes 786436
  3.8 3.2 %collective-permute-start.1 = (f32[2,2,16,128]{3,2,1,0:T(8,128)S(1)}, f32[2,2,16,128]{3,2,1,0:T(8,128)S(1)}, u32[]{:S(2)}, u32[]{:S(2)}) collective-permute-start(f32[2,2,16,128]{3,2,1,0:T(8,128)S(1)} %get-tuple-element.30), channel_id=1, source_target_pairs={{0,1},{1,0},{2,3},{3,2},{4,5},{5,4},{6,7},{7,6},{8,9},{9,8},{10,11... | collective-permute-start | bytes 98312 | tf_op jit(solution)/shard_map/ppermute | solution.py:502
  4.4 4.3 %collective-permute-start = (f32[2,2,16,128]{3,2,1,0:T(8,128)S(1)}, f32[2,2,16,128]{3,2,1,0:T(8,128)S(1)}, u32[]{:S(2)}, u32[]{:S(2)}) collective-permute-start(f32[2,2,16,128]{3,2,1,0:T(8,128)S(1)} %get-tuple-element.31), channel_id=1, source_target_pairs={{0,3},{1,2},{2,1},{3,0},{4,7},{5,6},{6,5},{7,4},{8,11},{9,10},{10,... | collective-permute-start | bytes 98312 | tf_op jit(solution)/shard_map/ppermute | solution.py:502
  8.7 3.3 %collective-permute-start.3 = (f32[2,14,8,128]{3,2,1,0:T(8,128)S(1)}, f32[2,14,8,128]{3,2,1,0:T(8,128)S(1)}, u32[]{:S(2)}, u32[]{:S(2)}) collective-permute-start(f32[2,14,8,128]{3,2,1,0:T(8,128)S(1)} %constant_dynamic-update-slice_fusion.own_ref), channel_id=1, source_target_pairs={{0,1},{1,0},{2,3},{3,2},{4,8},{5,9},{6,10},{7,11},{8,4},{9,5},{10,... | collective-permute-start | bytes 344072 | tf_op jit(solution)/shard_map/ppermute | solution.py:267
  8.9 7.9 %collective-permute-start.2 = (f32[2,14,8,128]{3,2,1,0:T(8,128)S(1)}, f32[2,14,8,128]{3,2,1,0:T(8,128)S(1)}, u32[]{:S(2)}, u32[]{:S(2)}) collective-permute-start(f32[2,14,8,128]{3,2,1,0:T(8,128)S(1)} %constant_dynamic-update-slice_fusion.own_ref), channel_id=1, source_target_pairs={{0,4},{1,5},{2,6},{3,7},{4,0},{5,1},{6,2},{7,3},{8,12},{9,13},{10,... | collective-permute-start | bytes 344072 | tf_op jit(solution)/shard_map/ppermute | solution.py:267
  16.8 33.6 %collective-permute-start.9 = (f32[2,2,64,512]{3,2,1,0:T(8,128)S(1)}, f32[2,2,64,512]{3,2,1,0:T(8,128)S(1)}, u32[]{:S(2)}, u32[]{:S(2)}) collective-permute-start(f32[2,2,64,512]{3,2,1,0:T(8,128)S(1)} %pad_maximum_fusion), channel_id=1, source_target_pairs={{0,1},{1,0},{2,3},{3,2},{4,8},{5,9},{6,10},{7,11},{8,4},{9,5},{10,... | collective-permute-start | bytes 1572872 | tf_op jit(solution)/shard_map/ppermute | solution.py:267
  16.8 33.6 %collective-permute-start.8 = (f32[2,2,64,512]{3,2,1,0:T(8,128)S(1)}, f32[2,2,64,512]{3,2,1,0:T(8,128)S(1)}, u32[]{:S(2)}, u32[]{:S(2)}) collective-permute-start(f32[2,2,64,512]{3,2,1,0:T(8,128)S(1)} %pad_maximum_fusion), channel_id=1, source_target_pairs={{0,4},{1,5},{2,6},{3,7},{4,0},{5,1},{6,2},{7,3},{8,12},{9,13},{10,... | collective-permute-start | bytes 1572872 | tf_op jit(solution)/shard_map/ppermute | solution.py:267
  20.8 0.7 %copy-start.4 = (s32[2,8]{1,0:T(2,128)S(1)}, s32[2,8]{1,0:T(2,128)}, u32[]{:S(2)}) copy-start(s32[2,8]{1,0:T(2,128)} %owners_ref.1) | copy-start | bytes 196
  20.8 0.7 %copy-start.2 = (s32[2,8,128]{2,1,0:T(8,128)S(1)}, s32[2,8,128]{2,1,0:T(8,128)}, u32[]{:S(2)}) copy-start(s32[2,8,128]{2,1,0:T(8,128)} %slots_ref.1) | copy-start | bytes 24580
  20.9 0.7 %copy-start.3 = (s32[2,8]{1,0:T(2,128)S(1)}, s32[2,8]{1,0:T(2,128)}, u32[]{:S(2)}) copy-start(s32[2,8]{1,0:T(2,128)} %exits_ref.3) | copy-start | bytes 196
  38.7 3.2 %collective-permute-start.5 = (f32[24,128]{1,0:T(8,128)S(1)}, f32[24,128]{1,0:T(8,128)S(1)}, u32[]{:S(2)}, u32[]{:S(2)}) collective-permute-start(f32[24,128]{1,0:T(8,128)S(1)} %get-tuple-element.16.sums_ref), channel_id=1, source_target_pairs={{0,3},{1,2},{2,1},{3,0},{4,7},{5,6},{6,5},{7,4},{8,11},{9,10},{10,... | collective-permute-start | bytes 36872 | tf_op jit(solution)/shard_map/ppermute | solution.py:267
  39.4 2.6 %collective-permute-start.4 = (f32[24,128]{1,0:T(8,128)S(1)}, f32[24,128]{1,0:T(8,128)S(1)}, u32[]{:S(2)}, u32[]{:S(2)}) collective-permute-start(f32[24,128]{1,0:T(8,128)S(1)} %get-tuple-element.16.sums_ref), channel_id=1, source_target_pairs={{0,1},{1,0},{2,3},{3,2},{4,5},{5,4},{6,7},{7,6},{8,9},{9,8},{10,11... | collective-permute-start | bytes 36872 | tf_op jit(solution)/shard_map/ppermute | solution.py:267
  42.0 7.1 %collective-permute-start.7 = (f32[136,128]{1,0:T(8,128)S(1)}, f32[136,128]{1,0:T(8,128)S(1)}, u32[]{:S(2)}, u32[]{:S(2)}) collective-permute-start(f32[136,128]{1,0:T(8,128)S(1)} %pad_maximum_fusion.1), channel_id=1, source_target_pairs={{0,28},{1,29},{2,30},{3,31},{4,8},{5,9},{6,10},{7,11},{8,4},{9,5},... | collective-permute-start | bytes 208904 | tf_op jit(solution)/shard_map/ppermute | solution.py:267
  45.5 5.0 %collective-permute-start.6 = (f32[136,128]{1,0:T(8,128)S(1)}, f32[136,128]{1,0:T(8,128)S(1)}, u32[]{:S(2)}, u32[]{:S(2)}) collective-permute-start(f32[136,128]{1,0:T(8,128)S(1)} %pad_maximum_fusion.1), channel_id=1, source_target_pairs={{0,4},{1,5},{2,6},{3,7},{4,0},{5,1},{6,2},{7,3},{8,12},{9,13},{10,... | collective-permute-start | bytes 208904 | tf_op jit(solution)/shard_map/ppermute | solution.py:267
  62.3 0.7 %copy-start.5 = (s32[1,8]{1,0:T(1,128)S(1)}, s32[1,8]{1,0:T(1,128)}, u32[]{:S(2)}) copy-start(s32[1,8]{1,0:T(1,128)} %inlets_ref.1) | copy-start | bytes 100

commit v3 on v2

--- a/solution.py
+++ b/solution.py
@@ -17,6 +17,9 @@
 COMPS = 8
 DEPTH = 2
 ROWS_OUT = 24
+FLAG_LANES = 16
+MIB = 1024 * 1024
+EXITS, OWNERS, INLETS = 0, 16, 32
 
 
 def rounded(value):
@@ -83,7 +86,11 @@
     up = jnp.where(up > 2, up - 3, up)
     side = kind - 4 * kind_row + (5 - c % 4) % 4
     side = jnp.where(side > 3, side - 4, side)
-    wanted = jnp.where(side < 3, 3 * up + side, LANES)
+    if DEPTH <= c < wide - DEPTH:
+        start = (c - DEPTH) * FLAG_LANES
+    else:
+        start = (lax.rem(r, DEPTH) * DEPTH + c % 2) * FLAG_LANES
+    wanted = jnp.where(side < 3, 3 * up + side + start, LANES)
     flags = jnp.sum(jnp.where(lane32 == wanted, tile[6:7, :], 0.0), axis=1, keepdims=True)
     barred = jnp.where(is_kind, -1024.0 * (1.0 - flags), 0.0)
     return jnp.concatenate([first, second, third, fourth], axis=0) + barred
@@ -124,23 +131,44 @@
     return jnp.where(row < 3, places, jnp.where(row < 6, speeds, tile))
 
 
+def position():
+    heights, groups = lax.axis_size("height"), lax.axis_size("cols")
+    h, c = lax.axis_index("height"), lax.axis_index("cols")
+    return c > 0, c < groups - 1, h > 0, h < heights - 1, lax.rem(h, 2) == 0, lax.rem(c, 2) == 0
+
+
+def halo_rows(rows, cols, d, r, c):
+    wide = cols + 2 * DEPTH
+    start = d * rows * wide
+    if c < DEPTH:
+        return start + rows * cols + r * DEPTH + c
+    if c >= cols + DEPTH:
+        return start + rows * (cols + DEPTH) + r * DEPTH + c - cols - DEPTH
+    return start + r * cols + c - DEPTH
+
+
 def particles_kernel(
-    where_ref, exits_ref, owners_ref, own_ref, first_ref, second_ref, slots_ref,
-    sums_ref, settled_ref, leaving_ref, state, turned, pulled, begun,
+    ints_ref, own_ref, first_ref, second_ref, slots_ref,
+    sums_ref, settled_ref, leaving_ref, state, turned, pulled, begun, blocks,
     *, rows, cols,
 ):
     wide = cols + 2 * DEPTH
     high = rows + 2 * DEPTH
-    left, right = where_ref[0], where_ref[1]
-    even, below, above = where_ref[2], where_ref[3], where_ref[4]
-    for r in range(rows):
-        for c in range(wide):
-            one, two = first_ref[r, c], second_ref[r, c]
-            low = jnp.where(even > 0, two, one)
-            top = jnp.where(even > 0, one, two)
-            state[r, c] = jnp.where(below > 0, low, 0.0)
-            state[rows + DEPTH + r, c] = jnp.where(above > 0, top, 0.0)
-            state[DEPTH + r, c] = own_ref[r, c]
+    left, right, below, above, even, _ = position()
+    one, two = first_ref[...], second_ref[...]
+    blocks[0] = jnp.where(below, jnp.where(even, two, one), 0.0)
+    blocks[1] = own_ref[...]
+    blocks[2] = jnp.where(above, jnp.where(even, one, two), 0.0)
+    flag_row = 6 * rows * wide
+    for block in range(3):
+        for r in range(rows):
+            for c in range(wide):
+                for d in range(6):
+                    row = halo_rows(rows, cols, d, r, c)
+                    state[block * rows + r, c, d : d + 1] = blocks[block, row : row + 1]
+                row = flag_row + (rows if c < DEPTH else rows + 1 if c >= cols + DEPTH else r)
+                state[block * rows + r, c, 6:7] = blocks[block, row : row + 1]
+                state[block * rows + r, c, 7:8] = jnp.zeros((1, LANES), f32)
 
     def fill(source, first, last):
         def one_row(r, carry):
@@ -164,11 +192,11 @@
             tiles = [state[r, c], state[r, c + 1]]
             forces = forces_on(tiles, r, c, high, wide, turned, pulled)
             for k in range(2):
-                inside = ((r >= DEPTH) | (below > 0)) & ((r < rows + DEPTH) | (above > 0))
+                inside = ((r >= DEPTH) | below) & ((r < rows + DEPTH) | above)
                 if c + k < DEPTH:
-                    inside = inside & (left > 0)
+                    inside = inside & left
                 if c + k >= cols + DEPTH:
-                    inside = inside & (right > 0)
+                    inside = inside & right
                 begun[r, c + k] = jnp.where(inside, stepped(tiles[k], forces[k]), 0.0)
         return carry
 
@@ -204,23 +232,24 @@
     lane = lax.broadcasted_iota(i32, (1, LANES), 1)
     owner_row = jnp.zeros((1, LANES), i32)
     for t in range(rows * cols):
-        owner_row = jnp.where(lax.rem(lane, rows * cols) == t, owners_ref[t // cols, t % cols], owner_row)
+        owner_row = jnp.where(lax.rem(lane, rows * cols) == t, ints_ref[0, OWNERS + t], owner_row)
     row = lax.broadcasted_iota(i32, (ROWS_OUT - rows * cols, LANES), 0)
     sums_ref[rows * cols :, :] = jnp.where(row == 0, owner_row.astype(f32), 0.0)
 
     leaving_ref[...] = jnp.zeros_like(leaving_ref)
     count = jnp.int32(0)
     for t in range(rows * cols):
-        flag = exits_ref[t // cols, t % cols]
+        flag = ints_ref[0, EXITS + t]
 
         @pl.when((flag > 0) & (count < cols))
         def _(t=t, count=count):
-            leaving_ref[count] = settled_ref[t // cols, t % cols]
+            for d in range(6):
+                leaving_ref[d, pl.ds(count, 1)] = settled_ref[t // cols, t % cols, d : d + 1]
 
         count = count + flag
 
 
-def particles(where, exits, owners, own, first, second, slots):
+def particles(ints, own, first, second, slots):
     rows, cols = slots.shape[:2]
     wide, high = cols + 2 * DEPTH, rows + 2 * DEPTH
     smem = pl.BlockSpec(memory_space=pltpu.SMEM)
@@ -230,19 +259,20 @@
         out_shape=(
             jax.ShapeDtypeStruct((ROWS_OUT, LANES), f32),
             jax.ShapeDtypeStruct((rows, cols, COMPS, LANES), f32),
-            jax.ShapeDtypeStruct((cols, COMPS, LANES), f32),
+            jax.ShapeDtypeStruct((6, cols, LANES), f32),
         ),
-        in_specs=[smem, smem, smem, vmem, vmem, vmem, vmem],
+        in_specs=[smem, vmem, vmem, vmem, vmem],
         out_specs=(vmem, vmem, vmem),
         scratch_shapes=[
             pltpu.VMEM((high, wide, COMPS, LANES), f32),
             pltpu.VMEM((high, wide // 4, LANES, LANES), bf16),
             pltpu.VMEM((high, wide, 16, LANES), bf16),
             pltpu.VMEM((high, wide, COMPS, LANES), f32),
+            pltpu.VMEM((3, *own.shape), f32),
         ],
-        compiler_params=pltpu.CompilerParams(vmem_limit_bytes=40 * 1024 * 1024),
+        compiler_params=pltpu.CompilerParams(vmem_limit_bytes=12 * MIB),
         name="particles",
-    )(where, exits, owners, own, first, second, slots)
+    )(ints, own, first, second, slots)
 
 
 def matching(heights, groups, axis, odd, wrap):
@@ -261,6 +291,15 @@
     return pairs
 
 
+def around_pairs(heights, groups):
+    pairs = []
+    for h in range(heights):
+        for c in range(groups):
+            target = (heights - 1 - h, c) if h in (0, heights - 1) else (h, c ^ 1)
+            pairs.append((h * groups + c, target[0] * groups + target[1]))
+    return pairs
+
+
 def exchanged(value, axis, wrap):
     heights, groups = lax.axis_size("height"), lax.axis_size("cols")
     return [
@@ -268,49 +307,235 @@
     ]
 
 
+LINES = 32
+
+
+def begin_kernel(zeros_ref):
+    zeros_ref[...] = jnp.zeros_like(zeros_ref)
+
+
+def begun_zeros():
+    return pl.pallas_call(
+        begin_kernel,
+        out_shape=jax.ShapeDtypeStruct((8, LANES), f32),
+        out_specs=pl.BlockSpec(memory_space=pltpu.VMEM),
+        cost_estimate=pl.CostEstimate(flops=10**10, bytes_accessed=4096, transcendentals=0),
+        compiler_params=pltpu.CompilerParams(vmem_limit_bytes=MIB),
+        name="begin",
+    )()
+
+
+def pack_kernel(
+    zeros_ref, exits_hbm, owners_hbm, inlets_hbm, positions_hbm, velocities_hbm, contacts_hbm, slots_hbm, gas_hbm, diagonal_hbm,
+    first_ref, second_ref, flags_ref, ints_ref, slots_ref, state_ref, cells_ref,
+    sides, wide_flags, contacts_ref, exits_ref, owners_ref, inlets_ref, arrived,
+):
+    rows, cols = state_ref.shape[1:3]
+    _, levels, across, along = cells_ref.shape
+    across = across - 8
+    pairs = (
+        (positions_hbm, state_ref.at[0:3]),
+        (velocities_hbm, state_ref.at[3:6]),
+        (gas_hbm, cells_ref.at[0, :, 0:across]),
+        (diagonal_hbm, cells_ref.at[1, :, 0:across]),
+        (contacts_hbm, contacts_ref),
+        (exits_hbm, exits_ref),
+        (owners_hbm, owners_ref),
+        (inlets_hbm, inlets_ref),
+        (slots_hbm, slots_ref),
+    )
+    copies = [pltpu.make_async_copy(source, target, arrived.at[n]) for n, (source, target) in enumerate(pairs)]
+    for copy in copies:
+        copy.start()
+    sides[...] = jnp.zeros_like(sides) + zeros_ref[0:1]
+    wide_flags[...] = jnp.zeros_like(wide_flags)
+    cells_ref[:, :, across:] = jnp.zeros((2, levels, 8, along), f32)
+    for copy in copies:
+        copy.wait()
+    lane = lax.broadcasted_iota(i32, (1, LANES), 1)
+    ints = jnp.zeros((1, LANES), i32)
+    for r in range(rows):
+        for c in range(cols):
+            ints = jnp.where(lane == EXITS + r * cols + c, exits_ref[r, c], ints)
+            ints = jnp.where(lane == OWNERS + r * cols + c, owners_ref[r, c], ints)
+    for c in range(cols):
+        ints = jnp.where(lane == INLETS + c, inlets_ref[0, c], ints)
+    ints_ref[...] = ints
+    wide_flags[:, :, 0 : contacts_ref.shape[2]] = contacts_ref[...].astype(f32)
+    flags = []
+    for r in range(rows):
+        spread = pltpu.roll(wide_flags[r], 0, 1, stride=FLAG_LANES, stride_axis=0)
+        flags.append(jnp.sum(spread, axis=0, keepdims=True))
+        flags_ref[r : r + 1] = flags[r]
+    for side in range(2):
+        shown = jnp.zeros((1, LANES), f32)
+        for r in range(rows):
+            for k in range(DEPTH):
+                c = k if side == 0 else cols - DEPTH + k
+                for d in range(6):
+                    row = d * rows * DEPTH + r * DEPTH + k
+                    sides[side, row : row + 1] = state_ref[d, r, c : c + 1]
+            turn = (r * DEPTH - (0 if side == 0 else cols - DEPTH)) * FLAG_LANES
+            part = pltpu.roll(flags[r], turn % LANES, 1)
+            shown = jnp.where(lane // (DEPTH * FLAG_LANES) == r, part, shown)
+        sides[side, 6 * rows * DEPTH : 6 * rows * DEPTH + 1] = shown
+        for z in range(levels):
+            for k in range(2):
+                x = k if side == 0 else across - 2 + k
+                for kind in range(2):
+                    for q in range(along // LANES):
+                        row = LINES + ((z * 2 + k) * 2 + kind) * (along // LANES) + q
+                        sides[side, row : row + 1] = cells_ref[kind, z, x : x + 1, q * LANES : (q + 1) * LANES]
+    even = position()[5]
+    first_ref[...] = jnp.where(even, sides[1], sides[0])
+    second_ref[...] = jnp.where(even, sides[0], sides[1])
+
+
+def packed(exits, owners, inlets, positions, velocities, contacts, slots, gas, diagonal):
+    levels, across, along = gas.shape
+    rows, cols = positions.shape[1:3]
+    side = jax.ShapeDtypeStruct((LINES + levels * 4 * (along // LANES), LANES), f32)
+    vmem = pl.BlockSpec(memory_space=pltpu.VMEM)
+    return pl.pallas_call(
+        pack_kernel,
+        out_shape=(
+            side,
+            side,
+            jax.ShapeDtypeStruct((rows, LANES), f32),
+            jax.ShapeDtypeStruct((1, LANES), i32),
+            jax.ShapeDtypeStruct(slots.shape, i32),
+            jax.ShapeDtypeStruct((6, rows, cols, LANES), f32),
+            jax.ShapeDtypeStruct((2, levels, across + 8, along), f32),
+        ),
+        in_specs=[vmem] + [pl.BlockSpec(memory_space=pl.ANY)] * 9,
+        out_specs=(vmem,) * 7,
+        scratch_shapes=[
+            pltpu.VMEM((2, *side.shape), f32),
+            pltpu.VMEM((rows, cols, LANES), f32),
+            pltpu.VMEM(contacts.shape, i32),
+            pltpu.SMEM(exits.shape, i32),
+            pltpu.SMEM(owners.shape, i32),
+            pltpu.SMEM(inlets.shape, i32),
+            pltpu.SemaphoreType.DMA((9,)),
+        ],
+        compiler_params=pltpu.CompilerParams(vmem_limit_bytes=8 * MIB),
+        name="pack",
+    )(begun_zeros(), exits, owners, inlets, positions, velocities, contacts, slots, gas, diagonal)
+
+
+def merge_kernel(state_ref, flags_ref, line_a, line_b, window_ref):
+    rows, cols = state_ref.shape[1:3]
+    each = rows * (cols + 2 * DEPTH)
+    count = 6 * rows * DEPTH
+    left, right, _, _, _, even = position()
+    one, two = line_a[0 : count + 8], line_b[0 : count + 8]
+    low = jnp.where(left, jnp.where(even, two, one), 0.0)
+    top = jnp.where(right, jnp.where(even, one, two), 0.0)
+    for d in range(6):
+        for r in range(rows):
+            window_ref[d * each + r * cols : d * each + (r + 1) * cols] = state_ref[d, r]
+        at = d * each + rows * cols
+        piece = slice(d * rows * DEPTH, (d + 1) * rows * DEPTH)
+        window_ref[at : at + rows * DEPTH] = low[piece]
+        window_ref[at + rows * DEPTH : at + 2 * rows * DEPTH] = top[piece]
+    window_ref[6 * each : 6 * each + 8] = jnp.concatenate(
+        [flags_ref[...], low[count : count + 1], top[count : count + 1], jnp.zeros((6 - rows, LANES), f32)], axis=0
+    )
+
+
+def merged(state, flags, lines):
+    rows, cols = state.shape[1:3]
+    vmem = pl.BlockSpec(memory_space=pltpu.VMEM)
+    return pl.pallas_call(
+        merge_kernel,
+        out_shape=jax.ShapeDtypeStruct((6 * rows * (cols + 2 * DEPTH) + 8, LANES), f32),
+        in_specs=[vmem] * 4,
+        out_specs=vmem,
+        compiler_params=pltpu.CompilerParams(vmem_limit_bytes=4 * MIB),
+        name="merge",
+    )(state, flags, *lines)
+
+
+def line_at(lines, z, k, kind, q, quarters):
+    row = LINES + ((z * 2 + k) * 2 + kind) * quarters + q
+    return lines[row : row + 1]
+
+
+def cells_kernel(cells_in, line_a, line_b, cells_ref):
+    kinds, levels, rows, along = cells_ref.shape
+    quarters = along // LANES
+    even = position()[5]
+    cells_ref[...] = cells_in[...]
+    for kind in range(kinds):
+        for z in range(levels):
+            for q in range(quarters):
+                low = [line_at(lines, z, 1, kind, q, quarters) for lines in (line_a, line_b)]
+                top = [line_at(lines, z, 0, kind, q, quarters) for lines in (line_a, line_b)]
+                cells_ref[kind, z, rows - 8 : rows, q * LANES : (q + 1) * LANES] = jnp.concatenate(
+                    [
+                        jnp.where(even, low[1], low[0]),
+                        jnp.where(even, top[0], top[1]),
+                        jnp.zeros((6, LANES), f32),
+                    ],
+                    axis=0,
+                )
+
+
+def cells_of(cells, lines):
+    vmem = pl.BlockSpec(memory_space=pltpu.VMEM)
+    return pl.pallas_call(
+        cells_kernel,
+        out_shape=jax.ShapeDtypeStruct(cells.shape, f32),
+        in_specs=[pl.BlockSpec(memory_space=pltpu.VMEM)] * 3,
+        out_specs=vmem,
+        compiler_params=pltpu.CompilerParams(vmem_limit_bytes=4 * MIB),
+        name="cells",
+    )(cells, *lines)
+
+
 def right_side_kernel(
-    where_ref, sums_ref, side_a, side_b, height_a, height_b, gas_ref, diagonal_ref, line_a, line_b,
-    corner_a, corner_b, gas_a, gas_b, rhs_ref, near_ref, far_ref, dots_ref, scaling, rhs, first, second,
-    *, cols,
+    sums_ref, side_a, side_b, height_a, height_b, cells_ref, line_a, line_b, gas_a, gas_b, rhs_ref, near_ref, far_ref, dots_ref, scaling, rhs, first, second,
 ):
-    levels, across, along = gas_ref.shape
+    _, levels, across, along = cells_ref.shape
+    across = across - 8
     edge = 8
     wide = across + 2 * edge
     quarters = along // LANES
-    left, right, even_c = where_ref[0], where_ref[1], where_ref[5]
-    even, below, above = where_ref[2], where_ref[3], where_ref[4]
+    left, right, below, above, even, even_c = position()
 
     def low_of(is_even, one, two):
-        return jnp.where(is_even > 0, two, one)
+        return jnp.where(is_even, two, one)
 
     def high_of(is_even, one, two):
-        return jnp.where(is_even > 0, one, two)
+        return jnp.where(is_even, one, two)
 
     for ref in (scaling, rhs):
         ref[:, 0:edge, :] = jnp.zeros((3 * levels, edge, along), f32)
         ref[:, edge + across :, :] = jnp.zeros((3 * levels, edge, along), f32)
-    scaling[levels : 2 * levels, edge : edge + across] = 1.0 / (6.0 + diagonal_ref[...])
-    rhs[levels : 2 * levels, edge : edge + across] = gas_ref[...]
+    scaling[levels : 2 * levels, edge : edge + across] = 1.0 / (6.0 + cells_ref[1, :, 0:across])
+    rhs[levels : 2 * levels, edge : edge + across] = cells_ref[0, :, 0:across]
     for level, choose, present in ((0, low_of, below), (2 * levels, high_of, above)):
         for z in range(levels):
-            rhs[level + z, edge : edge + across] = choose(even, gas_a[0, z], gas_b[0, z])
-            m = 1.0 / (6.0 + choose(even, gas_a[1, z], gas_b[1, z]))
-            scaling[level + z, edge : edge + across] = jnp.where(present > 0, m, 0.0)
-
-    def put_line(z, x, lines, present):
-        m = jnp.where(present, 1.0 / (6.0 + lines), 0.0)
-        for k in range(quarters):
-            rhs[z, x : x + 1, k * LANES : (k + 1) * LANES] = lines[k : k + 1]
-            scaling[z, x : x + 1, k * LANES : (k + 1) * LANES] = m[quarters + k : quarters + k + 1]
-
-    for z in range(levels):
-        for x in range(2):
-            put_line(levels + z, edge - 2 + x, low_of(even_c, line_a[z, x, 8:16], line_b[z, x, 8:16]), left > 0)
-            put_line(levels + z, edge + across + x, high_of(even_c, line_a[z, x, 8:16], line_b[z, x, 8:16]), right > 0)
-        for level, choose, present in ((0, low_of, below), (2 * levels, high_of, above)):
-            lines = [choose(even, corner_a[z, cols + 4 + x], corner_b[z, cols + 4 + x]) for x in range(2)]
-            put_line(level + z, edge - 1, lines[0], (present > 0) & (left > 0))
-            put_line(level + z, edge + across, lines[1], (present > 0) & (right > 0))
+            rhs[level + z, edge : edge + across] = choose(even, gas_a[0, z, 0:across], gas_b[0, z, 0:across])
+            m = 1.0 / (6.0 + choose(even, gas_a[1, z, 0:across], gas_b[1, z, 0:across]))
+            scaling[level + z, edge : edge + across] = jnp.where(present, m, 0.0)
+            for row, x, beside_it in ((across, edge - 1, left), (across + 1, edge + across, right)):
+                line = slice(row, row + 1)
+                rhs[level + z, x : x + 1] = choose(even, gas_a[0, z, line], gas_b[0, z, line])
+                m = 1.0 / (6.0 + choose(even, gas_a[1, z, line], gas_b[1, z, line]))
+                scaling[level + z, x : x + 1] = jnp.where(present & beside_it, m, 0.0)
+    for choose, start, present in ((low_of, edge - 2, left), (high_of, edge + across, right)):
+        for z in range(levels):
+            for k in range(2):
+                for q in range(quarters):
+                    part = slice(q * LANES, (q + 1) * LANES)
+                    x = slice(start + k, start + k + 1)
+                    kinds = [
+                        choose(even_c, *[line_at(lines, z, k, kind, q, quarters) for lines in (line_a, line_b)])
+                        for kind in range(2)
+                    ]
+                    rhs[levels + z, x, part] = kinds[0]
+                    scaling[levels + z, x, part] = jnp.where(present, 1.0 / (6.0 + kinds[1]), 0.0)
 
     lane = lax.broadcasted_iota(i32, (1, LANES), 1)
     tiles = 16
@@ -331,11 +556,11 @@
             here = ((lane >> 4) == n) | ((lane >> 4) == n + 3)
             here = here & (x >= edge - 2) & (x < edge + across + 2)
             if n == 0:
-                here = here & (left > 0)
+                here = here & left
             if n == 2:
-                here = here & (right > 0)
+                here = here & right
             if present is not None:
-                here = here & (present > 0)
+                here = here & present
             code = jnp.where(here, (z * wide + x) * quarters + (owner & (quarters - 1)), code)
         values = jnp.concatenate([part[0:tiles] for part in parts], axis=0)
         high = values.astype(bf16)
@@ -389,28 +614,28 @@
     dots_ref[...] = jnp.broadcast_to(line, dots_ref.shape)
 
 
-def right_side_of(where, sums, side, height, gas, diagonal, lines, corners, gases, devices, cols):
-    levels, across, along = gas.shape
-    smem = pl.BlockSpec(memory_space=pltpu.SMEM)
+def right_side_of(sums, side, height, cells, lines, gases, devices):
+    _, levels, across, along = cells.shape
+    across = across - 8
     vmem = pl.BlockSpec(memory_space=pltpu.VMEM)
     whole = pltpu.VMEM((3 * levels, across + 16, along), f32)
     return pl.pallas_call(
-        functools.partial(right_side_kernel, cols=cols),
-        out_shape=(jax.ShapeDtypeStruct(gas.shape, f32),) * 3 + (jax.ShapeDtypeStruct((devices, LANES), f32),),
-        in_specs=[smem] + [vmem] * 13,
+        right_side_kernel,
+        out_shape=(jax.ShapeDtypeStruct((levels, across, along), f32),) * 3 + (jax.ShapeDtypeStruct((devices, LANES), f32),),
+        in_specs=[vmem] * 10,
         out_specs=(vmem,) * 4,
         scratch_shapes=[whole] * 4,
-        compiler_params=pltpu.CompilerParams(vmem_limit_bytes=40 * 1024 * 1024),
+        compiler_params=pltpu.CompilerParams(vmem_limit_bytes=16 * MIB),
         name="right_side",
-    )(where, sums, *side, *height, gas, diagonal, *lines, *corners, *gases)
+    )(sums, *side, *height, cells, *lines, *gases)
 
 
 def results_kernel(
-    where_ref, exits_ref, inlets_ref, dots_ref, rhs_ref, near_ref, far_ref, diagonal_ref, settled_ref,
-    height_a, height_b, positions_ref, velocities_ref, pressure_ref, residual_ref,
+    ints_ref, dots_ref, rhs_ref, near_ref, far_ref, cells_ref, settled_ref,
+    height_a, height_b, around_ref, positions_ref, velocities_ref, pressure_ref, residual_ref,
 ):
     rows, cols = settled_ref.shape[:2]
-    even = where_ref[2]
+    _, _, below, _, even, _ = position()
     totals = jnp.sum(dots_ref[...], axis=0, keepdims=True)
     g00, g01, g11, g12 = [totals[:, k : k + 1] for k in range(4)]
     ratio = g01 / g00
@@ -424,41 +649,39 @@
     one = alpha + later * (1.0 - alpha + beta)
     two = later * alpha
     for z in range(rhs_ref.shape[0]):
-        m = 1.0 / (6.0 + diagonal_ref[z])
+        m = 1.0 / (6.0 + cells_ref[1, z, 0 : rhs_ref.shape[1]])
         rhs, near = rhs_ref[z], near_ref[z]
         pressure_ref[z] = m * (one * rhs + two * near)
         residual_ref[z] = (1.0 - one) * rhs + (one - two) * near + two * far_ref[z]
-    for r in range(rows):
+    for r in range(1, rows):
         for c in range(cols):
-            kept = jnp.where(exits_ref[r, c] > 0, 0.0, settled_ref[r, c])
-            if r > 0:
-                for d in range(3):
-                    positions_ref[d, r, c : c + 1] = kept[d : d + 1]
-                    velocities_ref[d, r, c : c + 1] = kept[d + 3 : d + 4]
+            kept = jnp.where(ints_ref[0, EXITS + r * cols + c] > 0, 0.0, settled_ref[r, c])
+            for d in range(3):
+                positions_ref[d, r, c : c + 1] = kept[d : d + 1]
+                velocities_ref[d, r, c : c + 1] = kept[d + 3 : d + 4]
     start = 3 * ROWS_OUT
-    for k in range(cols):
-        slot = slice(start + k * COMPS, start + (k + 1) * COMPS)
-        tile = jnp.where(even > 0, height_b[slot], height_a[slot])
-        c = inlets_ref[0, k]
-        for d in range(3):
-            positions_ref[d, 0, pl.ds(c, 1)] = tile[d : d + 1]
-            velocities_ref[d, 0, pl.ds(c, 1)] = tile[d + 3 : d + 4]
-
-
-def results_of(where, exits, inlets, dots, rhs, near, far, diagonal, settled, height):
+    for d in range(6):
+        block = slice(start + d * cols, start + (d + 1) * cols)
+        tiles = jnp.where(even, height_b[block], height_a[block])
+        target = positions_ref if d < 3 else velocities_ref
+        for k in range(cols):
+            target[d % 3, 0, pl.ds(ints_ref[0, INLETS + k], 1)] = tiles[k : k + 1]
+
+
+def results_of(ints, dots, rhs, near, far, cells, settled, height, around):
     rows, cols = settled.shape[:2]
     smem = pl.BlockSpec(memory_space=pltpu.SMEM)
     vmem = pl.BlockSpec(memory_space=pltpu.VMEM)
     particle = jax.ShapeDtypeStruct((3, rows, cols, LANES), f32)
-    cells = jax.ShapeDtypeStruct(rhs.shape, f32)
+    field = jax.ShapeDtypeStruct(rhs.shape, f32)
     return pl.pallas_call(
         results_kernel,
-        out_shape=(particle, particle, cells, cells),
-        in_specs=[smem] * 3 + [vmem] * 8,
+        out_shape=(particle, particle, field, field),
+        in_specs=[smem] + [vmem] * 9,
         out_specs=(vmem,) * 4,
-        compiler_params=pltpu.CompilerParams(vmem_limit_bytes=40 * 1024 * 1024),
+        compiler_params=pltpu.CompilerParams(vmem_limit_bytes=8 * MIB),
         name="results",
-    )(where, exits, inlets, dots, rhs, near, far, diagonal, settled, *height)
+    )(ints, dots, rhs, near, far, cells, settled, *height, around)
 
 
 def on_device(
@@ -466,59 +689,26 @@
 ):
     heights, groups = lax.axis_size("height"), lax.axis_size("cols")
     h, c = lax.axis_index("height"), lax.axis_index("cols")
-    rows, cols = positions.shape[1:3]
-    levels, across, along = gas_source.shape
-    where = jnp.stack([c > 0, c < groups - 1, h % 2 == 0, h > 0, h < heights - 1, c % 2 == 0, c < 0, c < 0])
-    where = where.astype(jnp.int32)
-    flags = jnp.pad(contacts.astype(f32).transpose(1, 2, 0), ((0, 0), (0, 0), (0, LANES - contacts.shape[0])))
-    tiles = jnp.concatenate(
-        [
-            positions.transpose(1, 2, 0, 3),
-            velocities.transpose(1, 2, 0, 3),
-            flags[:, :, None, :],
-            jnp.zeros((rows, cols, 1, LANES), f32),
-        ],
-        axis=2,
+    *sides, flags, ints, slots, state, cells = packed(
+        exit_flags, cell_blocks, inlet_slots, positions, velocities, contacts.transpose(1, 2, 0), cell_slots,
+        gas_source, diagonal,
     )
-
-    def edge_lines(lines):
-        return lines.reshape(levels, 2, along // LANES, LANES)
-
-    def side(first, last):
-        cells = slice(0, 2) if first else slice(across - 2, across)
-        return jnp.concatenate(
-            [
-                tiles[:, :DEPTH] if first else tiles[:, cols - DEPTH :],
-                edge_lines(gas_source[:, cells]),
-                edge_lines(diagonal[:, cells]),
-            ],
-            axis=2,
-        )
-
-    at_left, at_right = side(True, False), side(False, True)
-    even = c % 2 == 0
-    shared = [jnp.where(even, at_right, at_left), jnp.where(even, at_left, at_right)]
     lines = [
         lax.ppermute(value, ("height", "cols"), matching(heights, groups, "cols", odd, True))
-        for value, odd in zip(shared, (False, True))
+        for value, odd in zip(sides, (False, True))
     ]
-    low = jnp.where(c > 0, jnp.where(even, lines[1], lines[0]), 0.0)
-    high = jnp.where(c < groups - 1, jnp.where(even, lines[0], lines[1]), 0.0)
-    window = jnp.concatenate(
-        [low[:, :, :COMPS], tiles, high[:, :, :COMPS], low[:, 1:2, COMPS:], high[:, 0:1, COMPS:]], axis=1
-    )
+    window = merged(state, flags, lines)
     beside = exchanged(window, "height", False)
-    cells, beside = lax.optimization_barrier((jnp.stack([gas_source, diagonal]), beside))
-    gases = exchanged(cells, "height", False)
-    sums, settled, leaving = particles(where, exit_flags, cell_blocks, window, *beside, cell_slots)
-    sides = exchanged(sums, "cols", True)
-    parcel = jnp.concatenate([sums, *sides, leaving.reshape(cols * COMPS, LANES)], axis=0)
+    cells = cells_of(cells, lines)
+    sent, beside = lax.optimization_barrier((cells, beside))
+    gases = exchanged(sent, "height", False)
+    sums, settled, leaving = particles(ints, window, *beside, slots)
+    near = exchanged(sums, "cols", True)
+    parcel = jnp.concatenate([sums, *near, leaving.reshape(-1, LANES)], axis=0)
     parcels = exchanged(parcel, "height", True)
-    rhs, near, far, dots = right_side_of(
-        where, sums, sides, parcels, gas_source, diagonal, lines, beside, gases, heights * groups, cols
-    )
+    rhs, first, second, dots = right_side_of(sums, near, parcels, cells, lines, gases, heights * groups)
     dots = lax.all_to_all(dots, ("height", "cols"), 0, 0, tiled=True)
-    return results_of(where, exit_flags, inlet_slots, dots, rhs, near, far, diagonal, settled, parcels)
+    return results_of(ints, dots, rhs, first, second, cells, settled, parcels, leaving)
 
 
 def solution(mesh):

time: 65 us -> 61.2 us (0.942)
  local copies, waits for them, and re-layouts: 4.51 us -> 0.96 us
  waiting for transfers between devices: 13 us -> 11 us
  blocking collectives: 10.3 us -> 11.6 us
    ppermute x8, waiting for transfers between devices: 11.3 us -> 9.37 us  [exchanged(): lax.ppermute(value, ('height', 'cols'), matching(heights, groups, axis, o...]
    unnamed x22 -> x18, local copies, waits for them, and re-layouts: 2.66 us -> 0.96 us
    slice x3 -> x0, local copies, waits for them, and re-layouts: 1.57 us -> none  [the longest x1 0.78 us: side(): diagonal[:, cells]]
    all_to_all x1, blocking collectives: 10.3 us -> 11.6 us  [on_device(): dots = lax.all_to_all(dots, ('height', 'cols'), 0, 0, tiled=True)]
    pallas_call x2 -> x6, Pallas kernels: 3.24 us -> 3.74 us  [the longest x1 1.66 us: results_of(): pl.pallas_call(results_kernel, out_shape=(particle, particle, field, fiel...]
  transfers between devices with their start and end apart: 10 -> 10, of which waited for: 5 -> 5; matrix products, arithmetic and copies ran while one was open for 0% -> 0% of each run, Pallas kernels for 26% -> 28%
where the time goes in v3:
time: 61.2 us; the launch traced here: 61 us
  Pallas kernels  21 us (34%)
  starting transfers between devices  15.6 us (25%)
  blocking collectives  11.6 us (19%)
  waiting for transfers between devices  11 us (18%)
  local copies, waits for them, and re-layouts  0.96 us (2%)
  between operations  0.79 us (1%)
    pallas_call x1, Pallas kernels, particles(): pl.pallas_call(functools.partial(particles_kernel, rows=rows, cols=cols),...  17.3 us
    ppermute x8, starting transfers between devices, exchanged(): lax.ppermute(value, ('height', 'cols'), matching(heights, groups, axis, o...  12.4 us
    all_to_all x1, blocking collectives, on_device(): dots = lax.all_to_all(dots, ('height', 'cols'), 0, 0, tiled=True)  11.6 us
    ppermute x8, waiting for transfers between devices, exchanged(): lax.ppermute(value, ('height', 'cols'), matching(heights, groups, axis, o...  9.37 us
    ppermute x2, starting transfers between devices, on_device(): lax.ppermute(value, ('height', 'cols'), matching(heights, groups, 'cols',...  3.16 us
    ppermute x2, waiting for transfers between devices, on_device(): lax.ppermute(value, ('height', 'cols'), matching(heights, groups, 'cols',...  1.67 us
    pallas_call x1, Pallas kernels, results_of(): pl.pallas_call(results_kernel, out_shape=(particle, particle, field, fiel...  1.66 us
  transfers between devices with their start and end apart: 10, of which 5 were waited for; matrix products, arithmetic and copies ran while one was open for 0% of the time, Pallas kernels for 28%

profile of v3, /device:TPU:0, one launch (start us, length us, event | category | flops | bytes accessed | tf_op | source)
XLA Modules:
  0.0 61.0 jit_solution(13228471927509684125)
XLA Ops:
  0.6 0.0 copy-start.1
  0.6 0.0 copy-start
  0.7 0.0 copy-start.5
  0.7 0.0 copy-start.4
  0.7 0.0 copy-start.3
  0.7 0.0 copy-start.2
  0.7 0.0 copy-start.7
  0.7 0.0 copy-start.6
  0.7 0.0 copy-start.8
  0.7 0.8 %copy-done.1 = f32[2,64,512]{2,1,0:T(8,128)S(1)} copy-done((f32[2,64,512]{2,1,0:T(8,128)S(1)}, f32[2,64,512]{2,1,0:T(8,128)}, u32[]{:S(2)}) %copy-start.1) | copy-done | bytes 262168
  1.6 0.1 copy-done
  1.7 0.0 copy-done.5
  1.7 0.0 copy-done.4
  1.7 0.0 copy-done.3
  1.7 0.0 copy-done.2
  1.7 0.0 copy-done.7
  1.7 0.0 copy-done.6
  1.7 0.0 copy-done.8
  1.7 0.9 %pack.1 = (f32[64,128]{1,0:T(8,128)S(1)}, f32[64,128]{1,0:T(8,128)S(1)}, f32[2,128]{1,0:T(2,128)S(1)}, s32[1,128]{1,0:T(1,128)S(1)}, s32[2,8,128]{2,1,0:T(8,128)...) custom-call(f32[8,128]{1,0:T(8,128)S(1)} %begin.1.zeros_ref, s32[2,8]{1,0:T(2,128)S(1)} %copy-done.6, ...), custom_call_target="tpu_custom_call" | custom-call | tf_op jit(solution)/shard_map/pack/pallas_call | solution.py:399
  2.6 0.5 collective-permute-start
  3.2 2.6 %collective-permute-start.1 = (f32[64,128]{1,0:T(8,128)S(1)}, f32[64,128]{1,0:T(8,128)S(1)}, u32[]{:S(2)}, u32[]{:S(2)}) collective-permute-start(f32[64,128]{1,0:T(8,128)S(1)} %get-tuple-element.25), channel_id=1, source_target_pairs={{0,3},{1,2},{2,1},{3,0},{4,7},{5,6},{6,5},{7,4},{8,11},{9,10},{10,... | collective-permute-start | bytes 98312 | tf_op jit(solution)/shard_map/ppermute | solution.py:697
  5.8 0.0 collective-permute-done.line_a
  5.8 1.7 %collective-permute-done.1.line_b = f32[64,128]{1,0:T(8,128)S(1)} collective-permute-done((f32[64,128]{1,0:T(8,128)S(1)}, f32[64,128]{1,0:T(8,128)S(1)}, u32[]{:S(2)}, u32[]{:S(2)}) %collective-permute-start.1) | collective-permute-done | bytes 32800 | tf_op jit(solution)/shard_map/ppermute | solution.py:697
  7.5 0.2 collective-permute-start.3
  7.7 3.0 %collective-permute-start.2 = (f32[152,128]{1,0:T(8,128)S(1)}, f32[152,128]{1,0:T(8,128)S(1)}, u32[]{:S(2)}, u32[]{:S(2)}) collective-permute-start(f32[152,128]{1,0:T(8,128)S(1)} %merge.1.own_ref), channel_id=1, source_target_pairs={{0,4},{1,5},{2,6},{3,7},{4,0},{5,1},{6,2},{7,3},{8,12},{9,13},{10,... | collective-permute-start | bytes 233480 | tf_op jit(solution)/shard_map/ppermute | solution.py:306
  10.7 0.1 cells.1.cells_ref
  10.8 0.0 collective-permute-done.3.second_ref
  10.8 3.2 %collective-permute-done.2.first_ref = f32[152,128]{1,0:T(8,128)S(1)} collective-permute-done((f32[152,128]{1,0:T(8,128)S(1)}, f32[152,128]{1,0:T(8,128)S(1)}, u32[]{:S(2)}, u32[]{:S(2)}) %collective-permute-start.2) | collective-permute-done | bytes 77856 | tf_op jit(solution)/shard_map/ppermute | solution.py:306
  14.0 0.0 collective-permute-start.9
  14.0 4.0 %collective-permute-start.8 = (f32[2,2,72,512]{3,2,1,0:T(8,128)S(1)}, f32[2,2,72,512]{3,2,1,0:T(8,128)S(1)}, u32[]{:S(2)}, u32[]{:S(2)}) collective-permute-start(f32[2,2,72,512]{3,2,1,0:T(8,128)S(1)} %cells.1.cells_ref), channel_id=1, source_target_pairs={{0,4},{1,5},{2,6},{3,7},{4,0},{5,1},{6,2},{7,3},{8,12},{9,13},{10,... | collective-permute-start | bytes 1769480 | tf_op jit(solution)/shard_map/ppermute | solution.py:306
  18.0 17.3 %particles.1 = (f32[24,128]{1,0:T(8,128)S(1)}, f32[2,8,8,128]{3,2,1,0:T(8,128)S(1)}, f32[6,8,128]{2,1,0:T(8,128)S(1)}) custom-call(s32[1,128]{1,0:T(1,128)S(1)} %get-tuple-element.21.ints_ref, f32[152,128]{1,0:T(8,128)S(1)} %merge.1.own_ref, f32[152,128]{1,0:T(8,128)S(1)} %collective-permute-done.2.first_ref, ...), custom_call_target="tpu_custom_call" | custom-call | tf_op jit(solution)/shard_map/particles/pallas_call | solution.py:257
  35.2 0.7 %collective-permute-start.5 = (f32[24,128]{1,0:T(8,128)S(1)}, f32[24,128]{1,0:T(8,128)S(1)}, u32[]{:S(2)}, u32[]{:S(2)}) collective-permute-start(f32[24,128]{1,0:T(8,128)S(1)} %get-tuple-element.30.sums_ref), channel_id=1, source_target_pairs={{0,3},{1,2},{2,1},{3,0},{4,7},{5,6},{6,5},{7,4},{8,11},{9,10},{10,... | collective-permute-start | bytes 36872 | tf_op jit(solution)/shard_map/ppermute | solution.py:306
  35.9 1.0 %collective-permute-start.4 = (f32[24,128]{1,0:T(8,128)S(1)}, f32[24,128]{1,0:T(8,128)S(1)}, u32[]{:S(2)}, u32[]{:S(2)}) collective-permute-start(f32[24,128]{1,0:T(8,128)S(1)} %get-tuple-element.30.sums_ref), channel_id=1, source_target_pairs={{0,1},{1,0},{2,3},{3,2},{4,5},{5,4},{6,7},{7,6},{8,9},{9,8},{10,11... | collective-permute-start | bytes 36872 | tf_op jit(solution)/shard_map/ppermute | solution.py:306
  37.0 1.5 %collective-permute-done.5.side_b = f32[24,128]{1,0:T(8,128)S(1)} collective-permute-done((f32[24,128]{1,0:T(8,128)S(1)}, f32[24,128]{1,0:T(8,128)S(1)}, u32[]{:S(2)}, u32[]{:S(2)}) %collective-permute-start.5) | collective-permute-done | bytes 12320 | tf_op jit(solution)/shard_map/ppermute | solution.py:306
  38.5 0.0 collective-permute-done.4.side_a
  38.5 3.5 %collective-permute-start.7 = (f32[120,128]{1,0:T(8,128)S(1)}, f32[120,128]{1,0:T(8,128)S(1)}, u32[]{:S(2)}, u32[]{:S(2)}) collective-permute-start(f32[120,128]{1,0:T(8,128)S(1)} %pad_maximum_fusion), channel_id=1, source_target_pairs={{0,28},{1,29},{2,30},{3,31},{4,8},{5,9},{6,10},{7,11},{8,4},{9,5},... | collective-permute-start | bytes 184328 | tf_op jit(solution)/shard_map/ppermute | solution.py:306
  42.0 0.0 collective-permute-start.6
  42.0 3.6 %collective-permute-done.7.height_b = f32[120,128]{1,0:T(8,128)S(1)} collective-permute-done((f32[120,128]{1,0:T(8,128)S(1)}, f32[120,128]{1,0:T(8,128)S(1)}, u32[]{:S(2)}, u32[]{:S(2)}) %collective-permute-start.7) | collective-permute-done | bytes 61472 | tf_op jit(solution)/shard_map/ppermute | solution.py:306
  45.5 1.1 %collective-permute-done.6.height_a = f32[120,128]{1,0:T(8,128)S(1)} collective-permute-done((f32[120,128]{1,0:T(8,128)S(1)}, f32[120,128]{1,0:T(8,128)S(1)}, u32[]{:S(2)}, u32[]{:S(2)}) %collective-permute-start.6) | collective-permute-done | bytes 61472 | tf_op jit(solution)/shard_map/ppermute | solution.py:306
  46.6 0.0 collective-permute-done.9.gas_b
  46.6 0.0 collective-permute-done.8.gas_a
  46.6 1.1 %right_side.1 = (f32[2,64,512]{2,1,0:T(8,128)S(1)}, f32[2,64,512]{2,1,0:T(8,128)S(1)}, f32[2,64,512]{2,1,0:T(8,128)S(1)}, f32[32,128]{1,0:T(8,128)S(1)}) custom-call(f32[24,128]{1,0:T(8,128)S(1)} %get-tuple-element.30.sums_ref, f32[24,128]{1,0:T(8,128)S(1)} %collective-permute-done.4.side_a, f32[24,128]{1,0:T(8,128)S(1)} %collective-permute-done.5.side_b, ...), custom_call_target="tpu_custom_call" | custom-call | tf_op jit(solution)/shard_map/right_side/pallas_call | solution.py:622
  47.7 11.6 %all_to_all.11 = f32[32,1,128]{2,1,0:T(1,128)S(1)} all-to-all(f32[32,1,128]{2,1,0:T(1,128)S(1)} %bitcast.8), channel_id=1, replica_groups=mesh['height'=8,'cols'=4] {'height','cols'}, dimensions={0} | all-to-all | bytes 32768 | tf_op jit(solution)/shard_map/all_to_all | solution.py:710
  59.3 1.7 %results.1 = (f32[3,2,8,128]{3,2,1,0:T(8,128)}, f32[3,2,8,128]{3,2,1,0:T(8,128)}, f32[2,64,512]{2,1,0:T(8,128)}, f32[2,64,512]{2,1,0:T(8,128)}) custom-call(s32[1,128]{1,0:T(1,128)S(1)} %get-tuple-element.21.ints_ref, f32[32,128]{1,0:T(8,128)S(1)} %bitcast.7, f32[2,64,512]{2,1,0:T(8,128)S(1)} %get-tuple-element.34.rhs_ref, ...), custom_call_target="tpu_custom_call" | custom-call | tf_op jit(solution)/shard_map/results/pallas_call | solution.py:677
  (3 shorter events, 0.0 us)
Async XLA Ops:
  0.6 1.0 %copy-start.1 = (f32[2,64,512]{2,1,0:T(8,128)S(1)}, f32[2,64,512]{2,1,0:T(8,128)}, u32[]{:S(2)}) copy-start(f32[2,64,512]{2,1,0:T(8,128)} %diagonal_hbm.1) | copy-start | bytes 786436
  0.6 1.0 %copy-start = (f32[2,64,512]{2,1,0:T(8,128)S(1)}, f32[2,64,512]{2,1,0:T(8,128)}, u32[]{:S(2)}) copy-start(f32[2,64,512]{2,1,0:T(8,128)} %gas_hbm.1) | copy-start | bytes 786436
  0.7 1.0 %copy-start.5 = (s32[2,8,128]{2,1,0:T(8,128)S(1)}, s32[2,8,128]{2,1,0:T(8,128)}, u32[]{:S(2)}) copy-start(s32[2,8,128]{2,1,0:T(8,128)} %slots_hbm.1) | copy-start | bytes 24580
  0.7 1.0 %copy-start.4 = (s32[9,2,8]{0,2,1:T(8,128)S(1)}, s32[9,2,8]{0,2,1:T(8,128)}, u32[]{:S(2)}) copy-start(s32[9,2,8]{0,2,1:T(8,128)} %param.11) | copy-start | bytes 1732
  0.7 1.0 %copy-start.3 = (f32[3,2,8,128]{3,2,1,0:T(8,128)S(1)}, f32[3,2,8,128]{3,2,1,0:T(8,128)}, u32[]{:S(2)}) copy-start(f32[3,2,8,128]{3,2,1,0:T(8,128)} %velocities_hbm.1) | copy-start | bytes 73732
  0.7 1.0 %copy-start.2 = (f32[3,2,8,128]{3,2,1,0:T(8,128)S(1)}, f32[3,2,8,128]{3,2,1,0:T(8,128)}, u32[]{:S(2)}) copy-start(f32[3,2,8,128]{3,2,1,0:T(8,128)} %positions_hbm.1) | copy-start | bytes 73732
  0.7 1.0 %copy-start.7 = (s32[2,8]{1,0:T(2,128)S(1)}, s32[2,8]{1,0:T(2,128)}, u32[]{:S(2)}) copy-start(s32[2,8]{1,0:T(2,128)} %owners_hbm.1) | copy-start | bytes 196
  0.7 1.0 %copy-start.6 = (s32[2,8]{1,0:T(2,128)S(1)}, s32[2,8]{1,0:T(2,128)}, u32[]{:S(2)}) copy-start(s32[2,8]{1,0:T(2,128)} %exits_hbm.1) | copy-start | bytes 196
  0.7 1.0 %copy-start.8 = (s32[1,8]{1,0:T(1,128)S(1)}, s32[1,8]{1,0:T(1,128)}, u32[]{:S(2)}) copy-start(s32[1,8]{1,0:T(1,128)} %inlets_hbm.1) | copy-start | bytes 100
  2.6 3.2 %collective-permute-start = (f32[64,128]{1,0:T(8,128)S(1)}, f32[64,128]{1,0:T(8,128)S(1)}, u32[]{:S(2)}, u32[]{:S(2)}) collective-permute-start(f32[64,128]{1,0:T(8,128)S(1)} %get-tuple-element.24), channel_id=1, source_target_pairs={{0,1},{1,0},{2,3},{3,2},{4,5},{5,4},{6,7},{7,6},{8,9},{9,8},{10,11... | collective-permute-start | bytes 98312 | tf_op jit(solution)/shard_map/ppermute | solution.py:697
  3.2 4.3 %collective-permute-start.1 = (f32[64,128]{1,0:T(8,128)S(1)}, f32[64,128]{1,0:T(8,128)S(1)}, u32[]{:S(2)}, u32[]{:S(2)}) collective-permute-start(f32[64,128]{1,0:T(8,128)S(1)} %get-tuple-element.25), channel_id=1, source_target_pairs={{0,3},{1,2},{2,1},{3,0},{4,7},{5,6},{6,5},{7,4},{8,11},{9,10},{10,... | collective-permute-start | bytes 98312 | tf_op jit(solution)/shard_map/ppermute | solution.py:697
  7.5 3.3 %collective-permute-start.3 = (f32[152,128]{1,0:T(8,128)S(1)}, f32[152,128]{1,0:T(8,128)S(1)}, u32[]{:S(2)}, u32[]{:S(2)}) collective-permute-start(f32[152,128]{1,0:T(8,128)S(1)} %merge.1.own_ref), channel_id=1, source_target_pairs={{0,1},{1,0},{2,3},{3,2},{4,8},{5,9},{6,10},{7,11},{8,4},{9,5},{10,... | collective-permute-start | bytes 233480 | tf_op jit(solution)/shard_map/ppermute | solution.py:306
  7.7 6.3 %collective-permute-start.2 = (f32[152,128]{1,0:T(8,128)S(1)}, f32[152,128]{1,0:T(8,128)S(1)}, u32[]{:S(2)}, u32[]{:S(2)}) collective-permute-start(f32[152,128]{1,0:T(8,128)S(1)} %merge.1.own_ref), channel_id=1, source_target_pairs={{0,4},{1,5},{2,6},{3,7},{4,0},{5,1},{6,2},{7,3},{8,12},{9,13},{10,... | collective-permute-start | bytes 233480 | tf_op jit(solution)/shard_map/ppermute | solution.py:306
  14.0 32.7 %collective-permute-start.9 = (f32[2,2,72,512]{3,2,1,0:T(8,128)S(1)}, f32[2,2,72,512]{3,2,1,0:T(8,128)S(1)}, u32[]{:S(2)}, u32[]{:S(2)}) collective-permute-start(f32[2,2,72,512]{3,2,1,0:T(8,128)S(1)} %cells.1.cells_ref), channel_id=1, source_target_pairs={{0,1},{1,0},{2,3},{3,2},{4,8},{5,9},{6,10},{7,11},{8,4},{9,5},{10,... | collective-permute-start | bytes 1769480 | tf_op jit(solution)/shard_map/ppermute | solution.py:306
  14.0 32.6 %collective-permute-start.8 = (f32[2,2,72,512]{3,2,1,0:T(8,128)S(1)}, f32[2,2,72,512]{3,2,1,0:T(8,128)S(1)}, u32[]{:S(2)}, u32[]{:S(2)}) collective-permute-start(f32[2,2,72,512]{3,2,1,0:T(8,128)S(1)} %cells.1.cells_ref), channel_id=1, source_target_pairs={{0,4},{1,5},{2,6},{3,7},{4,0},{5,1},{6,2},{7,3},{8,12},{9,13},{10,... | collective-permute-start | bytes 1769480 | tf_op jit(solution)/shard_map/ppermute | solution.py:306
  35.2 3.2 %collective-permute-start.5 = (f32[24,128]{1,0:T(8,128)S(1)}, f32[24,128]{1,0:T(8,128)S(1)}, u32[]{:S(2)}, u32[]{:S(2)}) collective-permute-start(f32[24,128]{1,0:T(8,128)S(1)} %get-tuple-element.30.sums_ref), channel_id=1, source_target_pairs={{0,3},{1,2},{2,1},{3,0},{4,7},{5,6},{6,5},{7,4},{8,11},{9,10},{10,... | collective-permute-start | bytes 36872 | tf_op jit(solution)/shard_map/ppermute | solution.py:306
  35.9 2.6 %collective-permute-start.4 = (f32[24,128]{1,0:T(8,128)S(1)}, f32[24,128]{1,0:T(8,128)S(1)}, u32[]{:S(2)}, u32[]{:S(2)}) collective-permute-start(f32[24,128]{1,0:T(8,128)S(1)} %get-tuple-element.30.sums_ref), channel_id=1, source_target_pairs={{0,1},{1,0},{2,3},{3,2},{4,5},{5,4},{6,7},{7,6},{8,9},{9,8},{10,11... | collective-permute-start | bytes 36872 | tf_op jit(solution)/shard_map/ppermute | solution.py:306
  38.5 7.0 %collective-permute-start.7 = (f32[120,128]{1,0:T(8,128)S(1)}, f32[120,128]{1,0:T(8,128)S(1)}, u32[]{:S(2)}, u32[]{:S(2)}) collective-permute-start(f32[120,128]{1,0:T(8,128)S(1)} %pad_maximum_fusion), channel_id=1, source_target_pairs={{0,28},{1,29},{2,30},{3,31},{4,8},{5,9},{6,10},{7,11},{8,4},{9,5},... | collective-permute-start | bytes 184328 | tf_op jit(solution)/shard_map/ppermute | solution.py:306
  42.0 4.6 %collective-permute-start.6 = (f32[120,128]{1,0:T(8,128)S(1)}, f32[120,128]{1,0:T(8,128)S(1)}, u32[]{:S(2)}, u32[]{:S(2)}) collective-permute-start(f32[120,128]{1,0:T(8,128)S(1)} %pad_maximum_fusion), channel_id=1, source_target_pairs={{0,4},{1,5},{2,6},{3,7},{4,0},{5,1},{6,2},{7,3},{8,12},{9,13},{10,... | collective-permute-start | bytes 184328 | tf_op jit(solution)/shard_map/ppermute | solution.py:306

commit v4 on v3

--- a/solution.py
+++ b/solution.py
@@ -19,6 +19,7 @@
 ROWS_OUT = 24
 FLAG_LANES = 16
 MIB = 1024 * 1024
+NEARS = 6
 EXITS, OWNERS, INLETS = 0, 16, 32
 
 
@@ -96,30 +97,68 @@
     return jnp.concatenate([first, second, third, fourth], axis=0) + barred
 
 
-def forces_on(tiles, r, c, rows, wide, turned, pulled):
+def unit_operands(tiles, r, c, rows, wide):
     features = [target_features(tile, r, c + k, rows, wide) for k, tile in enumerate(tiles)]
-    target = jnp.concatenate(features, axis=1).astype(bf16)
-    weights = []
-    for k in range(4):
-        spread = [jnp.zeros((32, 2 * LANES), bf16)] * 4
-        spread[k] = target
-        weights.append(jnp.concatenate(spread, axis=0))
-    total = jnp.zeros((16, 2 * LANES), f32)
-    for i in range(3):
-        for j in range(4):
-            s = c - 1 + j
-            near = jnp.dot(turned[r + i - 1, s // 4], weights[s % 4], preferred_element_type=f32)
-            weight = jnp.maximum(near, 0.0)
-            pulls = pulled[r + i - 1, s]
-            high = weight.astype(bf16)
-            total = total + jnp.dot(pulls, high, preferred_element_type=f32)
-            low = (weight - high.astype(f32)).astype(bf16)
-            total = total + jnp.dot(pulls, low, preferred_element_type=f32)
+    features = jnp.concatenate(features, axis=1).astype(bf16)
+    start = (c - 1) // 4
+    ends = (c - 1, c + 2)
+
+    def spread(part, s):
+        at = 4 * (s // 4 - start) + s % 4
+        return jnp.concatenate([part if k == at else jnp.zeros_like(part) for k in range(8)], axis=0)
+
+    halves = [spread(features[:, k * LANES : (k + 1) * LANES], s) for k, s in enumerate(ends)]
+    return [spread(features, c), spread(features, c + 1), jnp.concatenate(halves, axis=1)]
+
+
+def forces_row(tiles, r, columns, rows, wide, turned, pulled, nears, founds):
+    ahead = len(nears) - 1
+    units = [(pair, kind, i) for pair in range(len(columns)) for kind in range(3) for i in range(3)]
+    blocks = wide // 4
+    operands = [None] * len(columns)
+
+    def begin(n):
+        pair, kind, i = units[n]
+        c = columns[pair]
+        staged = (3 * pair + kind) % 2
+        if i == 0:
+            if kind == 0:
+                operands[pair] = unit_operands(tiles[pair], r, c, rows, wide)
+            pltpu.matmul_push_rhs(operands[pair][kind], staged, 0)
+        start = (c - 1) // 4
+        after = start + 1 if start + 1 < blocks else 0
+        sources = jnp.concatenate([turned[r + i - 1, start], turned[r + i - 1, after]], axis=1)
+        pltpu.matmul_acc_lhs(nears[n % len(nears)], sources, load_staged_rhs=staged if i == 0 else None)
+
+    def finish(n):
+        pair, kind, i = units[n]
+        c = columns[pair]
+        weight = jnp.maximum(pltpu.matmul_pop(nears[n % len(nears)]), 0.0)
+        high = weight.astype(bf16)
+        low = (weight - high.astype(f32)).astype(bf16)
+        pltpu.matmul_push_rhs(jnp.concatenate([high, low], axis=0), n % 2, 1)
+        row = r + i - 1
+        if kind < 2:
+            pulls = pulled[row, c + kind]
+        else:
+            pulls = jnp.concatenate([pulled[row, c - 1], pulled[row, c + 2]], axis=0)
+        pulls = jnp.concatenate([pulls, pulls], axis=1)
+        pltpu.matmul_acc_lhs(founds[2 * pair + (kind == 2)], pulls, load_staged_rhs=n % 2)
+
+    for n in range(len(units) + ahead):
+        if n < len(units):
+            begin(n)
+        if n >= ahead:
+            finish(n - ahead)
     forces = []
-    for k, tile in enumerate(tiles):
-        first, second = total[0:8, k * LANES : (k + 1) * LANES], total[8:16, k * LANES : (k + 1) * LANES]
-        moving = centred(tile, r, c + k, rows, wide) - damping * pltpu.roll(tile, 5, 0)
-        forces.append((spring / cutoff_sq) * (moving * first[3:4, :] - first - second - pltpu.roll(second, 4, 0)))
+    for pair, c in enumerate(columns):
+        inner, outer = pltpu.matmul_pop(founds[2 * pair]), pltpu.matmul_pop(founds[2 * pair + 1])
+        for k, tile in enumerate(tiles[pair]):
+            part = slice(k * LANES, (k + 1) * LANES)
+            total = inner[:, part] + outer[16 * k : 16 * k + 16, part]
+            first, second = total[0:8], total[8:16]
+            moving = centred(tile, r, c + k, rows, wide) - damping * pltpu.roll(tile, 5, 0)
+            forces.append((spring / cutoff_sq) * (moving * first[3:4, :] - first - second - pltpu.roll(second, 4, 0)))
     return forces
 
 
@@ -148,8 +187,8 @@
 
 
 def particles_kernel(
-    ints_ref, own_ref, first_ref, second_ref, slots_ref,
-    sums_ref, settled_ref, leaving_ref, state, turned, pulled, begun, blocks,
+    ints_ref, own_ref, first_ref, second_ref,
+    settled_ref, leaving_ref, state, turned, pulled, begun, blocks,
     *, rows, cols,
 ):
     wide = cols + 2 * DEPTH
@@ -183,58 +222,45 @@
 
         lax.fori_loop(first, last, one_row, 0)
 
-    fill(state, 0, high)
-
-    def first_step(r, carry):
-        begun[r, 0] = jnp.zeros((COMPS, LANES), f32)
-        begun[r, wide - 1] = jnp.zeros((COMPS, LANES), f32)
-        for c in range(1, wide - 1, 2):
-            tiles = [state[r, c], state[r, c + 1]]
-            forces = forces_on(tiles, r, c, high, wide, turned, pulled)
-            for k in range(2):
+    def substeps(*accumulators):
+        nears, founds = accumulators[:NEARS], accumulators[NEARS:]
+        for accumulator in accumulators:
+            pltpu.matmul_pop(accumulator)
+        fill(state, 0, high)
+
+        def first_step(r, carry):
+            begun[r, 0] = jnp.zeros((COMPS, LANES), f32)
+            begun[r, wide - 1] = jnp.zeros((COMPS, LANES), f32)
+            columns = list(range(1, wide - 1, 2))
+            tiles = [[state[r, c], state[r, c + 1]] for c in columns]
+            forces = forces_row(tiles, r, columns, high, wide, turned, pulled, nears, founds)
+            for c in range(1, wide - 1):
                 inside = ((r >= DEPTH) | below) & ((r < rows + DEPTH) | above)
-                if c + k < DEPTH:
+                if c < DEPTH:
                     inside = inside & left
-                if c + k >= cols + DEPTH:
+                if c >= cols + DEPTH:
                     inside = inside & right
-                begun[r, c + k] = jnp.where(inside, stepped(tiles[k], forces[k]), 0.0)
-        return carry
-
-    lax.fori_loop(1, high - 1, first_step, 0)
-    fill(begun, 1, high - 1)
-
-    def second_step(r, carry):
-        for c in range(DEPTH, DEPTH + cols, 2):
-            tiles = [begun[r, c], begun[r, c + 1]]
-            forces = forces_on(tiles, r, c, high, wide, turned, pulled)
-            for k in range(2):
-                done = stepped(tiles[k], forces[k])
-                settled_ref[r - DEPTH, c + k - DEPTH] = done
-        return carry
-
-    lax.fori_loop(DEPTH, DEPTH + rows, second_step, 0)
-
-    def deposit(r, carry):
-        row = lax.broadcasted_iota(i32, (16, LANES), 0)
-        cell = lax.broadcasted_iota(i32, (LANES, LANES), 0)
-        for c in range(cols):
-            lift_high, lift_mid, lift_low = split(deposit_gain * settled_ref[r, c, 5:6, :])
-            parts = jnp.where(row == 0, lift_high, jnp.where(row == 1, lift_mid, jnp.where(row == 2, lift_low, 0.0)))
-            table = jnp.where(cell == slots_ref[r, c : c + 1, :], 1.0, 0.0).astype(bf16)
-            gathered = lax.dot_general(
-                parts.astype(bf16), table, (((1,), (1,)), ((), ())), preferred_element_type=f32
-            )
-            sums_ref[pl.ds(r * cols + c, 1), :] = jnp.sum(gathered, axis=0, keepdims=True)
-        return carry
-
-    lax.fori_loop(0, rows, deposit, 0)
-
-    lane = lax.broadcasted_iota(i32, (1, LANES), 1)
-    owner_row = jnp.zeros((1, LANES), i32)
-    for t in range(rows * cols):
-        owner_row = jnp.where(lax.rem(lane, rows * cols) == t, ints_ref[0, OWNERS + t], owner_row)
-    row = lax.broadcasted_iota(i32, (ROWS_OUT - rows * cols, LANES), 0)
-    sums_ref[rows * cols :, :] = jnp.where(row == 0, owner_row.astype(f32), 0.0)
+                begun[r, c] = jnp.where(inside, stepped(tiles[(c - 1) // 2][(c - 1) % 2], forces[c - 1]), 0.0)
+            return carry
+
+        lax.fori_loop(1, high - 1, first_step, 0)
+        fill(begun, 1, high - 1)
+
+        def second_step(r, carry):
+            columns = list(range(DEPTH, DEPTH + cols, 2))
+            tiles = [[begun[r, c], begun[r, c + 1]] for c in columns]
+            forces = forces_row(tiles, r, columns, high, wide, turned, pulled, nears, founds)
+            for c in range(cols):
+                settled_ref[r - DEPTH, c] = stepped(tiles[c // 2][c % 2], forces[c])
+            return carry
+
+        lax.fori_loop(DEPTH, DEPTH + rows, second_step, 0)
+
+    pl.run_scoped(
+        substeps,
+        *[pltpu.ACC(0)((LANES, 2 * LANES), f32)] * NEARS,
+        *[pltpu.ACC(1)((held, 2 * LANES), f32) for _ in range(wide // 2 - 1) for held in (16, 32)],
+    )
 
     leaving_ref[...] = jnp.zeros_like(leaving_ref)
     count = jnp.int32(0)
@@ -249,20 +275,18 @@
         count = count + flag
 
 
-def particles(ints, own, first, second, slots):
-    rows, cols = slots.shape[:2]
+def particles(ints, own, first, second, rows, cols):
     wide, high = cols + 2 * DEPTH, rows + 2 * DEPTH
     smem = pl.BlockSpec(memory_space=pltpu.SMEM)
     vmem = pl.BlockSpec(memory_space=pltpu.VMEM)
     return pl.pallas_call(
         functools.partial(particles_kernel, rows=rows, cols=cols),
         out_shape=(
-            jax.ShapeDtypeStruct((ROWS_OUT, LANES), f32),
             jax.ShapeDtypeStruct((rows, cols, COMPS, LANES), f32),
             jax.ShapeDtypeStruct((6, cols, LANES), f32),
         ),
-        in_specs=[smem, vmem, vmem, vmem, vmem],
-        out_specs=(vmem, vmem, vmem),
+        in_specs=[smem, vmem, vmem, vmem],
+        out_specs=(vmem, vmem),
         scratch_shapes=[
             pltpu.VMEM((high, wide, COMPS, LANES), f32),
             pltpu.VMEM((high, wide // 4, LANES, LANES), bf16),
@@ -272,7 +296,46 @@
         ],
         compiler_params=pltpu.CompilerParams(vmem_limit_bytes=12 * MIB),
         name="particles",
-    )(ints, own, first, second, slots)
+    )(ints, own, first, second)
+
+
+def deposit_kernel(ints_ref, settled_ref, slots_ref, blocks_ref, own_ref, shared_ref):
+    rows, cols = settled_ref.shape[:2]
+    quarters = blocks_ref.shape[0]
+    row = lax.broadcasted_iota(i32, (16, LANES), 0)
+    cell = lax.broadcasted_iota(i32, (LANES, LANES), 0)
+    lane = lax.broadcasted_iota(i32, (1, LANES), 1)
+    owner_row = jnp.zeros((1, LANES), i32)
+    for t in range(rows * cols):
+        r, c = t // cols, t % cols
+        owner = ints_ref[0, OWNERS + t]
+        owner_row = jnp.where(lax.rem(lane, rows * cols) == t, owner, owner_row)
+        lift_high, lift_mid, lift_low = split(deposit_gain * settled_ref[r, c, 5:6, :])
+        parts = jnp.where(row == 0, lift_high, jnp.where(row == 1, lift_mid, jnp.where(row == 2, lift_low, 0.0)))
+        table = jnp.where(cell == slots_ref[r, c : c + 1, :], 1.0, 0.0).astype(bf16)
+        gathered = lax.dot_general(parts.astype(bf16), table, (((1,), (1,)), ((), ())), preferred_element_type=f32)
+        sums = jnp.sum(gathered, axis=0, keepdims=True)
+        own_ref[t : t + 1, :] = sums
+        shared_ref[t : t + 1, :] = blocks_ref[owner % quarters, pl.ds(owner // quarters, 1), :] * sums
+    row = lax.broadcasted_iota(i32, (ROWS_OUT - rows * cols, LANES), 0)
+    shared_ref[rows * cols :, :] = jnp.where(row == 0, owner_row.astype(f32), 0.0)
+
+
+def deposits(ints, settled, slots, blocks):
+    rows, cols = settled.shape[:2]
+    smem = pl.BlockSpec(memory_space=pltpu.SMEM)
+    vmem = pl.BlockSpec(memory_space=pltpu.VMEM)
+    return pl.pallas_call(
+        deposit_kernel,
+        out_shape=(
+            jax.ShapeDtypeStruct((rows * cols, LANES), f32),
+            jax.ShapeDtypeStruct((ROWS_OUT, LANES), f32),
+        ),
+        in_specs=[smem, vmem, vmem, vmem],
+        out_specs=(vmem, vmem),
+        compiler_params=pltpu.CompilerParams(vmem_limit_bytes=4 * MIB),
+        name="deposits",
+    )(ints, settled, slots, blocks)
 
 
 def matching(heights, groups, axis, odd, wrap):
@@ -332,12 +395,11 @@
 ):
     rows, cols = state_ref.shape[1:3]
     _, levels, across, along = cells_ref.shape
-    across = across - 8
     pairs = (
         (positions_hbm, state_ref.at[0:3]),
         (velocities_hbm, state_ref.at[3:6]),
-        (gas_hbm, cells_ref.at[0, :, 0:across]),
-        (diagonal_hbm, cells_ref.at[1, :, 0:across]),
+        (gas_hbm, cells_ref.at[0]),
+        (diagonal_hbm, cells_ref.at[1]),
         (contacts_hbm, contacts_ref),
         (exits_hbm, exits_ref),
         (owners_hbm, owners_ref),
@@ -349,7 +411,6 @@
         copy.start()
     sides[...] = jnp.zeros_like(sides) + zeros_ref[0:1]
     wide_flags[...] = jnp.zeros_like(wide_flags)
-    cells_ref[:, :, across:] = jnp.zeros((2, levels, 8, along), f32)
     for copy in copies:
         copy.wait()
     lane = lax.broadcasted_iota(i32, (1, LANES), 1)
@@ -405,7 +466,7 @@
             jax.ShapeDtypeStruct((1, LANES), i32),
             jax.ShapeDtypeStruct(slots.shape, i32),
             jax.ShapeDtypeStruct((6, rows, cols, LANES), f32),
-            jax.ShapeDtypeStruct((2, levels, across + 8, along), f32),
+            jax.ShapeDtypeStruct((2, levels, across, along), f32),
         ),
         in_specs=[vmem] + [pl.BlockSpec(memory_space=pl.ANY)] * 9,
         out_specs=(vmem,) * 7,
@@ -461,45 +522,72 @@
     return lines[row : row + 1]
 
 
-def cells_kernel(cells_in, line_a, line_b, cells_ref):
-    kinds, levels, rows, along = cells_ref.shape
+def faces_kernel(cells_ref, line_a, line_b, scaling_ref, blocks_ref, first_ref, second_ref):
+    _, levels, across, along = cells_ref.shape
     quarters = along // LANES
-    even = position()[5]
-    cells_ref[...] = cells_in[...]
-    for kind in range(kinds):
-        for z in range(levels):
+    left, right, _, _, even, even_c = position()
+    row = lax.broadcasted_iota(i32, (across, along), 0)
+    place = lax.broadcasted_iota(i32, (across, along), 1)
+    scaled = []
+    for z in range(levels):
+        scaling_ref[z] = 1.0 / (6.0 + cells_ref[1, z])
+        scaled.append(scaling_ref[z] * cells_ref[0, z])
+        for q in range(quarters):
+            blocks_ref[q, z * across : (z + 1) * across] = scaling_ref[z, :, q * LANES : (q + 1) * LANES]
+    faces = []
+    for z in range(levels):
+        ends = []
+        for k, present, flip in ((1, left, False), (0, right, True)):
+            parts = []
             for q in range(quarters):
-                low = [line_at(lines, z, 1, kind, q, quarters) for lines in (line_a, line_b)]
-                top = [line_at(lines, z, 0, kind, q, quarters) for lines in (line_a, line_b)]
-                cells_ref[kind, z, rows - 8 : rows, q * LANES : (q + 1) * LANES] = jnp.concatenate(
-                    [
-                        jnp.where(even, low[1], low[0]),
-                        jnp.where(even, top[0], top[1]),
-                        jnp.zeros((6, LANES), f32),
-                    ],
-                    axis=0,
-                )
-
-
-def cells_of(cells, lines):
+                kinds = []
+                for kind in range(2):
+                    one, two = (line_at(lines, z, k, kind, q, quarters) for lines in (line_a, line_b))
+                    kinds.append(jnp.where(even_c, one, two) if flip else jnp.where(even_c, two, one))
+                parts.append(jnp.where(present, kinds[0] / (6.0 + kinds[1]), 0.0))
+            ends.append(jnp.concatenate(parts, axis=1))
+        mid = scaled[z]
+        total = scaled[levels - 1 - z]
+        total = total + jnp.where(row > 0, pltpu.roll(mid, 1, 0), ends[0])
+        total = total + jnp.where(row < across - 1, pltpu.roll(mid, across - 1, 0), ends[1])
+        total = total + jnp.where(place > 0, pltpu.roll(mid, 1, 1), 0.0)
+        total = total + jnp.where(place < along - 1, pltpu.roll(mid, along - 1, 1), 0.0)
+        outer = jnp.concatenate([*ends, jnp.zeros((6, along), f32)], axis=0)
+        faces.append((scaling_ref[z], mid, total, outer))
+    for n in range(4):
+        bottom, top = faces[0][n], faces[levels - 1][n]
+        at = slice(n * across, n * across + bottom.shape[0])
+        first_ref[at] = jnp.where(even, top, bottom)
+        second_ref[at] = jnp.where(even, bottom, top)
+
+
+def faces_of(cells, lines):
+    _, levels, across, along = cells.shape
     vmem = pl.BlockSpec(memory_space=pltpu.VMEM)
+    face = jax.ShapeDtypeStruct((3 * across + 8, along), f32)
     return pl.pallas_call(
-        cells_kernel,
-        out_shape=jax.ShapeDtypeStruct(cells.shape, f32),
-        in_specs=[pl.BlockSpec(memory_space=pltpu.VMEM)] * 3,
-        out_specs=vmem,
-        compiler_params=pltpu.CompilerParams(vmem_limit_bytes=4 * MIB),
-        name="cells",
+        faces_kernel,
+        out_shape=(
+            jax.ShapeDtypeStruct((levels, across, along), f32),
+            jax.ShapeDtypeStruct((along // LANES, levels * across, LANES), f32),
+            face,
+            face,
+        ),
+        in_specs=[vmem] * 3,
+        out_specs=(vmem,) * 4,
+        compiler_params=pltpu.CompilerParams(vmem_limit_bytes=8 * MIB),
+        name="faces",
     )(cells, *lines)
 
 
 def right_side_kernel(
-    sums_ref, side_a, side_b, height_a, height_b, cells_ref, line_a, line_b, gas_a, gas_b, rhs_ref, near_ref, far_ref, dots_ref, scaling, rhs, first, second,
+    own_ref, shared_ref, side_a, side_b, height_a, height_b, cells_ref, scaling_ref, line_a, line_b, face_a, face_b,
+    rhs_ref, near_ref, far_ref, dots_ref, first, second,
 ):
-    _, levels, across, along = cells_ref.shape
-    across = across - 8
+    levels, across, along = scaling_ref.shape
     edge = 8
     wide = across + 2 * edge
+    inner = slice(edge, edge + across)
     quarters = along // LANES
     left, right, below, above, even, even_c = position()
 
@@ -508,46 +596,21 @@
 
     def high_of(is_even, one, two):
         return jnp.where(is_even, one, two)
-
-    for ref in (scaling, rhs):
-        ref[:, 0:edge, :] = jnp.zeros((3 * levels, edge, along), f32)
-        ref[:, edge + across :, :] = jnp.zeros((3 * levels, edge, along), f32)
-    scaling[levels : 2 * levels, edge : edge + across] = 1.0 / (6.0 + cells_ref[1, :, 0:across])
-    rhs[levels : 2 * levels, edge : edge + across] = cells_ref[0, :, 0:across]
-    for level, choose, present in ((0, low_of, below), (2 * levels, high_of, above)):
-        for z in range(levels):
-            rhs[level + z, edge : edge + across] = choose(even, gas_a[0, z, 0:across], gas_b[0, z, 0:across])
-            m = 1.0 / (6.0 + choose(even, gas_a[1, z, 0:across], gas_b[1, z, 0:across]))
-            scaling[level + z, edge : edge + across] = jnp.where(present, m, 0.0)
-            for row, x, beside_it in ((across, edge - 1, left), (across + 1, edge + across, right)):
-                line = slice(row, row + 1)
-                rhs[level + z, x : x + 1] = choose(even, gas_a[0, z, line], gas_b[0, z, line])
-                m = 1.0 / (6.0 + choose(even, gas_a[1, z, line], gas_b[1, z, line]))
-                scaling[level + z, x : x + 1] = jnp.where(present & beside_it, m, 0.0)
-    for choose, start, present in ((low_of, edge - 2, left), (high_of, edge + across, right)):
-        for z in range(levels):
-            for k in range(2):
-                for q in range(quarters):
-                    part = slice(q * LANES, (q + 1) * LANES)
-                    x = slice(start + k, start + k + 1)
-                    kinds = [
-                        choose(even_c, *[line_at(lines, z, k, kind, q, quarters) for lines in (line_a, line_b)])
-                        for kind in range(2)
-                    ]
-                    rhs[levels + z, x, part] = kinds[0]
-                    scaling[levels + z, x, part] = jnp.where(present, 1.0 / (6.0 + kinds[1]), 0.0)
 
     lane = lax.broadcasted_iota(i32, (1, LANES), 1)
     tiles = 16
     shift_q, shift_x = quarters.bit_length() - 1, across.bit_length() - 1
-    groups = []
-    for name, choose, present in (("below", low_of, below), ("own", None, None), ("above", high_of, above)):
+    for level, choose, present in ((0, low_of, below), (levels, None, None), (2 * levels, high_of, above)):
         if choose is None:
-            parts = [low_of(even_c, side_a[...], side_b[...]), sums_ref[...], high_of(even_c, side_a[...], side_b[...])]
+            parts = [low_of(even_c, side_a[...], side_b[...]), shared_ref[...], high_of(even_c, side_a[...], side_b[...])]
+            values = [parts[0][0:tiles], own_ref[...], parts[2][0:tiles]]
         else:
-            block = [choose(even, height_a[k * ROWS_OUT : (k + 1) * ROWS_OUT], height_b[k * ROWS_OUT : (k + 1) * ROWS_OUT]) for k in range(3)]
+            block = [
+                choose(even, height_a[k * ROWS_OUT : (k + 1) * ROWS_OUT], height_b[k * ROWS_OUT : (k + 1) * ROWS_OUT])
+                for k in range(3)
+            ]
             parts = [low_of(even_c, block[1], block[2]), block[0], high_of(even_c, block[1], block[2])]
-        level = 0 if name == "below" else levels if name == "own" else 2 * levels
+            values = [part[0:tiles] for part in parts]
         code = jnp.full((1, LANES), -1, i32)
         for n, part in enumerate(parts):
             owner = part[tiles : tiles + 1].astype(i32)
@@ -562,7 +625,7 @@
             if present is not None:
                 here = here & present
             code = jnp.where(here, (z * wide + x) * quarters + (owner & (quarters - 1)), code)
-        values = jnp.concatenate([part[0:tiles] for part in parts], axis=0)
+        values = jnp.concatenate(values, axis=0)
         high = values.astype(bf16)
         low = (values - high.astype(f32)).astype(bf16)
         values = jnp.concatenate([high, low, jnp.zeros((LANES - 6 * tiles, LANES), bf16)], axis=0)
@@ -571,10 +634,27 @@
             table = jnp.where(code == spot + k, 1.0, 0.0).astype(bf16)
             added = jnp.dot(table, values, preferred_element_type=f32)
             for z in range(levels):
-                rhs[level + z, :, k * LANES : (k + 1) * LANES] -= added[z * wide : (z + 1) * wide]
-
-    for z in range(3 * levels):
-        first[z] = scaling[z] * rhs[z]
+                first[level + z, :, k * LANES : (k + 1) * LANES] = -added[z * wide : (z + 1) * wide]
+
+    second[:, 0:edge, :] = jnp.zeros((3 * levels, edge, along), f32)
+    second[:, edge + across :, :] = jnp.zeros((3 * levels, edge, along), f32)
+    for z in range(levels):
+        rhs = cells_ref[0, z] + first[levels + z, inner]
+        rhs_ref[z] = rhs
+        first[levels + z, inner] = scaling_ref[z] * rhs
+        for choose, start, present, beside_at in ((low_of, edge - 2, left, 1), (high_of, edge + across, right, 0)):
+            for k in range(2):
+                x = slice(start + k, start + k + 1)
+                for q in range(quarters):
+                    part = slice(q * LANES, (q + 1) * LANES)
+                    kinds = [
+                        choose(even_c, *[line_at(lines, z, k, kind, q, quarters) for lines in (line_a, line_b)])
+                        for kind in range(2)
+                    ]
+                    m = jnp.where(present, 1.0 / (6.0 + kinds[1]), 0.0)
+                    first[levels + z, x, part] += m * kinds[0]
+                    if k == beside_at:
+                        second[levels + z, x, part] = m
     place = lax.broadcasted_iota(i32, (wide, along), 1)
 
     def beside(ref, z):
@@ -583,30 +663,38 @@
         total = total + jnp.where(place > 0, pltpu.roll(mid, 1, 1), 0.0)
         return total + jnp.where(place < along - 1, pltpu.roll(mid, along - 1, 1), 0.0)
 
+    for z, choose, present in ((levels - 1, low_of, below), (2 * levels, high_of, above)):
+        part = [slice(n * across, (n + 1) * across) for n in range(3)]
+        near = beside(first, z)[inner] + choose(even, face_a[part[2]], face_b[part[2]])
+        second[z, inner] = jnp.where(present, choose(even, face_a[part[0]], face_b[part[0]]) * near, 0.0)
+        first[z, inner] += jnp.where(present, choose(even, face_a[part[1]], face_b[part[1]]), 0.0)
+        for n, x in enumerate((edge - 1, edge + across)):
+            line = slice(3 * across + n, 3 * across + n + 1)
+            first[z, x : x + 1] += jnp.where(present, choose(even, face_a[line], face_b[line]), 0.0)
+
     dots = [jnp.zeros((8, LANES), f32)] * 4
 
     def folded(value):
         value = jnp.sum(value.reshape(across // 8, 8, along), axis=0)
         return sum(value[:, k * LANES : (k + 1) * LANES] for k in range(quarters))
 
-    inner = slice(edge, edge + across)
-    for z in range(levels - 1, 2 * levels + 1):
+    ends = (slice(0, edge), slice(edge + across, wide))
+    for z in range(levels, 2 * levels):
         near = beside(first, z)
-        second[z] = scaling[z] * near
-        if levels <= z < 2 * levels:
-            near = near[inner]
-            near_ref[z - levels] = near
-            rhs_ref[z - levels] = rhs[z, inner]
-            z0 = first[z, inner]
-            dots[0] = dots[0] + folded(z0 * rhs[z, inner])
-            dots[1] = dots[1] + folded(z0 * near)
-            dots[2] = dots[2] + folded(second[z, inner] * near)
+        for end in ends:
+            second[z, end] = second[z, end] * near[end]
+        near = near[inner]
+        scaled = scaling_ref[z - levels] * near
+        second[z, inner] = scaled
+        near_ref[z - levels] = near
+        start = first[z, inner]
+        dots[0] = dots[0] + folded(start * rhs_ref[z - levels])
+        dots[1] = dots[1] + folded(start * near)
+        dots[2] = dots[2] + folded(scaled * near)
     for z in range(levels, 2 * levels):
         far = beside(second, z)[inner]
         far_ref[z - levels] = far
         dots[3] = dots[3] + folded(second[z, inner] * far)
-    row = lax.broadcasted_iota(i32, (8, LANES), 0)
-    lane8 = lax.broadcasted_iota(i32, (8, LANES), 1)
     line = jnp.zeros((1, LANES), f32)
     for k in range(4):
         total = jnp.sum(jnp.sum(dots[k], axis=0, keepdims=True), axis=1, keepdims=True)
@@ -614,24 +702,23 @@
     dots_ref[...] = jnp.broadcast_to(line, dots_ref.shape)
 
 
-def right_side_of(sums, side, height, cells, lines, gases, devices):
-    _, levels, across, along = cells.shape
-    across = across - 8
+def right_side_of(own, shared, side, height, cells, scaling, lines, faces, devices):
+    levels, across, along = scaling.shape
     vmem = pl.BlockSpec(memory_space=pltpu.VMEM)
     whole = pltpu.VMEM((3 * levels, across + 16, along), f32)
     return pl.pallas_call(
         right_side_kernel,
-        out_shape=(jax.ShapeDtypeStruct((levels, across, along), f32),) * 3 + (jax.ShapeDtypeStruct((devices, LANES), f32),),
-        in_specs=[vmem] * 10,
+        out_shape=(jax.ShapeDtypeStruct(scaling.shape, f32),) * 3 + (jax.ShapeDtypeStruct((devices, LANES), f32),),
+        in_specs=[vmem] * 12,
         out_specs=(vmem,) * 4,
-        scratch_shapes=[whole] * 4,
+        scratch_shapes=[whole] * 2,
         compiler_params=pltpu.CompilerParams(vmem_limit_bytes=16 * MIB),
         name="right_side",
-    )(sums, *side, *height, cells, *lines, *gases)
+    )(own, shared, *side, *height, cells, scaling, *lines, *faces)
 
 
 def results_kernel(
-    ints_ref, dots_ref, rhs_ref, near_ref, far_ref, cells_ref, settled_ref,
+    ints_ref, dots_ref, rhs_ref, near_ref, far_ref, scaling_ref, settled_ref,
     height_a, height_b, around_ref, positions_ref, velocities_ref, pressure_ref, residual_ref,
 ):
     rows, cols = settled_ref.shape[:2]
@@ -649,7 +736,7 @@
     one = alpha + later * (1.0 - alpha + beta)
     two = later * alpha
     for z in range(rhs_ref.shape[0]):
-        m = 1.0 / (6.0 + cells_ref[1, z, 0 : rhs_ref.shape[1]])
+        m = scaling_ref[z]
         rhs, near = rhs_ref[z], near_ref[z]
         pressure_ref[z] = m * (one * rhs + two * near)
         residual_ref[z] = (1.0 - one) * rhs + (one - two) * near + two * far_ref[z]
@@ -668,7 +755,7 @@
             target[d % 3, 0, pl.ds(ints_ref[0, INLETS + k], 1)] = tiles[k : k + 1]
 
 
-def results_of(ints, dots, rhs, near, far, cells, settled, height, around):
+def results_of(ints, dots, rhs, near, far, scaling, settled, height, around):
     rows, cols = settled.shape[:2]
     smem = pl.BlockSpec(memory_space=pltpu.SMEM)
     vmem = pl.BlockSpec(memory_space=pltpu.VMEM)
@@ -681,7 +768,7 @@
         out_specs=(vmem,) * 4,
         compiler_params=pltpu.CompilerParams(vmem_limit_bytes=8 * MIB),
         name="results",
-    )(ints, dots, rhs, near, far, cells, settled, *height, around)
+    )(ints, dots, rhs, near, far, scaling, settled, *height, around)
 
 
 def on_device(
@@ -699,16 +786,22 @@
     ]
     window = merged(state, flags, lines)
     beside = exchanged(window, "height", False)
-    cells = cells_of(cells, lines)
-    sent, beside = lax.optimization_barrier((cells, beside))
-    gases = exchanged(sent, "height", False)
-    sums, settled, leaving = particles(ints, window, *beside, slots)
-    near = exchanged(sums, "cols", True)
-    parcel = jnp.concatenate([sums, *near, leaving.reshape(-1, LANES)], axis=0)
+    scaling, blocks, *faces = faces_of(cells, lines)
+    faces, beside = lax.optimization_barrier((faces, beside))
+    faces = [
+        lax.ppermute(value, ("height", "cols"), matching(heights, groups, "height", odd, False))
+        for value, odd in zip(faces, (False, True))
+    ]
+    settled, leaving = particles(ints, window, *beside, *state.shape[1:3])
+    own, shared = deposits(ints, settled, slots, blocks)
+    near = exchanged(shared, "cols", True)
+    parcel = jnp.concatenate([shared, *near, leaving.reshape(-1, LANES)], axis=0)
     parcels = exchanged(parcel, "height", True)
-    rhs, first, second, dots = right_side_of(sums, near, parcels, cells, lines, gases, heights * groups)
+    rhs, first, second, dots = right_side_of(
+        own, shared, near, parcels, cells, scaling, lines, faces, heights * groups
+    )
     dots = lax.all_to_all(dots, ("height", "cols"), 0, 0, tiled=True)
-    return results_of(ints, dots, rhs, first, second, cells, settled, parcels, leaving)
+    return results_of(ints, dots, rhs, first, second, scaling, settled, parcels, leaving)
 
 
 def solution(mesh):

time: 61.2 us -> 56.2 us (0.918)
  Pallas kernels: 21 us -> 18.5 us
  starting transfers between devices: 15.6 us -> 14.2 us
  blocking collectives: 11.6 us -> 10.5 us
    ppermute x8 -> x6, starting transfers between devices: 12.4 us -> 8.54 us  [exchanged(): lax.ppermute(value, ('height', 'cols'), matching(heights, groups, axis, o...]
    pallas_call x1, Pallas kernels: 17.3 us -> 13.7 us  [particles(): pl.pallas_call(functools.partial(particles_kernel, rows=rows, cols=cols),...]
    ppermute x0 -> x2, starting transfers between devices: none -> 2.47 us  [on_device(): lax.ppermute(value, ('height', 'cols'), matching(heights, groups, 'height...]
    all_to_all x1, blocking collectives: 11.6 us -> 10.5 us  [on_device(): dots = lax.all_to_all(dots, ('height', 'cols'), 0, 0, tiled=True)]
    pallas_call x2 -> x3, Pallas kernels: 1.14 us -> 2.22 us  [the longest x1 1.01 us: right_side_of(): pl.pallas_call(right_side_kernel, out_shape=(jax.ShapeDtypeStruct(scaling...]
    ppermute x8 -> x6, waiting for transfers between devices: 9.37 us -> 9.31 us  [exchanged(): lax.ppermute(value, ('height', 'cols'), matching(heights, groups, axis, o...]
  transfers between devices with their start and end apart: 10 -> 10, of which waited for: 5 -> 5; matrix products, arithmetic and copies ran while one was open for 0% -> 0% of each run, Pallas kernels for 28% -> 27%
where the time goes in v4:
time: 56.2 us; the launch traced here: 56 us
  Pallas kernels  18.5 us (33%)
  starting transfers between devices  14.2 us (25%)
  waiting for transfers between devices  11 us (20%)
  blocking collectives  10.5 us (19%)
  local copies, waits for them, and re-layouts  0.96 us (2%)
  between operations  0.8 us (1%)
    pallas_call x1, Pallas kernels, particles(): pl.pallas_call(functools.partial(particles_kernel, rows=rows, cols=cols),...  13.7 us
    all_to_all x1, blocking collectives, on_device(): dots = lax.all_to_all(dots, ('height', 'cols'), 0, 0, tiled=True)  10.5 us
    ppermute x6, waiting for transfers between devices, exchanged(): lax.ppermute(value, ('height', 'cols'), matching(heights, groups, axis, o...  9.31 us
    ppermute x6, starting transfers between devices, exchanged(): lax.ppermute(value, ('height', 'cols'), matching(heights, groups, axis, o...  8.54 us
    ppermute x2, starting transfers between devices, on_device(): lax.ppermute(value, ('height', 'cols'), matching(heights, groups, 'cols',...  3.16 us
    ppermute x2, starting transfers between devices, on_device(): lax.ppermute(value, ('height', 'cols'), matching(heights, groups, 'height...  2.47 us
    ppermute x2, waiting for transfers between devices, on_device(): lax.ppermute(value, ('height', 'cols'), matching(heights, groups, 'cols',...  1.67 us
    pallas_call x1, Pallas kernels, results_of(): pl.pallas_call(results_kernel, out_shape=(particle, particle, field, fiel...  1.66 us
  transfers between devices with their start and end apart: 10, of which 5 were waited for; matrix products, arithmetic and copies ran while one was open for 0% of the time, Pallas kernels for 27%

profile of v4, /device:TPU:0, one launch (start us, length us, event | category | flops | bytes accessed | tf_op | source)
XLA Modules:
  0.0 56.0 jit_solution(8499066680633287046)
XLA Ops:
  0.6 0.0 copy-start.1
  0.6 0.0 copy-start
  0.7 0.0 copy-start.5
  0.7 0.0 copy-start.4
  0.7 0.0 copy-start.3
  0.7 0.0 copy-start.2
  0.7 0.0 copy-start.7
  0.7 0.0 copy-start.6
  0.7 0.0 copy-start.8
  0.7 0.8 %copy-done.1 = f32[2,64,512]{2,1,0:T(8,128)S(1)} copy-done((f32[2,64,512]{2,1,0:T(8,128)S(1)}, f32[2,64,512]{2,1,0:T(8,128)}, u32[]{:S(2)}) %copy-start.1) | copy-done | bytes 262168
  1.6 0.1 copy-done
  1.7 0.0 copy-done.5
  1.7 0.0 copy-done.4
  1.7 0.0 copy-done.3
  1.7 0.0 copy-done.2
  1.7 0.0 copy-done.7
  1.7 0.0 copy-done.6
  1.7 0.0 copy-done.8
  1.7 0.9 %pack.1 = (f32[64,128]{1,0:T(8,128)S(1)}, f32[64,128]{1,0:T(8,128)S(1)}, f32[2,128]{1,0:T(2,128)S(1)}, s32[1,128]{1,0:T(1,128)S(1)}, s32[2,8,128]{2,1,0:T(8,128)...) custom-call(f32[8,128]{1,0:T(8,128)S(1)} %begin.1.zeros_ref, s32[2,8]{1,0:T(2,128)S(1)} %copy-done.6, ...), custom_call_target="tpu_custom_call" | custom-call | tf_op jit(solution)/shard_map/pack/pallas_call | solution.py:460
  2.6 0.5 collective-permute-start
  3.2 2.6 %collective-permute-start.1 = (f32[64,128]{1,0:T(8,128)S(1)}, f32[64,128]{1,0:T(8,128)S(1)}, u32[]{:S(2)}, u32[]{:S(2)}) collective-permute-start(f32[64,128]{1,0:T(8,128)S(1)} %get-tuple-element.31), channel_id=1, source_target_pairs={{0,3},{1,2},{2,1},{3,0},{4,7},{5,6},{6,5},{7,4},{8,11},{9,10},{10,... | collective-permute-start | bytes 98312 | tf_op jit(solution)/shard_map/ppermute | solution.py:784
  5.8 0.0 collective-permute-done.line_a
  5.8 1.7 %collective-permute-done.1.line_b = f32[64,128]{1,0:T(8,128)S(1)} collective-permute-done((f32[64,128]{1,0:T(8,128)S(1)}, f32[64,128]{1,0:T(8,128)S(1)}, u32[]{:S(2)}, u32[]{:S(2)}) %collective-permute-start.1) | collective-permute-done | bytes 32800 | tf_op jit(solution)/shard_map/ppermute | solution.py:784
  7.5 0.2 collective-permute-start.3
  7.7 3.0 %collective-permute-start.2 = (f32[152,128]{1,0:T(8,128)S(1)}, f32[152,128]{1,0:T(8,128)S(1)}, u32[]{:S(2)}, u32[]{:S(2)}) collective-permute-start(f32[152,128]{1,0:T(8,128)S(1)} %merge.1.own_ref), channel_id=1, source_target_pairs={{0,4},{1,5},{2,6},{3,7},{4,0},{5,1},{6,2},{7,3},{8,12},{9,13},{10,... | collective-permute-start | bytes 233480 | tf_op jit(solution)/shard_map/ppermute | solution.py:369
  10.7 0.3 faces.1
  11.0 0.0 collective-permute-done.3.second_ref
  11.0 3.0 %collective-permute-done.2.first_ref = f32[152,128]{1,0:T(8,128)S(1)} collective-permute-done((f32[152,128]{1,0:T(8,128)S(1)}, f32[152,128]{1,0:T(8,128)S(1)}, u32[]{:S(2)}, u32[]{:S(2)}) %collective-permute-start.2) | collective-permute-done | bytes 77856 | tf_op jit(solution)/shard_map/ppermute | solution.py:369
  14.0 2.5 %collective-permute-start.8 = (f32[200,512]{1,0:T(8,128)S(1)}, f32[200,512]{1,0:T(8,128)S(1)}, u32[]{:S(2)}, u32[]{:S(2)}) collective-permute-start(f32[200,512]{1,0:T(8,128)S(1)} %get-tuple-element.44), channel_id=1, source_target_pairs={{0,4},{1,5},{2,6},{3,7},{4,0},{5,1},{6,2},{7,3},{8,12},{9,13},{10,... | collective-permute-start | bytes 1228808 | tf_op jit(solution)/shard_map/ppermute | solution.py:792
  16.4 0.0 collective-permute-start.9
  16.4 13.7 %particles.1 = (f32[2,8,8,128]{3,2,1,0:T(8,128)S(1)}, f32[6,8,128]{2,1,0:T(8,128)S(1)}) custom-call(s32[1,128]{1,0:T(1,128)S(1)} %get-tuple-element.27.ints_ref, f32[152,128]{1,0:T(8,128)S(1)} %merge.1.own_ref, f32[152,128]{1,0:T(8,128)S(1)} %collective-permute-done.2.first_ref, f32[152,128]{1,0:T(8,128)S(1)} %collective-permute-done.3.second_ref), custom_call_target="tpu_custom_call" | custom-call | tf_op jit(solution)/shard_map/particles/pallas_call | solution.py:282
  30.2 0.9 %deposits.1 = (f32[16,128]{1,0:T(8,128)S(1)}, f32[24,128]{1,0:T(8,128)S(1)}) custom-call(s32[1,128]{1,0:T(1,128)S(1)} %get-tuple-element.27.ints_ref, f32[2,8,8,128]{3,2,1,0:T(8,128)S(1)} %get-tuple-element.37.settled_ref, s32[2,8,128]{2,1,0:T(8,128)S(1)} %get-tuple-element.38.slots_ref, f32[4,128,128]{2,1,0:T(8,128)S(1)} %get-tuple-element.39.blocks_ref), custom_call_target="tpu_custom_call" | custom-call | tf_op jit(solution)/shard_map/deposits/pallas_call | solution.py:328
  31.1 1.7 %collective-permute-start.5 = (f32[24,128]{1,0:T(8,128)S(1)}, f32[24,128]{1,0:T(8,128)S(1)}, u32[]{:S(2)}, u32[]{:S(2)}) collective-permute-start(f32[24,128]{1,0:T(8,128)S(1)} %get-tuple-element.41.shared_ref), channel_id=1, source_target_pairs={{0,3},{1,2},{2,1},{3,0},{4,7},{5,6},{6,5},{7,4},{8,11},{9,10},{10,... | collective-permute-start | bytes 36872 | tf_op jit(solution)/shard_map/ppermute | solution.py:369
  32.8 0.0 collective-permute-start.4
  32.8 1.5 %collective-permute-done.5.side_b = f32[24,128]{1,0:T(8,128)S(1)} collective-permute-done((f32[24,128]{1,0:T(8,128)S(1)}, f32[24,128]{1,0:T(8,128)S(1)}, u32[]{:S(2)}, u32[]{:S(2)}) %collective-permute-start.5) | collective-permute-done | bytes 12320 | tf_op jit(solution)/shard_map/ppermute | solution.py:369
  34.3 0.0 collective-permute-done.4.side_a
  34.3 3.6 %collective-permute-start.7 = (f32[120,128]{1,0:T(8,128)S(1)}, f32[120,128]{1,0:T(8,128)S(1)}, u32[]{:S(2)}, u32[]{:S(2)}) collective-permute-start(f32[120,128]{1,0:T(8,128)S(1)} %pad_maximum_fusion), channel_id=1, source_target_pairs={{0,28},{1,29},{2,30},{3,31},{4,8},{5,9},{6,10},{7,11},{8,4},{9,5},... | collective-permute-start | bytes 184328 | tf_op jit(solution)/shard_map/ppermute | solution.py:369
  37.9 0.0 collective-permute-start.6
  37.9 3.6 %collective-permute-done.7.height_b = f32[120,128]{1,0:T(8,128)S(1)} collective-permute-done((f32[120,128]{1,0:T(8,128)S(1)}, f32[120,128]{1,0:T(8,128)S(1)}, u32[]{:S(2)}, u32[]{:S(2)}) %collective-permute-start.7) | collective-permute-done | bytes 61472 | tf_op jit(solution)/shard_map/ppermute | solution.py:369
  41.6 1.2 %collective-permute-done.6.height_a = f32[120,128]{1,0:T(8,128)S(1)} collective-permute-done((f32[120,128]{1,0:T(8,128)S(1)}, f32[120,128]{1,0:T(8,128)S(1)}, u32[]{:S(2)}, u32[]{:S(2)}) %collective-permute-start.6) | collective-permute-done | bytes 61472 | tf_op jit(solution)/shard_map/ppermute | solution.py:369
  42.8 0.0 collective-permute-done.8.face_a
  42.8 0.0 collective-permute-done.9.face_b
  42.8 1.0 %right_side.1 = (f32[2,64,512]{2,1,0:T(8,128)S(1)}, f32[2,64,512]{2,1,0:T(8,128)S(1)}, f32[2,64,512]{2,1,0:T(8,128)S(1)}, f32[32,128]{1,0:T(8,128)S(1)}) custom-call(f32[16,128]{1,0:T(8,128)S(1)} %get-tuple-element.40.own_ref, f32[24,128]{1,0:T(8,128)S(1)} %get-tuple-element.41.shared_ref, f32[24,128]{1,0:T(8,128)S(1)} %collective-permute-done.4.side_a, ...), custom_call_target="tpu_custom_call" | custom-call | tf_op jit(solution)/shard_map/right_side/pallas_call | solution.py:709
  43.8 10.5 %all_to_all.11 = f32[32,1,128]{2,1,0:T(1,128)S(1)} all-to-all(f32[32,1,128]{2,1,0:T(1,128)S(1)} %bitcast.8), channel_id=1, replica_groups=mesh['height'=8,'cols'=4] {'height','cols'}, dimensions={0} | all-to-all | bytes 32768 | tf_op jit(solution)/shard_map/all_to_all | solution.py:803
  54.3 1.7 %results.1 = (f32[3,2,8,128]{3,2,1,0:T(8,128)}, f32[3,2,8,128]{3,2,1,0:T(8,128)}, f32[2,64,512]{2,1,0:T(8,128)}, f32[2,64,512]{2,1,0:T(8,128)}) custom-call(s32[1,128]{1,0:T(1,128)S(1)} %get-tuple-element.27.ints_ref, f32[32,128]{1,0:T(8,128)S(1)} %bitcast.7, f32[2,64,512]{2,1,0:T(8,128)S(1)} %get-tuple-element.47.rhs_ref, ...), custom_call_target="tpu_custom_call" | custom-call | tf_op jit(solution)/shard_map/results/pallas_call | solution.py:764
  (3 shorter events, 0.0 us)
Async XLA Ops:
  0.6 1.0 %copy-start.1 = (f32[2,64,512]{2,1,0:T(8,128)S(1)}, f32[2,64,512]{2,1,0:T(8,128)}, u32[]{:S(2)}) copy-start(f32[2,64,512]{2,1,0:T(8,128)} %diagonal_hbm.1) | copy-start | bytes 786436
  0.6 1.0 %copy-start = (f32[2,64,512]{2,1,0:T(8,128)S(1)}, f32[2,64,512]{2,1,0:T(8,128)}, u32[]{:S(2)}) copy-start(f32[2,64,512]{2,1,0:T(8,128)} %gas_hbm.1) | copy-start | bytes 786436
  0.7 1.0 %copy-start.5 = (s32[2,8,128]{2,1,0:T(8,128)S(1)}, s32[2,8,128]{2,1,0:T(8,128)}, u32[]{:S(2)}) copy-start(s32[2,8,128]{2,1,0:T(8,128)} %slots_hbm.1) | copy-start | bytes 24580
  0.7 1.0 %copy-start.4 = (s32[9,2,8]{0,2,1:T(8,128)S(1)}, s32[9,2,8]{0,2,1:T(8,128)}, u32[]{:S(2)}) copy-start(s32[9,2,8]{0,2,1:T(8,128)} %param.11) | copy-start | bytes 1732
  0.7 1.0 %copy-start.3 = (f32[3,2,8,128]{3,2,1,0:T(8,128)S(1)}, f32[3,2,8,128]{3,2,1,0:T(8,128)}, u32[]{:S(2)}) copy-start(f32[3,2,8,128]{3,2,1,0:T(8,128)} %velocities_hbm.1) | copy-start | bytes 73732
  0.7 1.0 %copy-start.2 = (f32[3,2,8,128]{3,2,1,0:T(8,128)S(1)}, f32[3,2,8,128]{3,2,1,0:T(8,128)}, u32[]{:S(2)}) copy-start(f32[3,2,8,128]{3,2,1,0:T(8,128)} %positions_hbm.1) | copy-start | bytes 73732
  0.7 1.0 %copy-start.7 = (s32[2,8]{1,0:T(2,128)S(1)}, s32[2,8]{1,0:T(2,128)}, u32[]{:S(2)}) copy-start(s32[2,8]{1,0:T(2,128)} %owners_hbm.1) | copy-start | bytes 196
  0.7 1.0 %copy-start.6 = (s32[2,8]{1,0:T(2,128)S(1)}, s32[2,8]{1,0:T(2,128)}, u32[]{:S(2)}) copy-start(s32[2,8]{1,0:T(2,128)} %exits_hbm.1) | copy-start | bytes 196
  0.7 1.0 %copy-start.8 = (s32[1,8]{1,0:T(1,128)S(1)}, s32[1,8]{1,0:T(1,128)}, u32[]{:S(2)}) copy-start(s32[1,8]{1,0:T(1,128)} %inlets_hbm.1) | copy-start | bytes 100
  2.6 3.2 %collective-permute-start = (f32[64,128]{1,0:T(8,128)S(1)}, f32[64,128]{1,0:T(8,128)S(1)}, u32[]{:S(2)}, u32[]{:S(2)}) collective-permute-start(f32[64,128]{1,0:T(8,128)S(1)} %get-tuple-element.30), channel_id=1, source_target_pairs={{0,1},{1,0},{2,3},{3,2},{4,5},{5,4},{6,7},{7,6},{8,9},{9,8},{10,11... | collective-permute-start | bytes 98312 | tf_op jit(solution)/shard_map/ppermute | solution.py:784
  3.2 4.3 %collective-permute-start.1 = (f32[64,128]{1,0:T(8,128)S(1)}, f32[64,128]{1,0:T(8,128)S(1)}, u32[]{:S(2)}, u32[]{:S(2)}) collective-permute-start(f32[64,128]{1,0:T(8,128)S(1)} %get-tuple-element.31), channel_id=1, source_target_pairs={{0,3},{1,2},{2,1},{3,0},{4,7},{5,6},{6,5},{7,4},{8,11},{9,10},{10,... | collective-permute-start | bytes 98312 | tf_op jit(solution)/shard_map/ppermute | solution.py:784
  7.5 3.5 %collective-permute-start.3 = (f32[152,128]{1,0:T(8,128)S(1)}, f32[152,128]{1,0:T(8,128)S(1)}, u32[]{:S(2)}, u32[]{:S(2)}) collective-permute-start(f32[152,128]{1,0:T(8,128)S(1)} %merge.1.own_ref), channel_id=1, source_target_pairs={{0,1},{1,0},{2,3},{3,2},{4,8},{5,9},{6,10},{7,11},{8,4},{9,5},{10,... | collective-permute-start | bytes 233480 | tf_op jit(solution)/shard_map/ppermute | solution.py:369
  7.7 6.3 %collective-permute-start.2 = (f32[152,128]{1,0:T(8,128)S(1)}, f32[152,128]{1,0:T(8,128)S(1)}, u32[]{:S(2)}, u32[]{:S(2)}) collective-permute-start(f32[152,128]{1,0:T(8,128)S(1)} %merge.1.own_ref), channel_id=1, source_target_pairs={{0,4},{1,5},{2,6},{3,7},{4,0},{5,1},{6,2},{7,3},{8,12},{9,13},{10,... | collective-permute-start | bytes 233480 | tf_op jit(solution)/shard_map/ppermute | solution.py:369
  14.0 28.8 %collective-permute-start.8 = (f32[200,512]{1,0:T(8,128)S(1)}, f32[200,512]{1,0:T(8,128)S(1)}, u32[]{:S(2)}, u32[]{:S(2)}) collective-permute-start(f32[200,512]{1,0:T(8,128)S(1)} %get-tuple-element.44), channel_id=1, source_target_pairs={{0,4},{1,5},{2,6},{3,7},{4,0},{5,1},{6,2},{7,3},{8,12},{9,13},{10,... | collective-permute-start | bytes 1228808 | tf_op jit(solution)/shard_map/ppermute | solution.py:792
  16.4 26.4 %collective-permute-start.9 = (f32[200,512]{1,0:T(8,128)S(1)}, f32[200,512]{1,0:T(8,128)S(1)}, u32[]{:S(2)}, u32[]{:S(2)}) collective-permute-start(f32[200,512]{1,0:T(8,128)S(1)} %get-tuple-element.45), channel_id=1, source_target_pairs={{0,1},{1,0},{2,3},{3,2},{4,8},{5,9},{6,10},{7,11},{8,4},{9,5},{10,... | collective-permute-start | bytes 1228808 | tf_op jit(solution)/shard_map/ppermute | solution.py:792
  31.1 3.2 %collective-permute-start.5 = (f32[24,128]{1,0:T(8,128)S(1)}, f32[24,128]{1,0:T(8,128)S(1)}, u32[]{:S(2)}, u32[]{:S(2)}) collective-permute-start(f32[24,128]{1,0:T(8,128)S(1)} %get-tuple-element.41.shared_ref), channel_id=1, source_target_pairs={{0,3},{1,2},{2,1},{3,0},{4,7},{5,6},{6,5},{7,4},{8,11},{9,10},{10,... | collective-permute-start | bytes 36872 | tf_op jit(solution)/shard_map/ppermute | solution.py:369
  32.8 1.5 %collective-permute-start.4 = (f32[24,128]{1,0:T(8,128)S(1)}, f32[24,128]{1,0:T(8,128)S(1)}, u32[]{:S(2)}, u32[]{:S(2)}) collective-permute-start(f32[24,128]{1,0:T(8,128)S(1)} %get-tuple-element.41.shared_ref), channel_id=1, source_target_pairs={{0,1},{1,0},{2,3},{3,2},{4,5},{5,4},{6,7},{7,6},{8,9},{9,8},{10,11... | collective-permute-start | bytes 36872 | tf_op jit(solution)/shard_map/ppermute | solution.py:369
  34.3 7.3 %collective-permute-start.7 = (f32[120,128]{1,0:T(8,128)S(1)}, f32[120,128]{1,0:T(8,128)S(1)}, u32[]{:S(2)}, u32[]{:S(2)}) collective-permute-start(f32[120,128]{1,0:T(8,128)S(1)} %pad_maximum_fusion), channel_id=1, source_target_pairs={{0,28},{1,29},{2,30},{3,31},{4,8},{5,9},{6,10},{7,11},{8,4},{9,5},... | collective-permute-start | bytes 184328 | tf_op jit(solution)/shard_map/ppermute | solution.py:369
  37.9 4.9 %collective-permute-start.6 = (f32[120,128]{1,0:T(8,128)S(1)}, f32[120,128]{1,0:T(8,128)S(1)}, u32[]{:S(2)}, u32[]{:S(2)}) collective-permute-start(f32[120,128]{1,0:T(8,128)S(1)} %pad_maximum_fusion), channel_id=1, source_target_pairs={{0,4},{1,5},{2,6},{3,7},{4,0},{5,1},{6,2},{7,3},{8,12},{9,13},{10,... | collective-permute-start | bytes 184328 | tf_op jit(solution)/shard_map/ppermute | solution.py:369

commit v5 on v4

--- a/solution.py
+++ b/solution.py
@@ -111,9 +111,10 @@
     return [spread(features, c), spread(features, c + 1), jnp.concatenate(halves, axis=1)]
 
 
-def forces_row(tiles, r, columns, rows, wide, turned, pulled, nears, founds):
+def pulls_row(tiles, r, columns, source_rows, rows, wide, turned, pulled, nears, founds):
     ahead = len(nears) - 1
-    units = [(pair, kind, i) for pair in range(len(columns)) for kind in range(3) for i in range(3)]
+    count = len(source_rows)
+    units = [(pair, kind, i) for pair in range(len(columns)) for kind in range(3) for i in range(count)]
     blocks = wide // 4
     operands = [None] * len(columns)
 
@@ -127,7 +128,8 @@
             pltpu.matmul_push_rhs(operands[pair][kind], staged, 0)
         start = (c - 1) // 4
         after = start + 1 if start + 1 < blocks else 0
-        sources = jnp.concatenate([turned[r + i - 1, start], turned[r + i - 1, after]], axis=1)
+        row = source_rows[i]
+        sources = jnp.concatenate([turned(row)[start], turned(row)[after]], axis=1)
         pltpu.matmul_acc_lhs(nears[n % len(nears)], sources, load_staged_rhs=staged if i == 0 else None)
 
     def finish(n):
@@ -137,11 +139,11 @@
         high = weight.astype(bf16)
         low = (weight - high.astype(f32)).astype(bf16)
         pltpu.matmul_push_rhs(jnp.concatenate([high, low], axis=0), n % 2, 1)
-        row = r + i - 1
+        of_row = pulled(source_rows[i])
         if kind < 2:
-            pulls = pulled[row, c + kind]
+            pulls = of_row[c + kind]
         else:
-            pulls = jnp.concatenate([pulled[row, c - 1], pulled[row, c + 2]], axis=0)
+            pulls = jnp.concatenate([of_row[c - 1], of_row[c + 2]], axis=0)
         pulls = jnp.concatenate([pulls, pulls], axis=1)
         pltpu.matmul_acc_lhs(founds[2 * pair + (kind == 2)], pulls, load_staged_rhs=n % 2)
 
@@ -150,12 +152,18 @@
             begin(n)
         if n >= ahead:
             finish(n - ahead)
+    totals = []
+    for pair in range(len(columns)):
+        inner, outer = pltpu.matmul_pop(founds[2 * pair]), pltpu.matmul_pop(founds[2 * pair + 1])
+        totals.append(inner + jnp.concatenate([outer[0:16, 0:LANES], outer[16:32, LANES:]], axis=1))
+    return totals
+
+
+def forces_of(totals, tiles, r, columns, rows, wide):
     forces = []
     for pair, c in enumerate(columns):
-        inner, outer = pltpu.matmul_pop(founds[2 * pair]), pltpu.matmul_pop(founds[2 * pair + 1])
         for k, tile in enumerate(tiles[pair]):
-            part = slice(k * LANES, (k + 1) * LANES)
-            total = inner[:, part] + outer[16 * k : 16 * k + 16, part]
+            total = totals[pair][:, k * LANES : (k + 1) * LANES]
             first, second = total[0:8], total[8:16]
             moving = centred(tile, r, c + k, rows, wide) - damping * pltpu.roll(tile, 5, 0)
             forces.append((spring / cutoff_sq) * (moving * first[3:4, :] - first - second - pltpu.roll(second, 4, 0)))
@@ -186,8 +194,97 @@
     return start + r * cols + c - DEPTH
 
 
+def tiles_of_block(block, place, rows, cols):
+    wide = cols + 2 * DEPTH
+    flag_row = 6 * rows * wide
+    for r in range(rows):
+        for c in range(wide):
+            for d in range(6):
+                row = halo_rows(rows, cols, d, r, c)
+                place(r, c, d, block[row : row + 1])
+            row = flag_row + (rows if c < DEPTH else rows + 1 if c >= cols + DEPTH else r)
+            place(r, c, 6, block[row : row + 1])
+            place(r, c, 7, jnp.zeros((1, LANES), f32))
+
+
+def fill_row(tile_at, r, high, wide, turned_row, pulled_row):
+    for block in range(wide // 4):
+        near = []
+        for c in range(4 * block, 4 * block + 4):
+            places, moving = source_features(tile_at(c), r, c, high, wide)
+            near.append(places)
+            pulled_row[c] = moving
+        turned_row[block] = jnp.concatenate(near, axis=0).T.astype(bf16)
+
+
+def accumulators(wide):
+    return (
+        *[pltpu.ACC(0)((LANES, 2 * LANES), f32)] * NEARS,
+        *[pltpu.ACC(1)((held, 2 * LANES), f32) for _ in range(wide // 2 - 1) for held in (16, 32)],
+    )
+
+
+def emptied(refs):
+    for ref in refs:
+        pltpu.matmul_pop(ref)
+    return refs[:NEARS], refs[NEARS:]
+
+
+def own_kernel(own_ref, state_ref, turned_ref, pulled_ref, partial_ref, *, rows, cols):
+    wide = cols + 2 * DEPTH
+    high = rows + 2 * DEPTH
+    columns = list(range(1, wide - 1, 2))
+
+    def place(r, c, d, value):
+        state_ref[r, c, d : d + 1] = value
+
+    tiles_of_block(own_ref, place, rows, cols)
+
+    def one_row(r, carry):
+        fill_row(lambda c: state_ref[r, c], r + DEPTH, high, wide, turned_ref.at[r], pulled_ref.at[r])
+        return carry
+
+    lax.fori_loop(0, rows, one_row, 0)
+
+    def sums(*refs):
+        nears, founds = emptied(refs)
+
+        def one_sum(r, carry):
+            tiles = [[state_ref[r, c], state_ref[r, c + 1]] for c in columns]
+            totals = pulls_row(
+                tiles, r + DEPTH, columns, list(range(rows)), high, wide,
+                lambda row: turned_ref.at[row], lambda row: pulled_ref.at[row], nears, founds,
+            )
+            for pair, total in enumerate(totals):
+                partial_ref[r, pair] = total
+            return carry
+
+        lax.fori_loop(0, rows, one_sum, 0)
+
+    pl.run_scoped(sums, *accumulators(wide))
+
+
+def own_sums(own, rows, cols):
+    wide = cols + 2 * DEPTH
+    vmem = pl.BlockSpec(memory_space=pltpu.VMEM)
+    return pl.pallas_call(
+        functools.partial(own_kernel, rows=rows, cols=cols),
+        out_shape=(
+            jax.ShapeDtypeStruct((rows, wide, COMPS, LANES), f32),
+            jax.ShapeDtypeStruct((rows, wide // 4, LANES, LANES), bf16),
+            jax.ShapeDtypeStruct((rows, wide, 16, LANES), bf16),
+            jax.ShapeDtypeStruct((rows, wide // 2 - 1, 16, 2 * LANES), f32),
+        ),
+        in_specs=[vmem],
+        out_specs=(vmem,) * 4,
+        cost_estimate=pl.CostEstimate(flops=4 * 10**9, bytes_accessed=4096, transcendentals=0),
+        compiler_params=pltpu.CompilerParams(vmem_limit_bytes=8 * MIB),
+        name="own_sums",
+    )(own)
+
+
 def particles_kernel(
-    ints_ref, own_ref, first_ref, second_ref,
+    ints_ref, first_ref, second_ref, own_ref, own_turned, own_pulled, partial_ref,
     settled_ref, leaving_ref, state, turned, pulled, begun, blocks,
     *, rows, cols,
 ):
@@ -196,44 +293,35 @@
     left, right, below, above, even, _ = position()
     one, two = first_ref[...], second_ref[...]
     blocks[0] = jnp.where(below, jnp.where(even, two, one), 0.0)
-    blocks[1] = own_ref[...]
-    blocks[2] = jnp.where(above, jnp.where(even, one, two), 0.0)
-    flag_row = 6 * rows * wide
-    for block in range(3):
-        for r in range(rows):
-            for c in range(wide):
-                for d in range(6):
-                    row = halo_rows(rows, cols, d, r, c)
-                    state[block * rows + r, c, d : d + 1] = blocks[block, row : row + 1]
-                row = flag_row + (rows if c < DEPTH else rows + 1 if c >= cols + DEPTH else r)
-                state[block * rows + r, c, 6:7] = blocks[block, row : row + 1]
-                state[block * rows + r, c, 7:8] = jnp.zeros((1, LANES), f32)
-
-    def fill(source, first, last):
-        def one_row(r, carry):
-            for block in range(wide // 4):
-                near = []
-                for c in range(4 * block, 4 * block + 4):
-                    places, moving = source_features(source[r, c], r, c, high, wide)
-                    near.append(places)
-                    pulled[r, c] = moving
-                turned[r, block] = jnp.concatenate(near, axis=0).T.astype(bf16)
-            return carry
-
-        lax.fori_loop(first, last, one_row, 0)
-
-    def substeps(*accumulators):
-        nears, founds = accumulators[:NEARS], accumulators[NEARS:]
-        for accumulator in accumulators:
-            pltpu.matmul_pop(accumulator)
-        fill(state, 0, high)
-
-        def first_step(r, carry):
+    blocks[1] = jnp.where(above, jnp.where(even, one, two), 0.0)
+    for half, start in ((0, 0), (1, rows + DEPTH)):
+
+        def place(r, c, d, value, start=start):
+            state[start + r, c, d : d + 1] = value
+
+        tiles_of_block(blocks.at[half], place, rows, cols)
+
+    def far_row(n, carry):
+        r = n + jnp.where(n >= DEPTH, rows, 0)
+        fill_row(lambda c: state[r, c], r, high, wide, turned.at[r], pulled.at[r])
+        return carry
+
+    lax.fori_loop(0, 2 * DEPTH, far_row, 0)
+    for r in range(rows):
+        state[DEPTH + r] = own_ref[r]
+        turned[DEPTH + r] = own_turned[r]
+        pulled[DEPTH + r] = own_pulled[r]
+
+    def substeps(*refs):
+        nears, founds = emptied(refs)
+        sources = dict(turned=lambda row: turned.at[row], pulled=lambda row: pulled.at[row], nears=nears, founds=founds)
+        columns = list(range(1, wide - 1, 2))
+
+        def begin_row(r, totals):
+            tiles = [[state[r, c], state[r, c + 1]] for c in columns]
+            forces = forces_of(totals, tiles, r, columns, high, wide)
             begun[r, 0] = jnp.zeros((COMPS, LANES), f32)
             begun[r, wide - 1] = jnp.zeros((COMPS, LANES), f32)
-            columns = list(range(1, wide - 1, 2))
-            tiles = [[state[r, c], state[r, c + 1]] for c in columns]
-            forces = forces_row(tiles, r, columns, high, wide, turned, pulled, nears, founds)
             for c in range(1, wide - 1):
                 inside = ((r >= DEPTH) | below) & ((r < rows + DEPTH) | above)
                 if c < DEPTH:
@@ -241,26 +329,41 @@
                 if c >= cols + DEPTH:
                     inside = inside & right
                 begun[r, c] = jnp.where(inside, stepped(tiles[(c - 1) // 2][(c - 1) % 2], forces[c - 1]), 0.0)
+
+        def outer_step(n, carry):
+            r = 1 + n * (rows + 1)
+            tiles = [[state[r, c], state[r, c + 1]] for c in columns]
+            begin_row(r, pulls_row(tiles, r, columns, [r - 1, r, r + 1], high, wide, **sources))
             return carry
 
-        lax.fori_loop(1, high - 1, first_step, 0)
-        fill(begun, 1, high - 1)
+        def inner_step(n, carry):
+            r = DEPTH + n * (rows - 1)
+            tiles = [[state[r, c], state[r, c + 1]] for c in columns]
+            totals = pulls_row(tiles, r, columns, [1 + n * (rows + 1)], high, wide, **sources)
+            begin_row(r, [total + partial_ref[n * (rows - 1), pair] for pair, total in enumerate(totals)])
+            return carry
+
+        lax.fori_loop(0, 2, inner_step, 0)
+        lax.fori_loop(0, 2, outer_step, 0)
+
+        def begun_row(r, carry):
+            fill_row(lambda c: begun[r, c], r, high, wide, turned.at[r], pulled.at[r])
+            return carry
+
+        lax.fori_loop(1, high - 1, begun_row, 0)
 
         def second_step(r, carry):
             columns = list(range(DEPTH, DEPTH + cols, 2))
             tiles = [[begun[r, c], begun[r, c + 1]] for c in columns]
-            forces = forces_row(tiles, r, columns, high, wide, turned, pulled, nears, founds)
+            totals = pulls_row(tiles, r, columns, [r - 1, r, r + 1], high, wide, **sources)
+            forces = forces_of(totals, tiles, r, columns, high, wide)
             for c in range(cols):
                 settled_ref[r - DEPTH, c] = stepped(tiles[c // 2][c % 2], forces[c])
             return carry
 
         lax.fori_loop(DEPTH, DEPTH + rows, second_step, 0)
 
-    pl.run_scoped(
-        substeps,
-        *[pltpu.ACC(0)((LANES, 2 * LANES), f32)] * NEARS,
-        *[pltpu.ACC(1)((held, 2 * LANES), f32) for _ in range(wide // 2 - 1) for held in (16, 32)],
-    )
+    pl.run_scoped(substeps, *accumulators(wide))
 
     leaving_ref[...] = jnp.zeros_like(leaving_ref)
     count = jnp.int32(0)
@@ -275,8 +378,9 @@
         count = count + flag
 
 
-def particles(ints, own, first, second, rows, cols):
-    wide, high = cols + 2 * DEPTH, rows + 2 * DEPTH
+def particles(ints, first, second, own):
+    rows, wide = own[0].shape[:2]
+    cols, high = wide - 2 * DEPTH, rows + 2 * DEPTH
     smem = pl.BlockSpec(memory_space=pltpu.SMEM)
     vmem = pl.BlockSpec(memory_space=pltpu.VMEM)
     return pl.pallas_call(
@@ -285,18 +389,19 @@
             jax.ShapeDtypeStruct((rows, cols, COMPS, LANES), f32),
             jax.ShapeDtypeStruct((6, cols, LANES), f32),
         ),
-        in_specs=[smem, vmem, vmem, vmem],
+        in_specs=[smem] + [vmem] * 6,
         out_specs=(vmem, vmem),
         scratch_shapes=[
             pltpu.VMEM((high, wide, COMPS, LANES), f32),
             pltpu.VMEM((high, wide // 4, LANES, LANES), bf16),
             pltpu.VMEM((high, wide, 16, LANES), bf16),
             pltpu.VMEM((high, wide, COMPS, LANES), f32),
-            pltpu.VMEM((3, *own.shape), f32),
+            pltpu.VMEM((2, *first.shape), f32),
         ],
+        cost_estimate=pl.CostEstimate(flops=10**10, bytes_accessed=4096, transcendentals=0),
         compiler_params=pltpu.CompilerParams(vmem_limit_bytes=12 * MIB),
         name="particles",
-    )(ints, own, first, second)
+    )(ints, first, second, *own)
 
 
 def deposit_kernel(ints_ref, settled_ref, slots_ref, blocks_ref, own_ref, shared_ref):
@@ -389,39 +494,28 @@
 
 
 def pack_kernel(
-    zeros_ref, exits_hbm, owners_hbm, inlets_hbm, positions_hbm, velocities_hbm, contacts_hbm, slots_hbm, gas_hbm, diagonal_hbm,
-    first_ref, second_ref, flags_ref, ints_ref, slots_ref, state_ref, cells_ref,
-    sides, wide_flags, contacts_ref, exits_ref, owners_ref, inlets_ref, arrived,
+    zeros_ref, exits_ref, owners_ref, inlets_ref, positions_ref, velocities_ref, contacts_ref, slots_in, gas_ref,
+    diagonal_ref, first_ref, second_ref, flags_ref, ints_ref, slots_ref, state_ref, cells_ref, sides, wide_flags, small,
 ):
     rows, cols = state_ref.shape[1:3]
     _, levels, across, along = cells_ref.shape
-    pairs = (
-        (positions_hbm, state_ref.at[0:3]),
-        (velocities_hbm, state_ref.at[3:6]),
-        (gas_hbm, cells_ref.at[0]),
-        (diagonal_hbm, cells_ref.at[1]),
-        (contacts_hbm, contacts_ref),
-        (exits_hbm, exits_ref),
-        (owners_hbm, owners_ref),
-        (inlets_hbm, inlets_ref),
-        (slots_hbm, slots_ref),
-    )
-    copies = [pltpu.make_async_copy(source, target, arrived.at[n]) for n, (source, target) in enumerate(pairs)]
-    for copy in copies:
-        copy.start()
+    lane = lax.broadcasted_iota(i32, (1, LANES), 1)
     sides[...] = jnp.zeros_like(sides) + zeros_ref[0:1]
     wide_flags[...] = jnp.zeros_like(wide_flags)
-    for copy in copies:
-        copy.wait()
-    lane = lax.broadcasted_iota(i32, (1, LANES), 1)
+    small[...] = jnp.zeros_like(small)
+    state_ref[0:3] = positions_ref[...]
+    state_ref[3:6] = velocities_ref[...]
+    cells_ref[0] = gas_ref[...]
+    cells_ref[1] = diagonal_ref[...]
+    slots_ref[...] = slots_in[...]
+    small[0:rows, 0:cols] = exits_ref[...]
+    small[rows : 2 * rows, 0:cols] = owners_ref[...]
+    small[2 * rows : 2 * rows + 1, 0:cols] = inlets_ref[...]
     ints = jnp.zeros((1, LANES), i32)
     for r in range(rows):
-        for c in range(cols):
-            ints = jnp.where(lane == EXITS + r * cols + c, exits_ref[r, c], ints)
-            ints = jnp.where(lane == OWNERS + r * cols + c, owners_ref[r, c], ints)
-    for c in range(cols):
-        ints = jnp.where(lane == INLETS + c, inlets_ref[0, c], ints)
-    ints_ref[...] = ints
+        ints = ints + pltpu.roll(small[r : r + 1], EXITS + r * cols, 1)
+        ints = ints + pltpu.roll(small[rows + r : rows + r + 1], OWNERS + r * cols, 1)
+    ints_ref[...] = ints + pltpu.roll(small[2 * rows : 2 * rows + 1], INLETS, 1)
     wide_flags[:, :, 0 : contacts_ref.shape[2]] = contacts_ref[...].astype(f32)
     flags = []
     for r in range(rows):
@@ -468,16 +562,12 @@
             jax.ShapeDtypeStruct((6, rows, cols, LANES), f32),
             jax.ShapeDtypeStruct((2, levels, across, along), f32),
         ),
-        in_specs=[vmem] + [pl.BlockSpec(memory_space=pl.ANY)] * 9,
+        in_specs=[vmem] * 10,
         out_specs=(vmem,) * 7,
         scratch_shapes=[
             pltpu.VMEM((2, *side.shape), f32),
             pltpu.VMEM((rows, cols, LANES), f32),
-            pltpu.VMEM(contacts.shape, i32),
-            pltpu.SMEM(exits.shape, i32),
-            pltpu.SMEM(owners.shape, i32),
-            pltpu.SMEM(inlets.shape, i32),
-            pltpu.SemaphoreType.DMA((9,)),
+            pltpu.VMEM((8, LANES), i32),
         ],
         compiler_params=pltpu.CompilerParams(vmem_limit_bytes=8 * MIB),
         name="pack",
@@ -718,11 +808,31 @@
 
 
 def results_kernel(
-    ints_ref, dots_ref, rhs_ref, near_ref, far_ref, scaling_ref, settled_ref,
-    height_a, height_b, around_ref, positions_ref, velocities_ref, pressure_ref, residual_ref,
+    ints_ref, dots_ref, rhs_ref, near_ref, far_ref, scaling_ref, settled_ref, height_a, height_b,
+    positions_out, velocities_out, pressure_out, residual_out, positions, velocities, pressure, residual, sent,
 ):
     rows, cols = settled_ref.shape[:2]
-    _, _, below, _, even, _ = position()
+    levels = rhs_ref.shape[0]
+    even = position()[4]
+    for r in range(1, rows):
+        for c in range(cols):
+            kept = jnp.where(ints_ref[0, EXITS + r * cols + c] > 0, 0.0, settled_ref[r, c])
+            for d in range(3):
+                positions[d, r, c : c + 1] = kept[d : d + 1]
+                velocities[d, r, c : c + 1] = kept[d + 3 : d + 4]
+    start = 3 * ROWS_OUT
+    for d in range(6):
+        block = slice(start + d * cols, start + (d + 1) * cols)
+        tiles = jnp.where(even, height_b[block], height_a[block])
+        target = positions if d < 3 else velocities
+        for k in range(cols):
+            target[d % 3, 0, pl.ds(ints_ref[0, INLETS + k], 1)] = tiles[k : k + 1]
+    copies = [
+        pltpu.make_async_copy(positions, positions_out, sent.at[0]),
+        pltpu.make_async_copy(velocities, velocities_out, sent.at[1]),
+    ]
+    for copy in copies:
+        copy.start()
     totals = jnp.sum(dots_ref[...], axis=0, keepdims=True)
     g00, g01, g11, g12 = [totals[:, k : k + 1] for k in range(4)]
     ratio = g01 / g00
@@ -735,27 +845,19 @@
     later = renewed / curvature
     one = alpha + later * (1.0 - alpha + beta)
     two = later * alpha
-    for z in range(rhs_ref.shape[0]):
-        m = scaling_ref[z]
+    for z in range(levels):
         rhs, near = rhs_ref[z], near_ref[z]
-        pressure_ref[z] = m * (one * rhs + two * near)
-        residual_ref[z] = (1.0 - one) * rhs + (one - two) * near + two * far_ref[z]
-    for r in range(1, rows):
-        for c in range(cols):
-            kept = jnp.where(ints_ref[0, EXITS + r * cols + c] > 0, 0.0, settled_ref[r, c])
-            for d in range(3):
-                positions_ref[d, r, c : c + 1] = kept[d : d + 1]
-                velocities_ref[d, r, c : c + 1] = kept[d + 3 : d + 4]
-    start = 3 * ROWS_OUT
-    for d in range(6):
-        block = slice(start + d * cols, start + (d + 1) * cols)
-        tiles = jnp.where(even, height_b[block], height_a[block])
-        target = positions_ref if d < 3 else velocities_ref
-        for k in range(cols):
-            target[d % 3, 0, pl.ds(ints_ref[0, INLETS + k], 1)] = tiles[k : k + 1]
-
-
-def results_of(ints, dots, rhs, near, far, scaling, settled, height, around):
+        pressure[z] = scaling_ref[z] * (one * rhs + two * near)
+        residual[z] = (1.0 - one) * rhs + (one - two) * near + two * far_ref[z]
+        for n, (source, target) in enumerate(((pressure, pressure_out), (residual, residual_out))):
+            copy = pltpu.make_async_copy(source.at[z], target.at[z], sent.at[2 + 2 * z + n])
+            copy.start()
+            copies.append(copy)
+    for copy in copies:
+        copy.wait()
+
+
+def results_of(ints, dots, rhs, near, far, scaling, settled, height):
     rows, cols = settled.shape[:2]
     smem = pl.BlockSpec(memory_space=pltpu.SMEM)
     vmem = pl.BlockSpec(memory_space=pltpu.VMEM)
@@ -764,11 +866,16 @@
     return pl.pallas_call(
         results_kernel,
         out_shape=(particle, particle, field, field),
-        in_specs=[smem] + [vmem] * 9,
-        out_specs=(vmem,) * 4,
+        in_specs=[smem] + [vmem] * 8,
+        out_specs=(pl.BlockSpec(memory_space=pl.ANY),) * 4,
+        scratch_shapes=[
+            *[pltpu.VMEM(particle.shape, f32)] * 2,
+            *[pltpu.VMEM(field.shape, f32)] * 2,
+            pltpu.SemaphoreType.DMA((2 + 2 * rhs.shape[0],)),
+        ],
         compiler_params=pltpu.CompilerParams(vmem_limit_bytes=8 * MIB),
         name="results",
-    )(ints, dots, rhs, near, far, scaling, settled, *height, around)
+    )(ints, dots, rhs, near, far, scaling, settled, *height)
 
 
 def on_device(
@@ -786,13 +893,14 @@
     ]
     window = merged(state, flags, lines)
     beside = exchanged(window, "height", False)
+    own_parts = own_sums(window, *state.shape[1:3])
     scaling, blocks, *faces = faces_of(cells, lines)
     faces, beside = lax.optimization_barrier((faces, beside))
     faces = [
         lax.ppermute(value, ("height", "cols"), matching(heights, groups, "height", odd, False))
         for value, odd in zip(faces, (False, True))
     ]
-    settled, leaving = particles(ints, window, *beside, *state.shape[1:3])
+    settled, leaving = particles(ints, *beside, own_parts)
     own, shared = deposits(ints, settled, slots, blocks)
     near = exchanged(shared, "cols", True)
     parcel = jnp.concatenate([shared, *near, leaving.reshape(-1, LANES)], axis=0)
@@ -801,7 +909,7 @@
         own, shared, near, parcels, cells, scaling, lines, faces, heights * groups
     )
     dots = lax.all_to_all(dots, ("height", "cols"), 0, 0, tiled=True)
-    return results_of(ints, dots, rhs, first, second, scaling, settled, parcels, leaving)
+    return results_of(ints, dots, rhs, first, second, scaling, settled, parcels)
 
 
 def solution(mesh):

time: 56.2 us -> 53 us (0.943)
  waiting for transfers between devices: 11 us -> 8.02 us
    pallas_call x0 -> x1, Pallas kernels: none -> 3.26 us  [own_sums(): pl.pallas_call(functools.partial(own_kernel, rows=rows, cols=cols), out_s...]
    ppermute x6, waiting for transfers between devices: 9.31 us -> 6.35 us  [exchanged(): lax.ppermute(value, ('height', 'cols'), matching(heights, groups, axis, o...]
    pallas_call x1, Pallas kernels: 13.7 us -> 11.3 us  [particles(): pl.pallas_call(functools.partial(particles_kernel, rows=rows, cols=cols),...]
    pallas_call x1, Pallas kernels: 0.92 us -> 0.17 us  [packed(): pl.pallas_call(pack_kernel, out_shape=(side, side, jax.ShapeDtypeStruct((...]
  transfers between devices with their start and end apart: 10 -> 10, of which waited for: 5 -> 4; matrix products, arithmetic and copies ran while one was open for 0% -> 0% of each run, Pallas kernels for 27% -> 30%
where the time goes in v5:
time: 53 us; the launch traced here: 52.8 us
  Pallas kernels  18.7 us (35%)
  starting transfers between devices  13.8 us (26%)
  blocking collectives  10.5 us (20%)
  waiting for transfers between devices  8.02 us (15%)
  local copies, waits for them, and re-layouts  0.96 us (2%)
  between operations  0.8 us (2%)
    pallas_call x1, Pallas kernels, particles(): pl.pallas_call(functools.partial(particles_kernel, rows=rows, cols=cols),...  11.3 us
    all_to_all x1, blocking collectives, on_device(): dots = lax.all_to_all(dots, ('height', 'cols'), 0, 0, tiled=True)  10.5 us
    ppermute x6, starting transfers between devices, exchanged(): lax.ppermute(value, ('height', 'cols'), matching(heights, groups, axis, o...  8.54 us
    ppermute x6, waiting for transfers between devices, exchanged(): lax.ppermute(value, ('height', 'cols'), matching(heights, groups, axis, o...  6.35 us
    pallas_call x1, Pallas kernels, own_sums(): pl.pallas_call(functools.partial(own_kernel, rows=rows, cols=cols), out_s...  3.26 us
    ppermute x2, starting transfers between devices, on_device(): lax.ppermute(value, ('height', 'cols'), matching(heights, groups, 'cols',...  3.13 us
    ppermute x2, starting transfers between devices, on_device(): lax.ppermute(value, ('height', 'cols'), matching(heights, groups, 'height...  2.14 us
    pallas_call x1, Pallas kernels, results_of(): pl.pallas_call(results_kernel, out_shape=(particle, particle, field, fiel...  1.69 us
  transfers between devices with their start and end apart: 10, of which 4 were waited for; matrix products, arithmetic and copies ran while one was open for 0% of the time, Pallas kernels for 30%

profile of v5, /device:TPU:0, one launch (start us, length us, event | category | flops | bytes accessed | tf_op | source)
XLA Modules:
  0.0 52.8 jit_solution(7724052389004192031)
XLA Ops:
  0.6 0.0 copy-start.1
  0.6 0.0 copy-start
  0.7 0.0 copy-start.5
  0.7 0.0 copy-start.4
  0.7 0.0 copy-start.3
  0.7 0.0 copy-start.2
  0.7 0.0 copy-start.7
  0.7 0.0 copy-start.6
  0.7 0.0 copy-start.8
  0.7 0.8 %copy-done.1 = f32[2,64,512]{2,1,0:T(8,128)S(1)} copy-done((f32[2,64,512]{2,1,0:T(8,128)S(1)}, f32[2,64,512]{2,1,0:T(8,128)}, u32[]{:S(2)}) %copy-start.1) | copy-done | bytes 262168
  1.6 0.1 copy-done
  1.7 0.0 copy-done.5
  1.7 0.0 copy-done.4
  1.7 0.0 copy-done.3
  1.7 0.0 copy-done.2
  1.7 0.0 copy-done.7
  1.7 0.0 copy-done.6
  1.7 0.0 copy-done.8
  1.7 0.2 pack.1
  1.9 0.5 collective-permute-start
  2.4 2.6 %collective-permute-start.1 = (f32[64,128]{1,0:T(8,128)S(1)}, f32[64,128]{1,0:T(8,128)S(1)}, u32[]{:S(2)}, u32[]{:S(2)}) collective-permute-start(f32[64,128]{1,0:T(8,128)S(1)} %get-tuple-element.34), channel_id=1, source_target_pairs={{0,3},{1,2},{2,1},{3,0},{4,7},{5,6},{6,5},{7,4},{8,11},{9,10},{10,... | collective-permute-start | bytes 98312 | tf_op jit(solution)/shard_map/ppermute | solution.py:891
  5.0 0.0 collective-permute-done.line_a
  5.0 1.7 %collective-permute-done.1.line_b = f32[64,128]{1,0:T(8,128)S(1)} collective-permute-done((f32[64,128]{1,0:T(8,128)S(1)}, f32[64,128]{1,0:T(8,128)S(1)}, u32[]{:S(2)}, u32[]{:S(2)}) %collective-permute-start.1) | collective-permute-done | bytes 32800 | tf_op jit(solution)/shard_map/ppermute | solution.py:891
  6.7 0.2 collective-permute-start.3
  6.9 3.0 %collective-permute-start.2 = (f32[152,128]{1,0:T(8,128)S(1)}, f32[152,128]{1,0:T(8,128)S(1)}, u32[]{:S(2)}, u32[]{:S(2)}) collective-permute-start(f32[152,128]{1,0:T(8,128)S(1)} %merge.1.own_ref), channel_id=1, source_target_pairs={{0,4},{1,5},{2,6},{3,7},{4,0},{5,1},{6,2},{7,3},{8,12},{9,13},{10,... | collective-permute-start | bytes 233480 | tf_op jit(solution)/shard_map/ppermute | solution.py:474
  9.9 3.3 %own_sums.1 = (f32[2,12,8,128]{3,2,1,0:T(8,128)S(1)}, bf16[2,3,128,128]{3,2,1,0:T(8,128)(2,1)S(1)}, bf16[2,12,16,128]{3,2,1,0:T(8,128)(2,1)S(1)}, f32[2,5,16,256]{3,2,1,0:T(8,128)S(1)}) custom-call(f32[152,128]{1,0:T(8,128)S(1)} %merge.1.own_ref), custom_call_target="tpu_custom_call" | custom-call | flops 4000000000 | bytes 4096 | tf_op jit(solution)/shard_map/own_sums/pallas_call | solution.py:270
  13.2 0.3 faces.1
  13.5 0.0 collective-permute-done.3.second_ref
  13.5 0.0 collective-permute-done.2.first_ref
  13.5 2.1 %collective-permute-start.8 = (f32[200,512]{1,0:T(8,128)S(1)}, f32[200,512]{1,0:T(8,128)S(1)}, u32[]{:S(2)}, u32[]{:S(2)}) collective-permute-start(f32[200,512]{1,0:T(8,128)S(1)} %get-tuple-element.52), channel_id=1, source_target_pairs={{0,4},{1,5},{2,6},{3,7},{4,0},{5,1},{6,2},{7,3},{8,12},{9,13},{10,... | collective-permute-start | bytes 1228808 | tf_op jit(solution)/shard_map/ppermute | solution.py:900
  15.6 0.0 collective-permute-start.9
  15.6 11.3 %particles.1 = (f32[2,8,8,128]{3,2,1,0:T(8,128)S(1)}, f32[6,8,128]{2,1,0:T(8,128)S(1)}) custom-call(s32[1,128]{1,0:T(1,128)S(1)} %get-tuple-element.31.ints_ref, f32[152,128]{1,0:T(8,128)S(1)} %collective-permute-done.2.first_ref, f32[152,128]{1,0:T(8,128)S(1)} %collective-permute-done.3.second_ref, f32[2,12,8,128]{3,2,1,0:T(8,128)S(1)} %get-tuple-element.41.own_ref, ...), custom_call_target="tpu_custom_call" | custom-call | flops 10000000000 | bytes 4096 | tf_op jit(solution)/shard_map/particles/pallas_call | solution.py:386
  26.9 0.9 %deposits.1 = (f32[16,128]{1,0:T(8,128)S(1)}, f32[24,128]{1,0:T(8,128)S(1)}) custom-call(s32[1,128]{1,0:T(1,128)S(1)} %get-tuple-element.31.ints_ref, f32[2,8,8,128]{3,2,1,0:T(8,128)S(1)} %get-tuple-element.45.settled_ref, s32[2,8,128]{2,1,0:T(8,128)S(1)} %get-tuple-element.46.slots_ref, f32[4,128,128]{2,1,0:T(8,128)S(1)} %get-tuple-element.47.blocks_ref), custom_call_target="tpu_custom_call" | custom-call | tf_op jit(solution)/shard_map/deposits/pallas_call | solution.py:433
  27.9 1.7 %collective-permute-start.5 = (f32[24,128]{1,0:T(8,128)S(1)}, f32[24,128]{1,0:T(8,128)S(1)}, u32[]{:S(2)}, u32[]{:S(2)}) collective-permute-start(f32[24,128]{1,0:T(8,128)S(1)} %get-tuple-element.49.shared_ref), channel_id=1, source_target_pairs={{0,3},{1,2},{2,1},{3,0},{4,7},{5,6},{6,5},{7,4},{8,11},{9,10},{10,... | collective-permute-start | bytes 36872 | tf_op jit(solution)/shard_map/ppermute | solution.py:474
  29.6 0.0 collective-permute-start.4
  29.6 1.5 %collective-permute-done.5.side_b = f32[24,128]{1,0:T(8,128)S(1)} collective-permute-done((f32[24,128]{1,0:T(8,128)S(1)}, f32[24,128]{1,0:T(8,128)S(1)}, u32[]{:S(2)}, u32[]{:S(2)}) %collective-permute-start.5) | collective-permute-done | bytes 12320 | tf_op jit(solution)/shard_map/ppermute | solution.py:474
  31.1 0.0 collective-permute-done.4.side_a
  31.1 3.6 %collective-permute-start.7 = (f32[120,128]{1,0:T(8,128)S(1)}, f32[120,128]{1,0:T(8,128)S(1)}, u32[]{:S(2)}, u32[]{:S(2)}) collective-permute-start(f32[120,128]{1,0:T(8,128)S(1)} %pad_maximum_fusion), channel_id=1, source_target_pairs={{0,28},{1,29},{2,30},{3,31},{4,8},{5,9},{6,10},{7,11},{8,4},{9,5},... | collective-permute-start | bytes 184328 | tf_op jit(solution)/shard_map/ppermute | solution.py:474
  34.7 0.0 collective-permute-start.6
  34.7 3.6 %collective-permute-done.7.height_b = f32[120,128]{1,0:T(8,128)S(1)} collective-permute-done((f32[120,128]{1,0:T(8,128)S(1)}, f32[120,128]{1,0:T(8,128)S(1)}, u32[]{:S(2)}, u32[]{:S(2)}) %collective-permute-start.7) | collective-permute-done | bytes 61472 | tf_op jit(solution)/shard_map/ppermute | solution.py:474
  38.3 1.2 %collective-permute-done.6.height_a = f32[120,128]{1,0:T(8,128)S(1)} collective-permute-done((f32[120,128]{1,0:T(8,128)S(1)}, f32[120,128]{1,0:T(8,128)S(1)}, u32[]{:S(2)}, u32[]{:S(2)}) %collective-permute-start.6) | collective-permute-done | bytes 61472 | tf_op jit(solution)/shard_map/ppermute | solution.py:474
  39.6 0.0 collective-permute-done.8.face_a
  39.6 0.0 collective-permute-done.9.face_b
  39.6 1.0 %right_side.1 = (f32[2,64,512]{2,1,0:T(8,128)S(1)}, f32[2,64,512]{2,1,0:T(8,128)S(1)}, f32[2,64,512]{2,1,0:T(8,128)S(1)}, f32[32,128]{1,0:T(8,128)S(1)}) custom-call(f32[16,128]{1,0:T(8,128)S(1)} %get-tuple-element.48.own_ref, f32[24,128]{1,0:T(8,128)S(1)} %get-tuple-element.49.shared_ref, f32[24,128]{1,0:T(8,128)S(1)} %collective-permute-done.4.side_a, ...), custom_call_target="tpu_custom_call" | custom-call | tf_op jit(solution)/shard_map/right_side/pallas_call | solution.py:799
  40.6 10.5 %all_to_all.11 = f32[32,1,128]{2,1,0:T(1,128)S(1)} all-to-all(f32[32,1,128]{2,1,0:T(1,128)S(1)} %bitcast.8), channel_id=1, replica_groups=mesh['height'=8,'cols'=4] {'height','cols'}, dimensions={0} | all-to-all | bytes 32768 | tf_op jit(solution)/shard_map/all_to_all | solution.py:911
  51.1 1.7 %results.1 = (f32[3,2,8,128]{3,2,1,0:T(8,128)}, f32[3,2,8,128]{3,2,1,0:T(8,128)}, f32[2,64,512]{2,1,0:T(8,128)}, f32[2,64,512]{2,1,0:T(8,128)}) custom-call(s32[1,128]{1,0:T(1,128)S(1)} %get-tuple-element.31.ints_ref, f32[32,128]{1,0:T(8,128)S(1)} %bitcast.6, f32[2,64,512]{2,1,0:T(8,128)S(1)} %get-tuple-element.55.rhs_ref, ...), custom_call_target="tpu_custom_call" | custom-call | tf_op jit(solution)/shard_map/results/pallas_call | solution.py:866
  (3 shorter events, 0.0 us)
Async XLA Ops:
  0.6 1.0 %copy-start.1 = (f32[2,64,512]{2,1,0:T(8,128)S(1)}, f32[2,64,512]{2,1,0:T(8,128)}, u32[]{:S(2)}) copy-start(f32[2,64,512]{2,1,0:T(8,128)} %diagonal_ref.1) | copy-start | bytes 786436
  0.6 1.0 %copy-start = (f32[2,64,512]{2,1,0:T(8,128)S(1)}, f32[2,64,512]{2,1,0:T(8,128)}, u32[]{:S(2)}) copy-start(f32[2,64,512]{2,1,0:T(8,128)} %gas_ref.1) | copy-start | bytes 786436
  0.7 1.0 %copy-start.5 = (s32[2,8,128]{2,1,0:T(8,128)S(1)}, s32[2,8,128]{2,1,0:T(8,128)}, u32[]{:S(2)}) copy-start(s32[2,8,128]{2,1,0:T(8,128)} %slots_in.1) | copy-start | bytes 24580
  0.7 1.0 %copy-start.4 = (s32[9,2,8]{0,2,1:T(8,128)S(1)}, s32[9,2,8]{0,2,1:T(8,128)}, u32[]{:S(2)}) copy-start(s32[9,2,8]{0,2,1:T(8,128)} %param.11) | copy-start | bytes 1732
  0.7 1.0 %copy-start.3 = (f32[3,2,8,128]{3,2,1,0:T(8,128)S(1)}, f32[3,2,8,128]{3,2,1,0:T(8,128)}, u32[]{:S(2)}) copy-start(f32[3,2,8,128]{3,2,1,0:T(8,128)} %velocities_ref.1) | copy-start | bytes 73732
  0.7 1.0 %copy-start.2 = (f32[3,2,8,128]{3,2,1,0:T(8,128)S(1)}, f32[3,2,8,128]{3,2,1,0:T(8,128)}, u32[]{:S(2)}) copy-start(f32[3,2,8,128]{3,2,1,0:T(8,128)} %positions_ref.1) | copy-start | bytes 73732
  0.7 1.0 %copy-start.7 = (s32[2,8]{1,0:T(2,128)S(1)}, s32[2,8]{1,0:T(2,128)}, u32[]{:S(2)}) copy-start(s32[2,8]{1,0:T(2,128)} %owners_ref.1) | copy-start | bytes 196
  0.7 1.0 %copy-start.6 = (s32[2,8]{1,0:T(2,128)S(1)}, s32[2,8]{1,0:T(2,128)}, u32[]{:S(2)}) copy-start(s32[2,8]{1,0:T(2,128)} %exits_ref.1) | copy-start | bytes 196
  0.7 1.0 %copy-start.8 = (s32[1,8]{1,0:T(1,128)S(1)}, s32[1,8]{1,0:T(1,128)}, u32[]{:S(2)}) copy-start(s32[1,8]{1,0:T(1,128)} %inlets_ref.1) | copy-start | bytes 100
  1.9 3.1 %collective-permute-start = (f32[64,128]{1,0:T(8,128)S(1)}, f32[64,128]{1,0:T(8,128)S(1)}, u32[]{:S(2)}, u32[]{:S(2)}) collective-permute-start(f32[64,128]{1,0:T(8,128)S(1)} %get-tuple-element.33), channel_id=1, source_target_pairs={{0,1},{1,0},{2,3},{3,2},{4,5},{5,4},{6,7},{7,6},{8,9},{9,8},{10,11... | collective-permute-start | bytes 98312 | tf_op jit(solution)/shard_map/ppermute | solution.py:891
  2.4 4.3 %collective-permute-start.1 = (f32[64,128]{1,0:T(8,128)S(1)}, f32[64,128]{1,0:T(8,128)S(1)}, u32[]{:S(2)}, u32[]{:S(2)}) collective-permute-start(f32[64,128]{1,0:T(8,128)S(1)} %get-tuple-element.34), channel_id=1, source_target_pairs={{0,3},{1,2},{2,1},{3,0},{4,7},{5,6},{6,5},{7,4},{8,11},{9,10},{10,... | collective-permute-start | bytes 98312 | tf_op jit(solution)/shard_map/ppermute | solution.py:891
  6.7 6.8 %collective-permute-start.3 = (f32[152,128]{1,0:T(8,128)S(1)}, f32[152,128]{1,0:T(8,128)S(1)}, u32[]{:S(2)}, u32[]{:S(2)}) collective-permute-start(f32[152,128]{1,0:T(8,128)S(1)} %merge.1.own_ref), channel_id=1, source_target_pairs={{0,1},{1,0},{2,3},{3,2},{4,8},{5,9},{6,10},{7,11},{8,4},{9,5},{10,... | collective-permute-start | bytes 233480 | tf_op jit(solution)/shard_map/ppermute | solution.py:474
  6.9 6.6 %collective-permute-start.2 = (f32[152,128]{1,0:T(8,128)S(1)}, f32[152,128]{1,0:T(8,128)S(1)}, u32[]{:S(2)}, u32[]{:S(2)}) collective-permute-start(f32[152,128]{1,0:T(8,128)S(1)} %merge.1.own_ref), channel_id=1, source_target_pairs={{0,4},{1,5},{2,6},{3,7},{4,0},{5,1},{6,2},{7,3},{8,12},{9,13},{10,... | collective-permute-start | bytes 233480 | tf_op jit(solution)/shard_map/ppermute | solution.py:474
  13.5 26.1 %collective-permute-start.8 = (f32[200,512]{1,0:T(8,128)S(1)}, f32[200,512]{1,0:T(8,128)S(1)}, u32[]{:S(2)}, u32[]{:S(2)}) collective-permute-start(f32[200,512]{1,0:T(8,128)S(1)} %get-tuple-element.52), channel_id=1, source_target_pairs={{0,4},{1,5},{2,6},{3,7},{4,0},{5,1},{6,2},{7,3},{8,12},{9,13},{10,... | collective-permute-start | bytes 1228808 | tf_op jit(solution)/shard_map/ppermute | solution.py:900
  15.6 23.9 %collective-permute-start.9 = (f32[200,512]{1,0:T(8,128)S(1)}, f32[200,512]{1,0:T(8,128)S(1)}, u32[]{:S(2)}, u32[]{:S(2)}) collective-permute-start(f32[200,512]{1,0:T(8,128)S(1)} %get-tuple-element.53), channel_id=1, source_target_pairs={{0,1},{1,0},{2,3},{3,2},{4,8},{5,9},{6,10},{7,11},{8,4},{9,5},{10,... | collective-permute-start | bytes 1228808 | tf_op jit(solution)/shard_map/ppermute | solution.py:900
  27.9 3.2 %collective-permute-start.5 = (f32[24,128]{1,0:T(8,128)S(1)}, f32[24,128]{1,0:T(8,128)S(1)}, u32[]{:S(2)}, u32[]{:S(2)}) collective-permute-start(f32[24,128]{1,0:T(8,128)S(1)} %get-tuple-element.49.shared_ref), channel_id=1, source_target_pairs={{0,3},{1,2},{2,1},{3,0},{4,7},{5,6},{6,5},{7,4},{8,11},{9,10},{10,... | collective-permute-start | bytes 36872 | tf_op jit(solution)/shard_map/ppermute | solution.py:474
  29.6 1.5 %collective-permute-start.4 = (f32[24,128]{1,0:T(8,128)S(1)}, f32[24,128]{1,0:T(8,128)S(1)}, u32[]{:S(2)}, u32[]{:S(2)}) collective-permute-start(f32[24,128]{1,0:T(8,128)S(1)} %get-tuple-element.49.shared_ref), channel_id=1, source_target_pairs={{0,1},{1,0},{2,3},{3,2},{4,5},{5,4},{6,7},{7,6},{8,9},{9,8},{10,11... | collective-permute-start | bytes 36872 | tf_op jit(solution)/shard_map/ppermute | solution.py:474
  31.1 7.3 %collective-permute-start.7 = (f32[120,128]{1,0:T(8,128)S(1)}, f32[120,128]{1,0:T(8,128)S(1)}, u32[]{:S(2)}, u32[]{:S(2)}) collective-permute-start(f32[120,128]{1,0:T(8,128)S(1)} %pad_maximum_fusion), channel_id=1, source_target_pairs={{0,28},{1,29},{2,30},{3,31},{4,8},{5,9},{6,10},{7,11},{8,4},{9,5},... | collective-permute-start | bytes 184328 | tf_op jit(solution)/shard_map/ppermute | solution.py:474
  34.7 4.9 %collective-permute-start.6 = (f32[120,128]{1,0:T(8,128)S(1)}, f32[120,128]{1,0:T(8,128)S(1)}, u32[]{:S(2)}, u32[]{:S(2)}) collective-permute-start(f32[120,128]{1,0:T(8,128)S(1)} %pad_maximum_fusion), channel_id=1, source_target_pairs={{0,4},{1,5},{2,6},{3,7},{4,0},{5,1},{6,2},{7,3},{8,12},{9,13},{10,... | collective-permute-start | bytes 184328 | tf_op jit(solution)/shard_map/ppermute | solution.py:474

commit v6 on v5

--- a/solution.py
+++ b/solution.py
@@ -284,8 +284,8 @@
 
 
 def particles_kernel(
-    ints_ref, first_ref, second_ref, own_ref, own_turned, own_pulled, partial_ref,
-    settled_ref, leaving_ref, state, turned, pulled, begun, blocks,
+    picks_ref, first_ref, second_ref, own_ref, own_turned, own_pulled, partial_ref,
+    settled_ref, leaving_ref, state, turned, pulled, begun, begun_turned, begun_pulled, blocks,
     *, rows, cols,
 ):
     wide = cols + 2 * DEPTH
@@ -301,12 +301,14 @@
 
         tiles_of_block(blocks.at[half], place, rows, cols)
 
-    def far_row(n, carry):
-        r = n + jnp.where(n >= DEPTH, rows, 0)
+    def far_row(r):
         fill_row(lambda c: state[r, c], r, high, wide, turned.at[r], pulled.at[r])
+
+    def near_row(n, carry):
+        far_row(1 + n * (rows + 1))
         return carry
 
-    lax.fori_loop(0, 2 * DEPTH, far_row, 0)
+    lax.fori_loop(0, 2, near_row, 0)
     for r in range(rows):
         state[DEPTH + r] = own_ref[r]
         turned[DEPTH + r] = own_turned[r]
@@ -316,6 +318,13 @@
         nears, founds = emptied(refs)
         sources = dict(turned=lambda row: turned.at[row], pulled=lambda row: pulled.at[row], nears=nears, founds=founds)
         columns = list(range(1, wide - 1, 2))
+
+        later = dict(
+            turned=lambda row: begun_turned.at[row], pulled=lambda row: begun_pulled.at[row], nears=nears, founds=founds
+        )
+
+        def begun_row(r):
+            fill_row(lambda c: begun[r, c], r, high, wide, begun_turned.at[r], begun_pulled.at[r])
 
         def begin_row(r, totals):
             tiles = [[state[r, c], state[r, c + 1]] for c in columns]
@@ -332,12 +341,14 @@
 
         def outer_step(n, carry):
             r = 1 + n * (rows + 1)
+            begun_row(DEPTH + n * (rows - 1))
             tiles = [[state[r, c], state[r, c + 1]] for c in columns]
             begin_row(r, pulls_row(tiles, r, columns, [r - 1, r, r + 1], high, wide, **sources))
             return carry
 
         def inner_step(n, carry):
             r = DEPTH + n * (rows - 1)
+            far_row(n * (high - 1))
             tiles = [[state[r, c], state[r, c + 1]] for c in columns]
             totals = pulls_row(tiles, r, columns, [1 + n * (rows + 1)], high, wide, **sources)
             begin_row(r, [total + partial_ref[n * (rows - 1), pair] for pair, total in enumerate(totals)])
@@ -346,16 +357,13 @@
         lax.fori_loop(0, 2, inner_step, 0)
         lax.fori_loop(0, 2, outer_step, 0)
 
-        def begun_row(r, carry):
-            fill_row(lambda c: begun[r, c], r, high, wide, turned.at[r], pulled.at[r])
-            return carry
-
-        lax.fori_loop(1, high - 1, begun_row, 0)
+        begun_row(jnp.int32(1))
 
         def second_step(r, carry):
             columns = list(range(DEPTH, DEPTH + cols, 2))
             tiles = [[begun[r, c], begun[r, c + 1]] for c in columns]
-            totals = pulls_row(tiles, r, columns, [r - 1, r, r + 1], high, wide, **sources)
+            begun_row(jnp.int32(high - 2))
+            totals = pulls_row(tiles, r, columns, [r - 1, r, r + 1], high, wide, **later)
             forces = forces_of(totals, tiles, r, columns, high, wide)
             for c in range(cols):
                 settled_ref[r - DEPTH, c] = stepped(tiles[c // 2][c % 2], forces[c])
@@ -365,23 +373,17 @@
 
     pl.run_scoped(substeps, *accumulators(wide))
 
-    leaving_ref[...] = jnp.zeros_like(leaving_ref)
-    count = jnp.int32(0)
-    for t in range(rows * cols):
-        flag = ints_ref[0, EXITS + t]
-
-        @pl.when((flag > 0) & (count < cols))
-        def _(t=t, count=count):
-            for d in range(6):
-                leaving_ref[d, pl.ds(count, 1)] = settled_ref[t // cols, t % cols, d : d + 1]
-
-        count = count + flag
-
-
-def particles(ints, first, second, own):
+    for k in range(cols):
+        tile = jnp.zeros((COMPS, LANES), f32)
+        for c in range(cols):
+            tile = tile + picks_ref[k, c : c + 1] * settled_ref[rows - 1, c]
+        for d in range(6):
+            leaving_ref[d, k : k + 1] = tile[d : d + 1]
+
+
+def particles(picks, first, second, own):
     rows, wide = own[0].shape[:2]
     cols, high = wide - 2 * DEPTH, rows + 2 * DEPTH
-    smem = pl.BlockSpec(memory_space=pltpu.SMEM)
     vmem = pl.BlockSpec(memory_space=pltpu.VMEM)
     return pl.pallas_call(
         functools.partial(particles_kernel, rows=rows, cols=cols),
@@ -389,46 +391,42 @@
             jax.ShapeDtypeStruct((rows, cols, COMPS, LANES), f32),
             jax.ShapeDtypeStruct((6, cols, LANES), f32),
         ),
-        in_specs=[smem] + [vmem] * 6,
+        in_specs=[vmem] * 7,
         out_specs=(vmem, vmem),
         scratch_shapes=[
             pltpu.VMEM((high, wide, COMPS, LANES), f32),
             pltpu.VMEM((high, wide // 4, LANES, LANES), bf16),
             pltpu.VMEM((high, wide, 16, LANES), bf16),
             pltpu.VMEM((high, wide, COMPS, LANES), f32),
+            pltpu.VMEM((high, wide // 4, LANES, LANES), bf16),
+            pltpu.VMEM((high, wide, 16, LANES), bf16),
             pltpu.VMEM((2, *first.shape), f32),
         ],
         cost_estimate=pl.CostEstimate(flops=10**10, bytes_accessed=4096, transcendentals=0),
         compiler_params=pltpu.CompilerParams(vmem_limit_bytes=12 * MIB),
         name="particles",
-    )(ints, first, second, *own)
-
-
-def deposit_kernel(ints_ref, settled_ref, slots_ref, blocks_ref, own_ref, shared_ref):
+    )(picks, first, second, *own)
+
+
+def deposit_kernel(settled_ref, slots_ref, weights_ref, owners_ref, own_ref, shared_ref):
     rows, cols = settled_ref.shape[:2]
-    quarters = blocks_ref.shape[0]
     row = lax.broadcasted_iota(i32, (16, LANES), 0)
     cell = lax.broadcasted_iota(i32, (LANES, LANES), 0)
-    lane = lax.broadcasted_iota(i32, (1, LANES), 1)
-    owner_row = jnp.zeros((1, LANES), i32)
     for t in range(rows * cols):
         r, c = t // cols, t % cols
-        owner = ints_ref[0, OWNERS + t]
-        owner_row = jnp.where(lax.rem(lane, rows * cols) == t, owner, owner_row)
         lift_high, lift_mid, lift_low = split(deposit_gain * settled_ref[r, c, 5:6, :])
         parts = jnp.where(row == 0, lift_high, jnp.where(row == 1, lift_mid, jnp.where(row == 2, lift_low, 0.0)))
         table = jnp.where(cell == slots_ref[r, c : c + 1, :], 1.0, 0.0).astype(bf16)
         gathered = lax.dot_general(parts.astype(bf16), table, (((1,), (1,)), ((), ())), preferred_element_type=f32)
         sums = jnp.sum(gathered, axis=0, keepdims=True)
         own_ref[t : t + 1, :] = sums
-        shared_ref[t : t + 1, :] = blocks_ref[owner % quarters, pl.ds(owner // quarters, 1), :] * sums
+        shared_ref[t : t + 1, :] = weights_ref[t : t + 1] * sums
     row = lax.broadcasted_iota(i32, (ROWS_OUT - rows * cols, LANES), 0)
-    shared_ref[rows * cols :, :] = jnp.where(row == 0, owner_row.astype(f32), 0.0)
-
-
-def deposits(ints, settled, slots, blocks):
+    shared_ref[rows * cols :, :] = jnp.where(row == 0, owners_ref[...], 0.0)
+
+
+def deposits(settled, slots, weights, owners):
     rows, cols = settled.shape[:2]
-    smem = pl.BlockSpec(memory_space=pltpu.SMEM)
     vmem = pl.BlockSpec(memory_space=pltpu.VMEM)
     return pl.pallas_call(
         deposit_kernel,
@@ -436,11 +434,61 @@
             jax.ShapeDtypeStruct((rows * cols, LANES), f32),
             jax.ShapeDtypeStruct((ROWS_OUT, LANES), f32),
         ),
-        in_specs=[smem, vmem, vmem, vmem],
+        in_specs=[vmem] * 4,
         out_specs=(vmem, vmem),
         compiler_params=pltpu.CompilerParams(vmem_limit_bytes=4 * MIB),
         name="deposits",
-    )(ints, settled, slots, blocks)
+    )(settled, slots, weights, owners)
+
+
+def marks_kernel(ints_ref, cells_ref, picks_ref, keeps_ref, places_ref, weights_ref, owners_ref, blocks):
+    cols = keeps_ref.shape[0]
+    tiles = weights_ref.shape[0]
+    _, levels, across, along = cells_ref.shape
+    quarters = along // LANES
+    for z in range(levels):
+        for q in range(quarters):
+            blocks[q, z * across : (z + 1) * across] = cells_ref[1, z, :, q * LANES : (q + 1) * LANES]
+    lane = lax.broadcasted_iota(i32, (1, LANES), 1)
+    row = lax.broadcasted_iota(i32, (cols, LANES), 0)
+    owner_row = jnp.zeros((1, LANES), i32)
+    for t in range(tiles):
+        owner = ints_ref[0, OWNERS + t]
+        owner_row = jnp.where(lax.rem(lane, tiles) == t, owner, owner_row)
+        line = blocks[owner % quarters, pl.ds(owner // quarters, 1), :]
+        weights_ref[t : t + 1, :] = 1.0 / (6.0 + line)
+    owners_ref[...] = owner_row.astype(f32)
+    picks_ref[...] = jnp.zeros_like(picks_ref)
+    count = jnp.int32(0)
+    for c in range(cols):
+        flag = ints_ref[0, EXITS + tiles - cols + c]
+        keeps_ref[c : c + 1] = jnp.broadcast_to(jnp.where(flag > 0, 0.0, 1.0), (1, LANES))
+        for k in range(c + 1):
+            picks_ref[k, c : c + 1] = jnp.broadcast_to(jnp.where((flag > 0) & (count == k), 1.0, 0.0), (1, LANES))
+        count = count + flag
+        places_ref[c] = jnp.where(row == ints_ref[0, INLETS + c], 1.0, 0.0)
+
+
+def marks_of(ints, cells, tiles, cols):
+    _, levels, across, along = cells.shape
+    smem = pl.BlockSpec(memory_space=pltpu.SMEM)
+    vmem = pl.BlockSpec(memory_space=pltpu.VMEM)
+    return pl.pallas_call(
+        marks_kernel,
+        out_shape=(
+            jax.ShapeDtypeStruct((cols, cols, LANES), f32),
+            jax.ShapeDtypeStruct((cols, LANES), f32),
+            jax.ShapeDtypeStruct((cols, cols, LANES), f32),
+            jax.ShapeDtypeStruct((tiles, LANES), f32),
+            jax.ShapeDtypeStruct((1, LANES), f32),
+        ),
+        in_specs=[smem, vmem],
+        out_specs=(vmem,) * 5,
+        scratch_shapes=[pltpu.VMEM((along // LANES, levels * across, LANES), f32)],
+        cost_estimate=pl.CostEstimate(flops=10**9, bytes_accessed=4096, transcendentals=0),
+        compiler_params=pltpu.CompilerParams(vmem_limit_bytes=4 * MIB),
+        name="marks",
+    )(ints, cells)
 
 
 def matching(heights, groups, axis, odd, wrap):
@@ -574,7 +622,7 @@
     )(begun_zeros(), exits, owners, inlets, positions, velocities, contacts, slots, gas, diagonal)
 
 
-def merge_kernel(state_ref, flags_ref, line_a, line_b, window_ref):
+def merge_kernel(state_ref, flags_ref, line_a, line_b, owners_ref, window_ref):
     rows, cols = state_ref.shape[1:3]
     each = rows * (cols + 2 * DEPTH)
     count = 6 * rows * DEPTH
@@ -594,17 +642,17 @@
     )
 
 
-def merged(state, flags, lines):
+def merged(state, flags, lines, owners):
     rows, cols = state.shape[1:3]
     vmem = pl.BlockSpec(memory_space=pltpu.VMEM)
     return pl.pallas_call(
         merge_kernel,
         out_shape=jax.ShapeDtypeStruct((6 * rows * (cols + 2 * DEPTH) + 8, LANES), f32),
-        in_specs=[vmem] * 4,
+        in_specs=[vmem] * 5,
         out_specs=vmem,
         compiler_params=pltpu.CompilerParams(vmem_limit_bytes=4 * MIB),
         name="merge",
-    )(state, flags, *lines)
+    )(state, flags, *lines, owners)
 
 
 def line_at(lines, z, k, kind, q, quarters):
@@ -612,7 +660,7 @@
     return lines[row : row + 1]
 
 
-def faces_kernel(cells_ref, line_a, line_b, scaling_ref, blocks_ref, first_ref, second_ref):
+def faces_kernel(cells_ref, line_a, line_b, scaling_ref, first_ref, second_ref):
     _, levels, across, along = cells_ref.shape
     quarters = along // LANES
     left, right, _, _, even, even_c = position()
@@ -622,8 +670,6 @@
     for z in range(levels):
         scaling_ref[z] = 1.0 / (6.0 + cells_ref[1, z])
         scaled.append(scaling_ref[z] * cells_ref[0, z])
-        for q in range(quarters):
-            blocks_ref[q, z * across : (z + 1) * across] = scaling_ref[z, :, q * LANES : (q + 1) * LANES]
     faces = []
     for z in range(levels):
         ends = []
@@ -659,12 +705,11 @@
         faces_kernel,
         out_shape=(
             jax.ShapeDtypeStruct((levels, across, along), f32),
-            jax.ShapeDtypeStruct((along // LANES, levels * across, LANES), f32),
             face,
             face,
         ),
         in_specs=[vmem] * 3,
-        out_specs=(vmem,) * 4,
+        out_specs=(vmem,) * 3,
         compiler_params=pltpu.CompilerParams(vmem_limit_bytes=8 * MIB),
         name="faces",
     )(cells, *lines)
@@ -808,7 +853,7 @@
 
 
 def results_kernel(
-    ints_ref, dots_ref, rhs_ref, near_ref, far_ref, scaling_ref, settled_ref, height_a, height_b,
+    keeps_ref, places_ref, dots_ref, rhs_ref, near_ref, far_ref, scaling_ref, settled_ref, height_a, height_b,
     positions_out, velocities_out, pressure_out, residual_out, positions, velocities, pressure, residual, sent,
 ):
     rows, cols = settled_ref.shape[:2]
@@ -816,7 +861,9 @@
     even = position()[4]
     for r in range(1, rows):
         for c in range(cols):
-            kept = jnp.where(ints_ref[0, EXITS + r * cols + c] > 0, 0.0, settled_ref[r, c])
+            kept = settled_ref[r, c]
+            if r == rows - 1:
+                kept = kept * keeps_ref[c : c + 1]
             for d in range(3):
                 positions[d, r, c : c + 1] = kept[d : d + 1]
                 velocities[d, r, c : c + 1] = kept[d + 3 : d + 4]
@@ -825,8 +872,7 @@
         block = slice(start + d * cols, start + (d + 1) * cols)
         tiles = jnp.where(even, height_b[block], height_a[block])
         target = positions if d < 3 else velocities
-        for k in range(cols):
-            target[d % 3, 0, pl.ds(ints_ref[0, INLETS + k], 1)] = tiles[k : k + 1]
+        target[d % 3, 0] = sum(places_ref[k] * tiles[k : k + 1] for k in range(cols))
     copies = [
         pltpu.make_async_copy(positions, positions_out, sent.at[0]),
         pltpu.make_async_copy(velocities, velocities_out, sent.at[1]),
@@ -857,7 +903,7 @@
         copy.wait()
 
 
-def results_of(ints, dots, rhs, near, far, scaling, settled, height):
+def results_of(keeps, places, dots, rhs, near, far, scaling, settled, height):
     rows, cols = settled.shape[:2]
     smem = pl.BlockSpec(memory_space=pltpu.SMEM)
     vmem = pl.BlockSpec(memory_space=pltpu.VMEM)
@@ -866,7 +912,7 @@
     return pl.pallas_call(
         results_kernel,
         out_shape=(particle, particle, field, field),
-        in_specs=[smem] + [vmem] * 8,
+        in_specs=[vmem] * 10,
         out_specs=(pl.BlockSpec(memory_space=pl.ANY),) * 4,
         scratch_shapes=[
             *[pltpu.VMEM(particle.shape, f32)] * 2,
@@ -875,7 +921,7 @@
         ],
         compiler_params=pltpu.CompilerParams(vmem_limit_bytes=8 * MIB),
         name="results",
-    )(ints, dots, rhs, near, far, scaling, settled, *height)
+    )(keeps, places, dots, rhs, near, far, scaling, settled, *height)
 
 
 def on_device(
@@ -891,17 +937,19 @@
         lax.ppermute(value, ("height", "cols"), matching(heights, groups, "cols", odd, True))
         for value, odd in zip(sides, (False, True))
     ]
-    window = merged(state, flags, lines)
+    rows, cols = state.shape[1:3]
+    picks, keeps, places, weights, owners = marks_of(ints, cells, rows * cols, cols)
+    window = merged(state, flags, lines, owners)
     beside = exchanged(window, "height", False)
     own_parts = own_sums(window, *state.shape[1:3])
-    scaling, blocks, *faces = faces_of(cells, lines)
+    scaling, *faces = faces_of(cells, lines)
     faces, beside = lax.optimization_barrier((faces, beside))
     faces = [
         lax.ppermute(value, ("height", "cols"), matching(heights, groups, "height", odd, False))
         for value, odd in zip(faces, (False, True))
     ]
-    settled, leaving = particles(ints, *beside, own_parts)
-    own, shared = deposits(ints, settled, slots, blocks)
+    settled, leaving = particles(picks, *beside, own_parts)
+    own, shared = deposits(settled, slots, weights, owners)
     near = exchanged(shared, "cols", True)
     parcel = jnp.concatenate([shared, *near, leaving.reshape(-1, LANES)], axis=0)
     parcels = exchanged(parcel, "height", True)
@@ -909,7 +957,7 @@
         own, shared, near, parcels, cells, scaling, lines, faces, heights * groups
     )
     dots = lax.all_to_all(dots, ("height", "cols"), 0, 0, tiled=True)
-    return results_of(ints, dots, rhs, first, second, scaling, settled, parcels)
+    return results_of(keeps, places, dots, rhs, first, second, scaling, settled, parcels)
 
 
 def solution(mesh):

time: 53 us -> 51.2 us (0.966)
  Pallas kernels: 18.7 us -> 17 us
  waiting for transfers between devices: 8.02 us -> 7.31 us
  blocking collectives: 10.5 us -> 11.1 us
    pallas_call x1, Pallas kernels: 11.3 us -> 9.99 us  [particles(): pl.pallas_call(functools.partial(particles_kernel, rows=rows, cols=cols),...]
    ppermute x2, waiting for transfers between devices: 1.67 us -> 0.96 us  [on_device(): lax.ppermute(value, ('height', 'cols'), matching(heights, groups, 'cols',...]
    pallas_call x0 -> x1, Pallas kernels: none -> 0.69 us  [marks_of(): pl.pallas_call(marks_kernel, out_shape=(jax.ShapeDtypeStruct((cols, cols,...]
    all_to_all x1, blocking collectives: 10.5 us -> 11.1 us  [on_device(): dots = lax.all_to_all(dots, ('height', 'cols'), 0, 0, tiled=True)]
    pallas_call x1, Pallas kernels: 0.94 us -> 0.4 us  [deposits(): pl.pallas_call(deposit_kernel, out_shape=(jax.ShapeDtypeStruct((rows * co...]
    pallas_call x1, Pallas kernels: 1.69 us -> 1.15 us  [results_of(): pl.pallas_call(results_kernel, out_shape=(particle, particle, field, fiel...]
  transfers between devices with their start and end apart: 10 -> 10, of which waited for: 4 -> 4; matrix products, arithmetic and copies ran while one was open for 0% -> 0% of each run, Pallas kernels for 30% -> 29%
where the time goes in v6:
time: 51.2 us; the launch traced here: 51 us
  Pallas kernels  17 us (33%)
  starting transfers between devices  13.8 us (27%)
  blocking collectives  11.1 us (22%)
  waiting for transfers between devices  7.31 us (14%)
  local copies, waits for them, and re-layouts  0.96 us (2%)
  between operations  0.81 us (2%)
    all_to_all x1, blocking collectives, on_device(): dots = lax.all_to_all(dots, ('height', 'cols'), 0, 0, tiled=True)  11.1 us
    pallas_call x1, Pallas kernels, particles(): pl.pallas_call(functools.partial(particles_kernel, rows=rows, cols=cols),...  9.99 us
    ppermute x6, starting transfers between devices, exchanged(): lax.ppermute(value, ('height', 'cols'), matching(heights, groups, axis, o...  8.55 us
    ppermute x6, waiting for transfers between devices, exchanged(): lax.ppermute(value, ('height', 'cols'), matching(heights, groups, axis, o...  6.35 us
    pallas_call x1, Pallas kernels, own_sums(): pl.pallas_call(functools.partial(own_kernel, rows=rows, cols=cols), out_s...  3.26 us
    ppermute x2, starting transfers between devices, on_device(): lax.ppermute(value, ('height', 'cols'), matching(heights, groups, 'cols',...  3.13 us
    ppermute x2, starting transfers between devices, on_device(): lax.ppermute(value, ('height', 'cols'), matching(heights, groups, 'height...  2.15 us
    pallas_call x1, Pallas kernels, results_of(): pl.pallas_call(results_kernel, out_shape=(particle, particle, field, fiel...  1.15 us
  transfers between devices with their start and end apart: 10, of which 4 were waited for; matrix products, arithmetic and copies ran while one was open for 0% of the time, Pallas kernels for 29%

profile of v6, /device:TPU:0, one launch (start us, length us, event | category | flops | bytes accessed | tf_op | source)
XLA Modules:
  0.0 51.0 jit_solution(6656401123866205608)
XLA Ops:
  0.6 0.0 copy-start.1
  0.6 0.0 copy-start
  0.7 0.0 copy-start.5
  0.7 0.0 copy-start.4
  0.7 0.0 copy-start.3
  0.7 0.0 copy-start.2
  0.7 0.0 copy-start.7
  0.7 0.0 copy-start.6
  0.7 0.0 copy-start.8
  0.7 0.8 %copy-done.1 = f32[2,64,512]{2,1,0:T(8,128)S(1)} copy-done((f32[2,64,512]{2,1,0:T(8,128)S(1)}, f32[2,64,512]{2,1,0:T(8,128)}, u32[]{:S(2)}) %copy-start.1) | copy-done | bytes 262168
  1.6 0.1 copy-done
  1.7 0.0 copy-done.5
  1.7 0.0 copy-done.4
  1.7 0.0 copy-done.3
  1.7 0.0 copy-done.2
  1.7 0.0 copy-done.7
  1.7 0.0 copy-done.6
  1.7 0.0 copy-done.8
  1.7 0.2 pack.1
  1.9 0.5 collective-permute-start
  2.4 2.6 %collective-permute-start.1 = (f32[64,128]{1,0:T(8,128)S(1)}, f32[64,128]{1,0:T(8,128)S(1)}, u32[]{:S(2)}, u32[]{:S(2)}) collective-permute-start(f32[64,128]{1,0:T(8,128)S(1)} %get-tuple-element.41), channel_id=1, source_target_pairs={{0,3},{1,2},{2,1},{3,0},{4,7},{5,6},{6,5},{7,4},{8,11},{9,10},{10,... | collective-permute-start | bytes 98312 | tf_op jit(solution)/shard_map/ppermute | solution.py:937
  5.0 0.7 %marks.1 = (f32[8,8,128]{2,1,0:T(8,128)S(1)}, f32[8,128]{1,0:T(8,128)S(1)}, f32[8,8,128]{2,1,0:T(8,128)S(1)}, f32[16,128]{1,0:T(8,128)S(1)}, f32[1,128]{1,0:T(1,128)S(1)}) custom-call(s32[1,128]{1,0:T(1,128)S(1)} %get-tuple-element.35.ints_ref, f32[2,2,64,512]{3,2,1,0:T(8,128)S(1)} %get-tuple-element.36.cells_ref), custom_call_target="tpu_custom_call" | custom-call | flops 1000000000 | bytes 4096 | tf_op jit(solution)/shard_map/marks/pallas_call | solution.py:476
  5.7 0.0 collective-permute-done.line_a
  5.7 1.0 %collective-permute-done.1.line_b = f32[64,128]{1,0:T(8,128)S(1)} collective-permute-done((f32[64,128]{1,0:T(8,128)S(1)}, f32[64,128]{1,0:T(8,128)S(1)}, u32[]{:S(2)}, u32[]{:S(2)}) %collective-permute-start.1) | collective-permute-done | bytes 32800 | tf_op jit(solution)/shard_map/ppermute | solution.py:937
  6.7 0.2 collective-permute-start.3
  6.9 3.0 %collective-permute-start.2 = (f32[152,128]{1,0:T(8,128)S(1)}, f32[152,128]{1,0:T(8,128)S(1)}, u32[]{:S(2)}, u32[]{:S(2)}) collective-permute-start(f32[152,128]{1,0:T(8,128)S(1)} %merge.1.own_ref), channel_id=1, source_target_pairs={{0,4},{1,5},{2,6},{3,7},{4,0},{5,1},{6,2},{7,3},{8,12},{9,13},{10,... | collective-permute-start | bytes 233480 | tf_op jit(solution)/shard_map/ppermute | solution.py:522
  9.9 3.3 %own_sums.1 = (f32[2,12,8,128]{3,2,1,0:T(8,128)S(1)}, bf16[2,3,128,128]{3,2,1,0:T(8,128)(2,1)S(1)}, bf16[2,12,16,128]{3,2,1,0:T(8,128)(2,1)S(1)}, f32[2,5,16,256]{3,2,1,0:T(8,128)S(1)}) custom-call(f32[152,128]{1,0:T(8,128)S(1)} %merge.1.own_ref), custom_call_target="tpu_custom_call" | custom-call | flops 4000000000 | bytes 4096 | tf_op jit(solution)/shard_map/own_sums/pallas_call | solution.py:270
  13.2 0.3 faces.1
  13.5 0.0 collective-permute-done.3.second_ref
  13.5 0.0 collective-permute-done.2.first_ref
  13.5 2.1 %collective-permute-start.8 = (f32[200,512]{1,0:T(8,128)S(1)}, f32[200,512]{1,0:T(8,128)S(1)}, u32[]{:S(2)}, u32[]{:S(2)}) collective-permute-start(f32[200,512]{1,0:T(8,128)S(1)} %get-tuple-element.60), channel_id=1, source_target_pairs={{0,4},{1,5},{2,6},{3,7},{4,0},{5,1},{6,2},{7,3},{8,12},{9,13},{10,... | collective-permute-start | bytes 1228808 | tf_op jit(solution)/shard_map/ppermute | solution.py:948
  15.6 0.0 collective-permute-start.9
  15.6 10.0 %particles.1 = (f32[2,8,8,128]{3,2,1,0:T(8,128)S(1)}, f32[6,8,128]{2,1,0:T(8,128)S(1)}) custom-call(f32[8,8,128]{2,1,0:T(8,128)S(1)} %get-tuple-element.39.picks_ref, f32[152,128]{1,0:T(8,128)S(1)} %collective-permute-done.2.first_ref, f32[152,128]{1,0:T(8,128)S(1)} %collective-permute-done.3.second_ref, f32[2,12,8,128]{3,2,1,0:T(8,128)S(1)} %get-tuple-element.49.own_ref, ...), custom_call_target="tpu_custom_call" | custom-call | flops 10000000000 | bytes 4096 | tf_op jit(solution)/shard_map/particles/pallas_call | solution.py:388
  25.6 0.4 deposits.1
  26.0 1.7 %collective-permute-start.5 = (f32[24,128]{1,0:T(8,128)S(1)}, f32[24,128]{1,0:T(8,128)S(1)}, u32[]{:S(2)}, u32[]{:S(2)}) collective-permute-start(f32[24,128]{1,0:T(8,128)S(1)} %get-tuple-element.57.shared_ref), channel_id=1, source_target_pairs={{0,3},{1,2},{2,1},{3,0},{4,7},{5,6},{6,5},{7,4},{8,11},{9,10},{10,... | collective-permute-start | bytes 36872 | tf_op jit(solution)/shard_map/ppermute | solution.py:522
  27.7 0.0 collective-permute-start.4
  27.7 1.5 %collective-permute-done.5.side_b = f32[24,128]{1,0:T(8,128)S(1)} collective-permute-done((f32[24,128]{1,0:T(8,128)S(1)}, f32[24,128]{1,0:T(8,128)S(1)}, u32[]{:S(2)}, u32[]{:S(2)}) %collective-permute-start.5) | collective-permute-done | bytes 12320 | tf_op jit(solution)/shard_map/ppermute | solution.py:522
  29.2 0.0 collective-permute-done.4.side_a
  29.2 3.6 %collective-permute-start.7 = (f32[120,128]{1,0:T(8,128)S(1)}, f32[120,128]{1,0:T(8,128)S(1)}, u32[]{:S(2)}, u32[]{:S(2)}) collective-permute-start(f32[120,128]{1,0:T(8,128)S(1)} %pad_maximum_fusion), channel_id=1, source_target_pairs={{0,28},{1,29},{2,30},{3,31},{4,8},{5,9},{6,10},{7,11},{8,4},{9,5},... | collective-permute-start | bytes 184328 | tf_op jit(solution)/shard_map/ppermute | solution.py:522
  32.9 0.0 collective-permute-start.6
  32.9 3.6 %collective-permute-done.7.height_b = f32[120,128]{1,0:T(8,128)S(1)} collective-permute-done((f32[120,128]{1,0:T(8,128)S(1)}, f32[120,128]{1,0:T(8,128)S(1)}, u32[]{:S(2)}, u32[]{:S(2)}) %collective-permute-start.7) | collective-permute-done | bytes 61472 | tf_op jit(solution)/shard_map/ppermute | solution.py:522
  36.5 1.2 %collective-permute-done.6.height_a = f32[120,128]{1,0:T(8,128)S(1)} collective-permute-done((f32[120,128]{1,0:T(8,128)S(1)}, f32[120,128]{1,0:T(8,128)S(1)}, u32[]{:S(2)}, u32[]{:S(2)}) %collective-permute-start.6) | collective-permute-done | bytes 61472 | tf_op jit(solution)/shard_map/ppermute | solution.py:522
  37.7 0.0 collective-permute-done.8.face_a
  37.7 0.0 collective-permute-done.9.face_b
  37.7 1.0 %right_side.1 = (f32[2,64,512]{2,1,0:T(8,128)S(1)}, f32[2,64,512]{2,1,0:T(8,128)S(1)}, f32[2,64,512]{2,1,0:T(8,128)S(1)}, f32[32,128]{1,0:T(8,128)S(1)}) custom-call(f32[16,128]{1,0:T(8,128)S(1)} %get-tuple-element.56.own_ref, f32[24,128]{1,0:T(8,128)S(1)} %get-tuple-element.57.shared_ref, f32[24,128]{1,0:T(8,128)S(1)} %collective-permute-done.4.side_a, ...), custom_call_target="tpu_custom_call" | custom-call | tf_op jit(solution)/shard_map/right_side/pallas_call | solution.py:844
  38.8 11.1 %all_to_all.11 = f32[32,1,128]{2,1,0:T(1,128)S(1)} all-to-all(f32[32,1,128]{2,1,0:T(1,128)S(1)} %bitcast.8), channel_id=1, replica_groups=mesh['height'=8,'cols'=4] {'height','cols'}, dimensions={0} | all-to-all | bytes 32768 | tf_op jit(solution)/shard_map/all_to_all | solution.py:959
  49.9 1.2 %results.1 = (f32[3,2,8,128]{3,2,1,0:T(8,128)}, f32[3,2,8,128]{3,2,1,0:T(8,128)}, f32[2,64,512]{2,1,0:T(8,128)}, f32[2,64,512]{2,1,0:T(8,128)}) custom-call(f32[8,128]{1,0:T(8,128)S(1)} %get-tuple-element.37.keeps_ref, f32[8,8,128]{2,1,0:T(8,128)S(1)} %get-tuple-element.38.places_ref, f32[32,128]{1,0:T(8,128)S(1)} %bitcast.6, ...), custom_call_target="tpu_custom_call" | custom-call | tf_op jit(solution)/shard_map/results/pallas_call | solution.py:912
  (3 shorter events, 0.0 us)
Async XLA Ops:
  0.6 1.0 %copy-start.1 = (f32[2,64,512]{2,1,0:T(8,128)S(1)}, f32[2,64,512]{2,1,0:T(8,128)}, u32[]{:S(2)}) copy-start(f32[2,64,512]{2,1,0:T(8,128)} %diagonal_ref.1) | copy-start | bytes 786436
  0.6 1.0 %copy-start = (f32[2,64,512]{2,1,0:T(8,128)S(1)}, f32[2,64,512]{2,1,0:T(8,128)}, u32[]{:S(2)}) copy-start(f32[2,64,512]{2,1,0:T(8,128)} %gas_ref.1) | copy-start | bytes 786436
  0.7 1.0 %copy-start.5 = (s32[2,8,128]{2,1,0:T(8,128)S(1)}, s32[2,8,128]{2,1,0:T(8,128)}, u32[]{:S(2)}) copy-start(s32[2,8,128]{2,1,0:T(8,128)} %slots_in.1) | copy-start | bytes 24580
  0.7 1.0 %copy-start.4 = (s32[9,2,8]{0,2,1:T(8,128)S(1)}, s32[9,2,8]{0,2,1:T(8,128)}, u32[]{:S(2)}) copy-start(s32[9,2,8]{0,2,1:T(8,128)} %param.11) | copy-start | bytes 1732
  0.7 1.0 %copy-start.3 = (f32[3,2,8,128]{3,2,1,0:T(8,128)S(1)}, f32[3,2,8,128]{3,2,1,0:T(8,128)}, u32[]{:S(2)}) copy-start(f32[3,2,8,128]{3,2,1,0:T(8,128)} %velocities_ref.1) | copy-start | bytes 73732
  0.7 1.0 %copy-start.2 = (f32[3,2,8,128]{3,2,1,0:T(8,128)S(1)}, f32[3,2,8,128]{3,2,1,0:T(8,128)}, u32[]{:S(2)}) copy-start(f32[3,2,8,128]{3,2,1,0:T(8,128)} %positions_ref.1) | copy-start | bytes 73732
  0.7 1.0 %copy-start.7 = (s32[2,8]{1,0:T(2,128)S(1)}, s32[2,8]{1,0:T(2,128)}, u32[]{:S(2)}) copy-start(s32[2,8]{1,0:T(2,128)} %owners_ref.1) | copy-start | bytes 196
  0.7 1.0 %copy-start.6 = (s32[2,8]{1,0:T(2,128)S(1)}, s32[2,8]{1,0:T(2,128)}, u32[]{:S(2)}) copy-start(s32[2,8]{1,0:T(2,128)} %exits_ref.1) | copy-start | bytes 196
  0.7 1.0 %copy-start.8 = (s32[1,8]{1,0:T(1,128)S(1)}, s32[1,8]{1,0:T(1,128)}, u32[]{:S(2)}) copy-start(s32[1,8]{1,0:T(1,128)} %inlets_ref.1) | copy-start | bytes 100
  1.9 3.8 %collective-permute-start = (f32[64,128]{1,0:T(8,128)S(1)}, f32[64,128]{1,0:T(8,128)S(1)}, u32[]{:S(2)}, u32[]{:S(2)}) collective-permute-start(f32[64,128]{1,0:T(8,128)S(1)} %get-tuple-element.40), channel_id=1, source_target_pairs={{0,1},{1,0},{2,3},{3,2},{4,5},{5,4},{6,7},{7,6},{8,9},{9,8},{10,11... | collective-permute-start | bytes 98312 | tf_op jit(solution)/shard_map/ppermute | solution.py:937
  2.4 4.3 %collective-permute-start.1 = (f32[64,128]{1,0:T(8,128)S(1)}, f32[64,128]{1,0:T(8,128)S(1)}, u32[]{:S(2)}, u32[]{:S(2)}) collective-permute-start(f32[64,128]{1,0:T(8,128)S(1)} %get-tuple-element.41), channel_id=1, source_target_pairs={{0,3},{1,2},{2,1},{3,0},{4,7},{5,6},{6,5},{7,4},{8,11},{9,10},{10,... | collective-permute-start | bytes 98312 | tf_op jit(solution)/shard_map/ppermute | solution.py:937
  6.7 6.8 %collective-permute-start.3 = (f32[152,128]{1,0:T(8,128)S(1)}, f32[152,128]{1,0:T(8,128)S(1)}, u32[]{:S(2)}, u32[]{:S(2)}) collective-permute-start(f32[152,128]{1,0:T(8,128)S(1)} %merge.1.own_ref), channel_id=1, source_target_pairs={{0,1},{1,0},{2,3},{3,2},{4,8},{5,9},{6,10},{7,11},{8,4},{9,5},{10,... | collective-permute-start | bytes 233480 | tf_op jit(solution)/shard_map/ppermute | solution.py:522
  6.9 6.6 %collective-permute-start.2 = (f32[152,128]{1,0:T(8,128)S(1)}, f32[152,128]{1,0:T(8,128)S(1)}, u32[]{:S(2)}, u32[]{:S(2)}) collective-permute-start(f32[152,128]{1,0:T(8,128)S(1)} %merge.1.own_ref), channel_id=1, source_target_pairs={{0,4},{1,5},{2,6},{3,7},{4,0},{5,1},{6,2},{7,3},{8,12},{9,13},{10,... | collective-permute-start | bytes 233480 | tf_op jit(solution)/shard_map/ppermute | solution.py:522
  13.5 24.3 %collective-permute-start.8 = (f32[200,512]{1,0:T(8,128)S(1)}, f32[200,512]{1,0:T(8,128)S(1)}, u32[]{:S(2)}, u32[]{:S(2)}) collective-permute-start(f32[200,512]{1,0:T(8,128)S(1)} %get-tuple-element.60), channel_id=1, source_target_pairs={{0,4},{1,5},{2,6},{3,7},{4,0},{5,1},{6,2},{7,3},{8,12},{9,13},{10,... | collective-permute-start | bytes 1228808 | tf_op jit(solution)/shard_map/ppermute | solution.py:948
  15.6 22.1 %collective-permute-start.9 = (f32[200,512]{1,0:T(8,128)S(1)}, f32[200,512]{1,0:T(8,128)S(1)}, u32[]{:S(2)}, u32[]{:S(2)}) collective-permute-start(f32[200,512]{1,0:T(8,128)S(1)} %get-tuple-element.61), channel_id=1, source_target_pairs={{0,1},{1,0},{2,3},{3,2},{4,8},{5,9},{6,10},{7,11},{8,4},{9,5},{10,... | collective-permute-start | bytes 1228808 | tf_op jit(solution)/shard_map/ppermute | solution.py:948
  26.0 3.2 %collective-permute-start.5 = (f32[24,128]{1,0:T(8,128)S(1)}, f32[24,128]{1,0:T(8,128)S(1)}, u32[]{:S(2)}, u32[]{:S(2)}) collective-permute-start(f32[24,128]{1,0:T(8,128)S(1)} %get-tuple-element.57.shared_ref), channel_id=1, source_target_pairs={{0,3},{1,2},{2,1},{3,0},{4,7},{5,6},{6,5},{7,4},{8,11},{9,10},{10,... | collective-permute-start | bytes 36872 | tf_op jit(solution)/shard_map/ppermute | solution.py:522
  27.7 1.5 %collective-permute-start.4 = (f32[24,128]{1,0:T(8,128)S(1)}, f32[24,128]{1,0:T(8,128)S(1)}, u32[]{:S(2)}, u32[]{:S(2)}) collective-permute-start(f32[24,128]{1,0:T(8,128)S(1)} %get-tuple-element.57.shared_ref), channel_id=1, source_target_pairs={{0,1},{1,0},{2,3},{3,2},{4,5},{5,4},{6,7},{7,6},{8,9},{9,8},{10,11... | collective-permute-start | bytes 36872 | tf_op jit(solution)/shard_map/ppermute | solution.py:522
  29.2 7.3 %collective-permute-start.7 = (f32[120,128]{1,0:T(8,128)S(1)}, f32[120,128]{1,0:T(8,128)S(1)}, u32[]{:S(2)}, u32[]{:S(2)}) collective-permute-start(f32[120,128]{1,0:T(8,128)S(1)} %pad_maximum_fusion), channel_id=1, source_target_pairs={{0,28},{1,29},{2,30},{3,31},{4,8},{5,9},{6,10},{7,11},{8,4},{9,5},... | collective-permute-start | bytes 184328 | tf_op jit(solution)/shard_map/ppermute | solution.py:522
  32.9 4.9 %collective-permute-start.6 = (f32[120,128]{1,0:T(8,128)S(1)}, f32[120,128]{1,0:T(8,128)S(1)}, u32[]{:S(2)}, u32[]{:S(2)}) collective-permute-start(f32[120,128]{1,0:T(8,128)S(1)} %pad_maximum_fusion), channel_id=1, source_target_pairs={{0,4},{1,5},{2,6},{3,7},{4,0},{5,1},{6,2},{7,3},{8,12},{9,13},{10,... | collective-permute-start | bytes 184328 | tf_op jit(solution)/shard_map/ppermute | solution.py:522

commit v7 on v6

--- a/solution.py
+++ b/solution.py
@@ -518,9 +518,10 @@
 
 def exchanged(value, axis, wrap):
     heights, groups = lax.axis_size("height"), lax.axis_size("cols")
-    return [
-        lax.ppermute(value, ("height", "cols"), matching(heights, groups, axis, odd, wrap)) for odd in (False, True)
+    second, first = [
+        lax.ppermute(value, ("height", "cols"), matching(heights, groups, axis, odd, wrap)) for odd in (True, False)
     ]
+    return [first, second]
 
 
 LINES = 32
@@ -715,69 +716,80 @@
     )(cells, *lines)
 
 
+EDGE = 8
+TILES = 16
+
+
+def placed(parts, values, present, levels, across, along):
+    quarters = along // LANES
+    wide = across + 2 * EDGE
+    left, right = position()[:2]
+    lane = lax.broadcasted_iota(i32, (1, LANES), 1)
+    shift_q, shift_x = quarters.bit_length() - 1, across.bit_length() - 1
+    code = jnp.full((1, LANES), -1, i32)
+    for n, part in enumerate(parts):
+        owner = part[TILES : TILES + 1].astype(i32)
+        x = ((owner >> shift_q) & (across - 1)) + (EDGE + (n - 1) * across)
+        z = owner >> (shift_q + shift_x)
+        here = ((lane >> 4) == n) | ((lane >> 4) == n + 3)
+        here = here & (x >= EDGE - 2) & (x < EDGE + across + 2)
+        if n == 0:
+            here = here & left
+        if n == 2:
+            here = here & right
+        if present is not None:
+            here = here & present
+        code = jnp.where(here, (z * wide + x) * quarters + (owner & (quarters - 1)), code)
+    values = jnp.concatenate(values, axis=0)
+    high = values.astype(bf16)
+    low = (values - high.astype(f32)).astype(bf16)
+    values = jnp.concatenate([high, low, jnp.zeros((LANES - 6 * TILES, LANES), bf16)], axis=0)
+    spot = lax.broadcasted_iota(i32, (levels * wide, LANES), 0) * quarters
+    found = []
+    for k in range(quarters):
+        table = jnp.where(code == spot + k, 1.0, 0.0).astype(bf16)
+        found.append(jnp.dot(table, values, preferred_element_type=f32))
+    return found
+
+
+def low_of(is_even, one, two):
+    return jnp.where(is_even, two, one)
+
+
+def high_of(is_even, one, two):
+    return jnp.where(is_even, one, two)
+
+
+def across_and_along(mid):
+    wide, along = mid.shape
+    place = lax.broadcasted_iota(i32, (wide, along), 1)
+    total = pltpu.roll(mid, 1, 0) + pltpu.roll(mid, wide - 1, 0)
+    total = total + jnp.where(place > 0, pltpu.roll(mid, 1, 1), 0.0)
+    return total + jnp.where(place < along - 1, pltpu.roll(mid, along - 1, 1), 0.0)
+
+
 def right_side_kernel(
-    own_ref, shared_ref, side_a, side_b, height_a, height_b, cells_ref, scaling_ref, line_a, line_b, face_a, face_b,
-    rhs_ref, near_ref, far_ref, dots_ref, first, second,
+    own_ref, shared_ref, side_a, side_b, cells_ref, scaling_ref, line_a, line_b, rhs_ref, mid_ref, part_ref, ends_ref
 ):
     levels, across, along = scaling_ref.shape
-    edge = 8
-    wide = across + 2 * edge
-    inner = slice(edge, edge + across)
+    wide = across + 2 * EDGE
+    inner = slice(EDGE, EDGE + across)
     quarters = along // LANES
-    left, right, below, above, even, even_c = position()
-
-    def low_of(is_even, one, two):
-        return jnp.where(is_even, two, one)
-
-    def high_of(is_even, one, two):
-        return jnp.where(is_even, one, two)
-
-    lane = lax.broadcasted_iota(i32, (1, LANES), 1)
-    tiles = 16
-    shift_q, shift_x = quarters.bit_length() - 1, across.bit_length() - 1
-    for level, choose, present in ((0, low_of, below), (levels, None, None), (2 * levels, high_of, above)):
-        if choose is None:
-            parts = [low_of(even_c, side_a[...], side_b[...]), shared_ref[...], high_of(even_c, side_a[...], side_b[...])]
-            values = [parts[0][0:tiles], own_ref[...], parts[2][0:tiles]]
-        else:
-            block = [
-                choose(even, height_a[k * ROWS_OUT : (k + 1) * ROWS_OUT], height_b[k * ROWS_OUT : (k + 1) * ROWS_OUT])
-                for k in range(3)
-            ]
-            parts = [low_of(even_c, block[1], block[2]), block[0], high_of(even_c, block[1], block[2])]
-            values = [part[0:tiles] for part in parts]
-        code = jnp.full((1, LANES), -1, i32)
-        for n, part in enumerate(parts):
-            owner = part[tiles : tiles + 1].astype(i32)
-            x = ((owner >> shift_q) & (across - 1)) + (edge + (n - 1) * across)
-            z = owner >> (shift_q + shift_x)
-            here = ((lane >> 4) == n) | ((lane >> 4) == n + 3)
-            here = here & (x >= edge - 2) & (x < edge + across + 2)
-            if n == 0:
-                here = here & left
-            if n == 2:
-                here = here & right
-            if present is not None:
-                here = here & present
-            code = jnp.where(here, (z * wide + x) * quarters + (owner & (quarters - 1)), code)
-        values = jnp.concatenate(values, axis=0)
-        high = values.astype(bf16)
-        low = (values - high.astype(f32)).astype(bf16)
-        values = jnp.concatenate([high, low, jnp.zeros((LANES - 6 * tiles, LANES), bf16)], axis=0)
-        spot = lax.broadcasted_iota(i32, (levels * wide, LANES), 0) * quarters
-        for k in range(quarters):
-            table = jnp.where(code == spot + k, 1.0, 0.0).astype(bf16)
-            added = jnp.dot(table, values, preferred_element_type=f32)
-            for z in range(levels):
-                first[level + z, :, k * LANES : (k + 1) * LANES] = -added[z * wide : (z + 1) * wide]
-
-    second[:, 0:edge, :] = jnp.zeros((3 * levels, edge, along), f32)
-    second[:, edge + across :, :] = jnp.zeros((3 * levels, edge, along), f32)
+    left, right, _, _, _, even_c = position()
+    parts = [low_of(even_c, side_a[...], side_b[...]), shared_ref[...], high_of(even_c, side_a[...], side_b[...])]
+    values = [parts[0][0:TILES], own_ref[...], parts[2][0:TILES]]
+    for k, found in enumerate(placed(parts, values, None, levels, across, along)):
+        for z in range(levels):
+            mid_ref[z, :, k * LANES : (k + 1) * LANES] = -found[z * wide : (z + 1) * wide]
+    ends_ref[...] = jnp.zeros_like(ends_ref)
     for z in range(levels):
-        rhs = cells_ref[0, z] + first[levels + z, inner]
+        rhs = cells_ref[0, z] + mid_ref[z, inner]
         rhs_ref[z] = rhs
-        first[levels + z, inner] = scaling_ref[z] * rhs
-        for choose, start, present, beside_at in ((low_of, edge - 2, left, 1), (high_of, edge + across, right, 0)):
+        mid_ref[z, inner] = scaling_ref[z] * rhs
+        for choose, start, present, beside_at, end in (
+            (low_of, EDGE - 2, left, 1, EDGE - 1),
+            (high_of, EDGE + across, right, 0, EDGE),
+        ):
             for k in range(2):
                 x = slice(start + k, start + k + 1)
                 for q in range(quarters):
@@ -787,25 +799,71 @@
                         for kind in range(2)
                     ]
                     m = jnp.where(present, 1.0 / (6.0 + kinds[1]), 0.0)
-                    first[levels + z, x, part] += m * kinds[0]
+                    mid_ref[z, x, part] += m * kinds[0]
                     if k == beside_at:
-                        second[levels + z, x, part] = m
-    place = lax.broadcasted_iota(i32, (wide, along), 1)
-
-    def beside(ref, z):
-        mid = ref[z]
-        total = ref[z - 1] + ref[z + 1] + pltpu.roll(mid, 1, 0) + pltpu.roll(mid, wide - 1, 0)
-        total = total + jnp.where(place > 0, pltpu.roll(mid, 1, 1), 0.0)
-        return total + jnp.where(place < along - 1, pltpu.roll(mid, along - 1, 1), 0.0)
-
-    for z, choose, present in ((levels - 1, low_of, below), (2 * levels, high_of, above)):
+                        ends_ref[z, end : end + 1, part] = m
+    for z in range(levels):
+        total = across_and_along(mid_ref[z])
+        if z > 0:
+            total = total + mid_ref[z - 1]
+        if z < levels - 1:
+            total = total + mid_ref[z + 1]
+        part_ref[z] = total
+
+
+def right_side_of(own, shared, side, cells, scaling, lines):
+    levels, across, along = scaling.shape
+    vmem = pl.BlockSpec(memory_space=pltpu.VMEM)
+    whole = jax.ShapeDtypeStruct((levels, across + 2 * EDGE, along), f32)
+    return pl.pallas_call(
+        right_side_kernel,
+        out_shape=(
+            jax.ShapeDtypeStruct(scaling.shape, f32),
+            whole,
+            whole,
+            jax.ShapeDtypeStruct((levels, 2 * EDGE, along), f32),
+        ),
+        in_specs=[vmem] * 8,
+        out_specs=(vmem,) * 4,
+        cost_estimate=pl.CostEstimate(flops=10**9, bytes_accessed=4096, transcendentals=0),
+        compiler_params=pltpu.CompilerParams(vmem_limit_bytes=8 * MIB),
+        name="right_side",
+    )(own, shared, *side, cells, scaling, *lines)
+
+
+def products_kernel(
+    height_b, height_a, rhs_ref, mid_ref, part_ref, ends_ref, scaling_ref, face_a, face_b,
+    near_ref, far_ref, dots_ref, outer, second,
+):
+    levels, across, along = scaling_ref.shape
+    wide = across + 2 * EDGE
+    inner = slice(EDGE, EDGE + across)
+    quarters = along // LANES
+    _, _, below, above, even, even_c = position()
+    for start, choose, present in ((0, low_of, below), (levels, high_of, above)):
+        block = [
+            choose(even, height_a[k * ROWS_OUT : (k + 1) * ROWS_OUT], height_b[k * ROWS_OUT : (k + 1) * ROWS_OUT])
+            for k in range(3)
+        ]
+        parts = [low_of(even_c, block[1], block[2]), block[0], high_of(even_c, block[1], block[2])]
+        values = [part[0:TILES] for part in parts]
+        for k, found in enumerate(placed(parts, values, present, levels, across, along)):
+            for z in range(levels):
+                outer[start + z, :, k * LANES : (k + 1) * LANES] = -found[z * wide : (z + 1) * wide]
+    for n, (layer, far_layer, own_layer, choose, present) in enumerate(
+        ((levels - 1, levels - 2, 0, low_of, below), (levels, levels + 1, levels - 1, high_of, above))
+    ):
+        at = 0 if n == 0 else levels + 1
+        second[at, 0:EDGE] = jnp.zeros((EDGE, along), f32)
+        second[at, EDGE + across :] = jnp.zeros((EDGE, along), f32)
         part = [slice(n * across, (n + 1) * across) for n in range(3)]
-        near = beside(first, z)[inner] + choose(even, face_a[part[2]], face_b[part[2]])
-        second[z, inner] = jnp.where(present, choose(even, face_a[part[0]], face_b[part[0]]) * near, 0.0)
-        first[z, inner] += jnp.where(present, choose(even, face_a[part[1]], face_b[part[1]]), 0.0)
-        for n, x in enumerate((edge - 1, edge + across)):
+        near = across_and_along(outer[layer]) + outer[far_layer] + mid_ref[own_layer]
+        near = near[inner] + choose(even, face_a[part[2]], face_b[part[2]])
+        second[at, inner] = jnp.where(present, choose(even, face_a[part[0]], face_b[part[0]]) * near, 0.0)
+        outer[layer, inner] += jnp.where(present, choose(even, face_a[part[1]], face_b[part[1]]), 0.0)
+        for n, x in enumerate((EDGE - 1, EDGE + across)):
             line = slice(3 * across + n, 3 * across + n + 1)
-            first[z, x : x + 1] += jnp.where(present, choose(even, face_a[line], face_b[line]), 0.0)
+            outer[layer, x : x + 1] += jnp.where(present, choose(even, face_a[line], face_b[line]), 0.0)
 
     dots = [jnp.zeros((8, LANES), f32)] * 4
 
@@ -813,23 +871,27 @@
         value = jnp.sum(value.reshape(across // 8, 8, along), axis=0)
         return sum(value[:, k * LANES : (k + 1) * LANES] for k in range(quarters))
 
-    ends = (slice(0, edge), slice(edge + across, wide))
-    for z in range(levels, 2 * levels):
-        near = beside(first, z)
-        for end in ends:
-            second[z, end] = second[z, end] * near[end]
+    for z in range(levels):
+        near = part_ref[z]
+        if z == 0:
+            near = near + outer[levels - 1]
+        if z == levels - 1:
+            near = near + outer[levels]
+        second[z + 1, 0:EDGE] = ends_ref[z, 0:EDGE] * near[0:EDGE]
+        second[z + 1, EDGE + across :] = ends_ref[z, EDGE:] * near[EDGE + across :]
         near = near[inner]
-        scaled = scaling_ref[z - levels] * near
-        second[z, inner] = scaled
-        near_ref[z - levels] = near
-        start = first[z, inner]
-        dots[0] = dots[0] + folded(start * rhs_ref[z - levels])
+        scaled = scaling_ref[z] * near
+        second[z + 1, inner] = scaled
+        near_ref[z] = near
+        start = mid_ref[z, inner]
+        dots[0] = dots[0] + folded(start * rhs_ref[z])
         dots[1] = dots[1] + folded(start * near)
         dots[2] = dots[2] + folded(scaled * near)
-    for z in range(levels, 2 * levels):
-        far = beside(second, z)[inner]
-        far_ref[z - levels] = far
-        dots[3] = dots[3] + folded(second[z, inner] * far)
+    for z in range(levels):
+        far = (across_and_along(second[z + 1]) + second[z] + second[z + 2])[inner]
+        far_ref[z] = far
+        dots[3] = dots[3] + folded(second[z + 1, inner] * far)
+    lane = lax.broadcasted_iota(i32, (1, LANES), 1)
     line = jnp.zeros((1, LANES), f32)
     for k in range(4):
         total = jnp.sum(jnp.sum(dots[k], axis=0, keepdims=True), axis=1, keepdims=True)
@@ -837,19 +899,21 @@
     dots_ref[...] = jnp.broadcast_to(line, dots_ref.shape)
 
 
-def right_side_of(own, shared, side, height, cells, scaling, lines, faces, devices):
+def products_of(height, rhs, mid, part, ends, scaling, faces, devices):
     levels, across, along = scaling.shape
     vmem = pl.BlockSpec(memory_space=pltpu.VMEM)
-    whole = pltpu.VMEM((3 * levels, across + 16, along), f32)
     return pl.pallas_call(
-        right_side_kernel,
-        out_shape=(jax.ShapeDtypeStruct(scaling.shape, f32),) * 3 + (jax.ShapeDtypeStruct((devices, LANES), f32),),
-        in_specs=[vmem] * 12,
-        out_specs=(vmem,) * 4,
-        scratch_shapes=[whole] * 2,
+        products_kernel,
+        out_shape=(jax.ShapeDtypeStruct(scaling.shape, f32),) * 2 + (jax.ShapeDtypeStruct((devices, LANES), f32),),
+        in_specs=[vmem] * 9,
+        out_specs=(vmem,) * 3,
+        scratch_shapes=[
+            pltpu.VMEM((2 * levels, across + 2 * EDGE, along), f32),
+            pltpu.VMEM((levels + 2, across + 2 * EDGE, along), f32),
+        ],
         compiler_params=pltpu.CompilerParams(vmem_limit_bytes=16 * MIB),
-        name="right_side",
-    )(own, shared, *side, *height, cells, scaling, *lines, *faces)
+        name="products",
+    )(*reversed(height), rhs, mid, part, ends, scaling, *faces)
 
 
 def results_kernel(
@@ -953,9 +1017,8 @@
     near = exchanged(shared, "cols", True)
     parcel = jnp.concatenate([shared, *near, leaving.reshape(-1, LANES)], axis=0)
     parcels = exchanged(parcel, "height", True)
-    rhs, first, second, dots = right_side_of(
-        own, shared, near, parcels, cells, scaling, lines, faces, heights * groups
-    )
+    rhs, mid, part, ends = right_side_of(own, shared, near, cells, scaling, lines)
+    first, second, dots = products_of(parcels, rhs, mid, part, ends, scaling, faces, heights * groups)
     dots = lax.all_to_all(dots, ("height", "cols"), 0, 0, tiled=True)
     return results_of(keeps, places, dots, rhs, first, second, scaling, settled, parcels)
 

time: 51.2 us -> 50.3 us (0.982)
  starting transfers between devices: 13.8 us -> 13.2 us
    ppermute x6, starting transfers between devices: 8.55 us -> 7.3 us  [exchanged(): lax.ppermute(value, ('height', 'cols'), matching(heights, groups, axis, o...]
    pallas_call x0 -> x1, Pallas kernels: none -> 0.82 us  [products_of(): pl.pallas_call(products_kernel, out_shape=(jax.ShapeDtypeStruct(scaling.s...]
    ppermute x2, starting transfers between devices: 2.15 us -> 2.76 us  [on_device(): lax.ppermute(value, ('height', 'cols'), matching(heights, groups, 'height...]
    pallas_call x1, Pallas kernels: 1.02 us -> 0.43 us  [right_side_of(): pl.pallas_call(right_side_kernel, out_shape=(jax.ShapeDtypeStruct(scaling...]
  transfers between devices with their start and end apart: 10 -> 10, of which waited for: 4 -> 5; matrix products, arithmetic and copies ran while one was open for 0% -> 0% of each run, Pallas kernels for 29% -> 30%
where the time goes in v7:
time: 50.3 us; the launch traced here: 50 us
  Pallas kernels  17.2 us (34%)
  starting transfers between devices  13.2 us (26%)
  blocking collectives  10.8 us (21%)
  waiting for transfers between devices  7.05 us (14%)
  local copies, waits for them, and re-layouts  1 us (2%)
  between operations  0.78 us (2%)
    all_to_all x1, blocking collectives, on_device(): dots = lax.all_to_all(dots, ('height', 'cols'), 0, 0, tiled=True)  10.8 us
    pallas_call x1, Pallas kernels, particles(): pl.pallas_call(functools.partial(particles_kernel, rows=rows, cols=cols),...  9.99 us
    ppermute x6, starting transfers between devices, exchanged(): lax.ppermute(value, ('height', 'cols'), matching(heights, groups, axis, o...  7.3 us
    ppermute x6, waiting for transfers between devices, exchanged(): lax.ppermute(value, ('height', 'cols'), matching(heights, groups, axis, o...  6.09 us
    pallas_call x1, Pallas kernels, own_sums(): pl.pallas_call(functools.partial(own_kernel, rows=rows, cols=cols), out_s...  3.26 us
    ppermute x2, starting transfers between devices, on_device(): lax.ppermute(value, ('height', 'cols'), matching(heights, groups, 'cols',...  3.12 us
    ppermute x2, starting transfers between devices, on_device(): lax.ppermute(value, ('height', 'cols'), matching(heights, groups, 'height...  2.76 us
    pallas_call x1, Pallas kernels, results_of(): pl.pallas_call(results_kernel, out_shape=(particle, particle, field, fiel...  1.15 us
  transfers between devices with their start and end apart: 10, of which 5 were waited for; matrix products, arithmetic and copies ran while one was open for 0% of the time, Pallas kernels for 30%

profile of v7, /device:TPU:0, one launch (start us, length us, event | category | flops | bytes accessed | tf_op | source)
XLA Modules:
  0.0 50.0 jit_solution(8310871120712469632)
XLA Ops:
  0.6 0.0 copy-start.4
  0.6 0.0 copy-start.3
  0.7 0.0 copy-start.5
  0.7 0.0 copy-start
  0.7 0.0 copy-start.1
  0.7 0.0 copy-start.2
  0.7 0.0 copy-start.7
  0.7 0.0 copy-start.6
  0.7 0.0 copy-start.8
  0.7 0.6 %copy-done.4 = s32[9,2,8]{0,2,1:T(8,128)S(1)} copy-done((s32[9,2,8]{0,2,1:T(8,128)S(1)}, s32[9,2,8]{0,2,1:T(8,128)}, u32[]{:S(2)}) %copy-start.4) | copy-done | bytes 600
  1.3 0.1 copy-done.3
  1.4 0.0 copy-done.5
  1.4 0.2 copy-done
  1.6 0.1 copy-done.1
  1.7 0.0 copy-done.2
  1.7 0.0 copy-done.7
  1.7 0.0 copy-done.6
  1.7 0.0 copy-done.8
  1.7 0.2 pack.1
  1.9 0.5 collective-permute-start
  2.4 2.6 %collective-permute-start.1 = (f32[64,128]{1,0:T(8,128)S(1)}, f32[64,128]{1,0:T(8,128)S(1)}, u32[]{:S(2)}, u32[]{:S(2)}) collective-permute-start(f32[64,128]{1,0:T(8,128)S(1)} %get-tuple-element.44), channel_id=1, source_target_pairs={{0,3},{1,2},{2,1},{3,0},{4,7},{5,6},{6,5},{7,4},{8,11},{9,10},{10,... | collective-permute-start | bytes 98312 | tf_op jit(solution)/shard_map/ppermute | solution.py:1001
  5.0 0.7 %marks.1 = (f32[8,8,128]{2,1,0:T(8,128)S(1)}, f32[8,128]{1,0:T(8,128)S(1)}, f32[8,8,128]{2,1,0:T(8,128)S(1)}, f32[16,128]{1,0:T(8,128)S(1)}, f32[1,128]{1,0:T(1,128)S(1)}) custom-call(s32[1,128]{1,0:T(1,128)S(1)} %get-tuple-element.38.ints_ref, f32[2,2,64,512]{3,2,1,0:T(8,128)S(1)} %get-tuple-element.39.cells_ref), custom_call_target="tpu_custom_call" | custom-call | flops 1000000000 | bytes 4096 | tf_op jit(solution)/shard_map/marks/pallas_call | solution.py:476
  5.7 0.0 collective-permute-done.line_a
  5.7 1.0 %collective-permute-done.1.line_b = f32[64,128]{1,0:T(8,128)S(1)} collective-permute-done((f32[64,128]{1,0:T(8,128)S(1)}, f32[64,128]{1,0:T(8,128)S(1)}, u32[]{:S(2)}, u32[]{:S(2)}) %collective-permute-start.1) | collective-permute-done | bytes 32800 | tf_op jit(solution)/shard_map/ppermute | solution.py:1001
  6.7 1.7 %collective-permute-start.2 = (f32[152,128]{1,0:T(8,128)S(1)}, f32[152,128]{1,0:T(8,128)S(1)}, u32[]{:S(2)}, u32[]{:S(2)}) collective-permute-start(f32[152,128]{1,0:T(8,128)S(1)} %merge.1.own_ref), channel_id=1, source_target_pairs={{0,4},{1,5},{2,6},{3,7},{4,0},{5,1},{6,2},{7,3},{8,12},{9,13},{10,... | collective-permute-start | bytes 233480 | tf_op jit(solution)/shard_map/ppermute | solution.py:522
  8.4 0.2 collective-permute-start.3
  8.5 3.3 %own_sums.1 = (f32[2,12,8,128]{3,2,1,0:T(8,128)S(1)}, bf16[2,3,128,128]{3,2,1,0:T(8,128)(2,1)S(1)}, bf16[2,12,16,128]{3,2,1,0:T(8,128)(2,1)S(1)}, f32[2,5,16,256]{3,2,1,0:T(8,128)S(1)}) custom-call(f32[152,128]{1,0:T(8,128)S(1)} %merge.1.own_ref), custom_call_target="tpu_custom_call" | custom-call | flops 4000000000 | bytes 4096 | tf_op jit(solution)/shard_map/own_sums/pallas_call | solution.py:270
  11.8 0.3 faces.1
  12.1 0.2 collective-permute-done.2.first_ref
  12.3 0.0 collective-permute-done.3.second_ref
  12.3 2.8 %collective-permute-start.8 = (f32[200,512]{1,0:T(8,128)S(1)}, f32[200,512]{1,0:T(8,128)S(1)}, u32[]{:S(2)}, u32[]{:S(2)}) collective-permute-start(f32[200,512]{1,0:T(8,128)S(1)} %get-tuple-element.67), channel_id=1, source_target_pairs={{0,4},{1,5},{2,6},{3,7},{4,0},{5,1},{6,2},{7,3},{8,12},{9,13},{10,... | collective-permute-start | bytes 1228808 | tf_op jit(solution)/shard_map/ppermute | solution.py:1012
  15.1 0.0 collective-permute-start.9
  15.1 10.0 %particles.1 = (f32[2,8,8,128]{3,2,1,0:T(8,128)S(1)}, f32[6,8,128]{2,1,0:T(8,128)S(1)}) custom-call(f32[8,8,128]{2,1,0:T(8,128)S(1)} %get-tuple-element.42.picks_ref, f32[152,128]{1,0:T(8,128)S(1)} %collective-permute-done.2.first_ref, f32[152,128]{1,0:T(8,128)S(1)} %collective-permute-done.3.second_ref, f32[2,12,8,128]{3,2,1,0:T(8,128)S(1)} %get-tuple-element.52.own_ref, ...), custom_call_target="tpu_custom_call" | custom-call | flops 10000000000 | bytes 4096 | tf_op jit(solution)/shard_map/particles/pallas_call | solution.py:388
  25.1 0.4 deposits.1
  25.5 0.6 %collective-permute-start.4 = (f32[24,128]{1,0:T(8,128)S(1)}, f32[24,128]{1,0:T(8,128)S(1)}, u32[]{:S(2)}, u32[]{:S(2)}) collective-permute-start(f32[24,128]{1,0:T(8,128)S(1)} %get-tuple-element.59.shared_ref), channel_id=1, source_target_pairs={{0,1},{1,0},{2,3},{3,2},{4,5},{5,4},{6,7},{7,6},{8,9},{9,8},{10,11... | collective-permute-start | bytes 36872 | tf_op jit(solution)/shard_map/ppermute | solution.py:522
  26.0 1.2 %collective-permute-start.5 = (f32[24,128]{1,0:T(8,128)S(1)}, f32[24,128]{1,0:T(8,128)S(1)}, u32[]{:S(2)}, u32[]{:S(2)}) collective-permute-start(f32[24,128]{1,0:T(8,128)S(1)} %get-tuple-element.59.shared_ref), channel_id=1, source_target_pairs={{0,3},{1,2},{2,1},{3,0},{4,7},{5,6},{6,5},{7,4},{8,11},{9,10},{10,... | collective-permute-start | bytes 36872 | tf_op jit(solution)/shard_map/ppermute | solution.py:522
  27.2 0.0 collective-permute-done.4.side_a
  27.2 1.9 %collective-permute-done.5.side_b = f32[24,128]{1,0:T(8,128)S(1)} collective-permute-done((f32[24,128]{1,0:T(8,128)S(1)}, f32[24,128]{1,0:T(8,128)S(1)}, u32[]{:S(2)}, u32[]{:S(2)}) %collective-permute-start.5) | collective-permute-done | bytes 12320 | tf_op jit(solution)/shard_map/ppermute | solution.py:522
  29.2 3.7 %collective-permute-start.6 = (f32[120,128]{1,0:T(8,128)S(1)}, f32[120,128]{1,0:T(8,128)S(1)}, u32[]{:S(2)}, u32[]{:S(2)}) collective-permute-start(f32[120,128]{1,0:T(8,128)S(1)} %pad_maximum_fusion), channel_id=1, source_target_pairs={{0,28},{1,29},{2,30},{3,31},{4,8},{5,9},{6,10},{7,11},{8,4},{9,5},... | collective-permute-start | bytes 184328 | tf_op jit(solution)/shard_map/ppermute | solution.py:522
  32.9 0.0 collective-permute-start.7
  32.9 0.4 right_side.1
  33.3 2.9 %collective-permute-done.6.height_b = f32[120,128]{1,0:T(8,128)S(1)} collective-permute-done((f32[120,128]{1,0:T(8,128)S(1)}, f32[120,128]{1,0:T(8,128)S(1)}, u32[]{:S(2)}, u32[]{:S(2)}) %collective-permute-start.6) | collective-permute-done | bytes 61472 | tf_op jit(solution)/shard_map/ppermute | solution.py:522
  36.2 1.1 %collective-permute-done.7.height_a = f32[120,128]{1,0:T(8,128)S(1)} collective-permute-done((f32[120,128]{1,0:T(8,128)S(1)}, f32[120,128]{1,0:T(8,128)S(1)}, u32[]{:S(2)}, u32[]{:S(2)}) %collective-permute-start.7) | collective-permute-done | bytes 61472 | tf_op jit(solution)/shard_map/ppermute | solution.py:522
  37.3 0.0 collective-permute-done.8.face_a
  37.3 0.0 collective-permute-done.9.face_b
  37.3 0.8 %products.1 = (f32[2,64,512]{2,1,0:T(8,128)S(1)}, f32[2,64,512]{2,1,0:T(8,128)S(1)}, f32[32,128]{1,0:T(8,128)S(1)}) custom-call(f32[120,128]{1,0:T(8,128)S(1)} %collective-permute-done.6.height_b, f32[120,128]{1,0:T(8,128)S(1)} %collective-permute-done.7.height_a, f32[2,64,512]{2,1,0:T(8,128)S(1)} %get-tuple-element.63.rhs_ref, ...), custom_call_target="tpu_custom_call" | custom-call | tf_op jit(solution)/shard_map/products/pallas_call | solution.py:905
  38.1 10.8 %all_to_all.11 = f32[32,1,128]{2,1,0:T(1,128)S(1)} all-to-all(f32[32,1,128]{2,1,0:T(1,128)S(1)} %bitcast.8), channel_id=1, replica_groups=mesh['height'=8,'cols'=4] {'height','cols'}, dimensions={0} | all-to-all | bytes 32768 | tf_op jit(solution)/shard_map/all_to_all | solution.py:1022
  48.9 1.2 %results.1 = (f32[3,2,8,128]{3,2,1,0:T(8,128)}, f32[3,2,8,128]{3,2,1,0:T(8,128)}, f32[2,64,512]{2,1,0:T(8,128)}, f32[2,64,512]{2,1,0:T(8,128)}) custom-call(f32[8,128]{1,0:T(8,128)S(1)} %get-tuple-element.40.keeps_ref, f32[8,8,128]{2,1,0:T(8,128)S(1)} %get-tuple-element.41.places_ref, f32[32,128]{1,0:T(8,128)S(1)} %bitcast.6, ...), custom_call_target="tpu_custom_call" | custom-call | tf_op jit(solution)/shard_map/results/pallas_call | solution.py:976
  (3 shorter events, 0.0 us)
Async XLA Ops:
  0.6 0.7 %copy-start.4 = (s32[9,2,8]{0,2,1:T(8,128)S(1)}, s32[9,2,8]{0,2,1:T(8,128)}, u32[]{:S(2)}) copy-start(s32[9,2,8]{0,2,1:T(8,128)} %param.11) | copy-start | bytes 1732
  0.6 0.7 %copy-start.3 = (f32[3,2,8,128]{3,2,1,0:T(8,128)S(1)}, f32[3,2,8,128]{3,2,1,0:T(8,128)}, u32[]{:S(2)}) copy-start(f32[3,2,8,128]{3,2,1,0:T(8,128)} %velocities_ref.1) | copy-start | bytes 73732
  0.7 0.7 %copy-start.5 = (s32[2,8,128]{2,1,0:T(8,128)S(1)}, s32[2,8,128]{2,1,0:T(8,128)}, u32[]{:S(2)}) copy-start(s32[2,8,128]{2,1,0:T(8,128)} %slots_in.1) | copy-start | bytes 24580
  0.7 1.0 %copy-start = (f32[2,64,512]{2,1,0:T(8,128)S(1)}, f32[2,64,512]{2,1,0:T(8,128)}, u32[]{:S(2)}) copy-start(f32[2,64,512]{2,1,0:T(8,128)} %gas_ref.1) | copy-start | bytes 786436
  0.7 1.0 %copy-start.1 = (f32[2,64,512]{2,1,0:T(8,128)S(1)}, f32[2,64,512]{2,1,0:T(8,128)}, u32[]{:S(2)}) copy-start(f32[2,64,512]{2,1,0:T(8,128)} %diagonal_ref.1) | copy-start | bytes 786436
  0.7 1.0 %copy-start.2 = (f32[3,2,8,128]{3,2,1,0:T(8,128)S(1)}, f32[3,2,8,128]{3,2,1,0:T(8,128)}, u32[]{:S(2)}) copy-start(f32[3,2,8,128]{3,2,1,0:T(8,128)} %positions_ref.1) | copy-start | bytes 73732
  0.7 1.0 %copy-start.7 = (s32[2,8]{1,0:T(2,128)S(1)}, s32[2,8]{1,0:T(2,128)}, u32[]{:S(2)}) copy-start(s32[2,8]{1,0:T(2,128)} %owners_ref.1) | copy-start | bytes 196
  0.7 1.0 %copy-start.6 = (s32[2,8]{1,0:T(2,128)S(1)}, s32[2,8]{1,0:T(2,128)}, u32[]{:S(2)}) copy-start(s32[2,8]{1,0:T(2,128)} %exits_ref.1) | copy-start | bytes 196
  0.7 1.0 %copy-start.8 = (s32[1,8]{1,0:T(1,128)S(1)}, s32[1,8]{1,0:T(1,128)}, u32[]{:S(2)}) copy-start(s32[1,8]{1,0:T(1,128)} %inlets_ref.1) | copy-start | bytes 100
  1.9 3.8 %collective-permute-start = (f32[64,128]{1,0:T(8,128)S(1)}, f32[64,128]{1,0:T(8,128)S(1)}, u32[]{:S(2)}, u32[]{:S(2)}) collective-permute-start(f32[64,128]{1,0:T(8,128)S(1)} %get-tuple-element.43), channel_id=1, source_target_pairs={{0,1},{1,0},{2,3},{3,2},{4,5},{5,4},{6,7},{7,6},{8,9},{9,8},{10,11... | collective-permute-start | bytes 98312 | tf_op jit(solution)/shard_map/ppermute | solution.py:1001
  2.4 4.3 %collective-permute-start.1 = (f32[64,128]{1,0:T(8,128)S(1)}, f32[64,128]{1,0:T(8,128)S(1)}, u32[]{:S(2)}, u32[]{:S(2)}) collective-permute-start(f32[64,128]{1,0:T(8,128)S(1)} %get-tuple-element.44), channel_id=1, source_target_pairs={{0,3},{1,2},{2,1},{3,0},{4,7},{5,6},{6,5},{7,4},{8,11},{9,10},{10,... | collective-permute-start | bytes 98312 | tf_op jit(solution)/shard_map/ppermute | solution.py:1001
  6.7 5.6 %collective-permute-start.2 = (f32[152,128]{1,0:T(8,128)S(1)}, f32[152,128]{1,0:T(8,128)S(1)}, u32[]{:S(2)}, u32[]{:S(2)}) collective-permute-start(f32[152,128]{1,0:T(8,128)S(1)} %merge.1.own_ref), channel_id=1, source_target_pairs={{0,4},{1,5},{2,6},{3,7},{4,0},{5,1},{6,2},{7,3},{8,12},{9,13},{10,... | collective-permute-start | bytes 233480 | tf_op jit(solution)/shard_map/ppermute | solution.py:522
  8.4 3.9 %collective-permute-start.3 = (f32[152,128]{1,0:T(8,128)S(1)}, f32[152,128]{1,0:T(8,128)S(1)}, u32[]{:S(2)}, u32[]{:S(2)}) collective-permute-start(f32[152,128]{1,0:T(8,128)S(1)} %merge.1.own_ref), channel_id=1, source_target_pairs={{0,1},{1,0},{2,3},{3,2},{4,8},{5,9},{6,10},{7,11},{8,4},{9,5},{10,... | collective-permute-start | bytes 233480 | tf_op jit(solution)/shard_map/ppermute | solution.py:522
  12.3 25.0 %collective-permute-start.8 = (f32[200,512]{1,0:T(8,128)S(1)}, f32[200,512]{1,0:T(8,128)S(1)}, u32[]{:S(2)}, u32[]{:S(2)}) collective-permute-start(f32[200,512]{1,0:T(8,128)S(1)} %get-tuple-element.67), channel_id=1, source_target_pairs={{0,4},{1,5},{2,6},{3,7},{4,0},{5,1},{6,2},{7,3},{8,12},{9,13},{10,... | collective-permute-start | bytes 1228808 | tf_op jit(solution)/shard_map/ppermute | solution.py:1012
  15.1 22.2 %collective-permute-start.9 = (f32[200,512]{1,0:T(8,128)S(1)}, f32[200,512]{1,0:T(8,128)S(1)}, u32[]{:S(2)}, u32[]{:S(2)}) collective-permute-start(f32[200,512]{1,0:T(8,128)S(1)} %get-tuple-element.68), channel_id=1, source_target_pairs={{0,1},{1,0},{2,3},{3,2},{4,8},{5,9},{6,10},{7,11},{8,4},{9,5},{10,... | collective-permute-start | bytes 1228808 | tf_op jit(solution)/shard_map/ppermute | solution.py:1012
  25.5 1.8 %collective-permute-start.4 = (f32[24,128]{1,0:T(8,128)S(1)}, f32[24,128]{1,0:T(8,128)S(1)}, u32[]{:S(2)}, u32[]{:S(2)}) collective-permute-start(f32[24,128]{1,0:T(8,128)S(1)} %get-tuple-element.59.shared_ref), channel_id=1, source_target_pairs={{0,1},{1,0},{2,3},{3,2},{4,5},{5,4},{6,7},{7,6},{8,9},{9,8},{10,11... | collective-permute-start | bytes 36872 | tf_op jit(solution)/shard_map/ppermute | solution.py:522
  26.0 3.1 %collective-permute-start.5 = (f32[24,128]{1,0:T(8,128)S(1)}, f32[24,128]{1,0:T(8,128)S(1)}, u32[]{:S(2)}, u32[]{:S(2)}) collective-permute-start(f32[24,128]{1,0:T(8,128)S(1)} %get-tuple-element.59.shared_ref), channel_id=1, source_target_pairs={{0,3},{1,2},{2,1},{3,0},{4,7},{5,6},{6,5},{7,4},{8,11},{9,10},{10,... | collective-permute-start | bytes 36872 | tf_op jit(solution)/shard_map/ppermute | solution.py:522
  29.2 7.0 %collective-permute-start.6 = (f32[120,128]{1,0:T(8,128)S(1)}, f32[120,128]{1,0:T(8,128)S(1)}, u32[]{:S(2)}, u32[]{:S(2)}) collective-permute-start(f32[120,128]{1,0:T(8,128)S(1)} %pad_maximum_fusion), channel_id=1, source_target_pairs={{0,28},{1,29},{2,30},{3,31},{4,8},{5,9},{6,10},{7,11},{8,4},{9,5},... | collective-permute-start | bytes 184328 | tf_op jit(solution)/shard_map/ppermute | solution.py:522
  32.9 4.4 %collective-permute-start.7 = (f32[120,128]{1,0:T(8,128)S(1)}, f32[120,128]{1,0:T(8,128)S(1)}, u32[]{:S(2)}, u32[]{:S(2)}) collective-permute-start(f32[120,128]{1,0:T(8,128)S(1)} %pad_maximum_fusion), channel_id=1, source_target_pairs={{0,4},{1,5},{2,6},{3,7},{4,0},{5,1},{6,2},{7,3},{8,12},{9,13},{10,... | collective-permute-start | bytes 184328 | tf_op jit(solution)/shard_map/ppermute | solution.py:522

commit v8 on v7

--- a/solution.py
+++ b/solution.py
@@ -718,17 +718,41 @@
 
 EDGE = 8
 TILES = 16
-
-
-def placed(parts, values, present, levels, across, along):
+PARCEL = 3 * TILES + 8
+
+
+def parcel_kernel(shared_ref, side_a, side_b, leaving_ref, parcel_ref):
+    refs = (shared_ref, side_a, side_b)
+    for k, ref in enumerate(refs):
+        parcel_ref[k * TILES : (k + 1) * TILES] = ref[0:TILES]
+    rows = [ref[TILES : TILES + 1] for ref in refs]
+    parcel_ref[3 * TILES : PARCEL] = jnp.concatenate([*rows, jnp.zeros((5, LANES), f32)], axis=0)
+    count = leaving_ref.shape[1]
+    for d in range(6):
+        parcel_ref[PARCEL + d * count : PARCEL + (d + 1) * count] = leaving_ref[d]
+
+
+def parcel_of(shared, side, leaving):
+    vmem = pl.BlockSpec(memory_space=pltpu.VMEM)
+    return pl.pallas_call(
+        parcel_kernel,
+        out_shape=jax.ShapeDtypeStruct((PARCEL + leaving.shape[0] * leaving.shape[1], LANES), f32),
+        in_specs=[vmem] * 4,
+        out_specs=vmem,
+        compiler_params=pltpu.CompilerParams(vmem_limit_bytes=4 * MIB),
+        name="parcel",
+    )(shared, *side, leaving)
+
+
+def placed(owners, values, present, levels, across, along):
     quarters = along // LANES
     wide = across + 2 * EDGE
     left, right = position()[:2]
     lane = lax.broadcasted_iota(i32, (1, LANES), 1)
     shift_q, shift_x = quarters.bit_length() - 1, across.bit_length() - 1
     code = jnp.full((1, LANES), -1, i32)
-    for n, part in enumerate(parts):
-        owner = part[TILES : TILES + 1].astype(i32)
+    for n, owner in enumerate(owners):
+        owner = owner.astype(i32)
         x = ((owner >> shift_q) & (across - 1)) + (EDGE + (n - 1) * across)
         z = owner >> (shift_q + shift_x)
         here = ((lane >> 4) == n) | ((lane >> 4) == n + 3)
@@ -778,7 +802,8 @@
     left, right, _, _, _, even_c = position()
     parts = [low_of(even_c, side_a[...], side_b[...]), shared_ref[...], high_of(even_c, side_a[...], side_b[...])]
     values = [parts[0][0:TILES], own_ref[...], parts[2][0:TILES]]
-    for k, found in enumerate(placed(parts, values, None, levels, across, along)):
+    owners = [part[TILES : TILES + 1] for part in parts]
+    for k, found in enumerate(placed(owners, values, None, levels, across, along)):
         for z in range(levels):
             mid_ref[z, :, k * LANES : (k + 1) * LANES] = -found[z * wide : (z + 1) * wide]
     ends_ref[...] = jnp.zeros_like(ends_ref)
@@ -841,13 +866,12 @@
     quarters = along // LANES
     _, _, below, above, even, even_c = position()
     for start, choose, present in ((0, low_of, below), (levels, high_of, above)):
-        block = [
-            choose(even, height_a[k * ROWS_OUT : (k + 1) * ROWS_OUT], height_b[k * ROWS_OUT : (k + 1) * ROWS_OUT])
-            for k in range(3)
-        ]
-        parts = [low_of(even_c, block[1], block[2]), block[0], high_of(even_c, block[1], block[2])]
-        values = [part[0:TILES] for part in parts]
-        for k, found in enumerate(placed(parts, values, present, levels, across, along)):
+        block = choose(even, height_a[0:PARCEL], height_b[0:PARCEL])
+        tiles = [block[k * TILES : (k + 1) * TILES] for k in range(3)]
+        rows = [block[3 * TILES + k : 3 * TILES + k + 1] for k in range(3)]
+        values = [low_of(even_c, tiles[1], tiles[2]), tiles[0], high_of(even_c, tiles[1], tiles[2])]
+        owners = [low_of(even_c, rows[1], rows[2]), rows[0], high_of(even_c, rows[1], rows[2])]
+        for k, found in enumerate(placed(owners, values, present, levels, across, along)):
             for z in range(levels):
                 outer[start + z, :, k * LANES : (k + 1) * LANES] = -found[z * wide : (z + 1) * wide]
     for n, (layer, far_layer, own_layer, choose, present) in enumerate(
@@ -931,7 +955,7 @@
             for d in range(3):
                 positions[d, r, c : c + 1] = kept[d : d + 1]
                 velocities[d, r, c : c + 1] = kept[d + 3 : d + 4]
-    start = 3 * ROWS_OUT
+    start = PARCEL
     for d in range(6):
         block = slice(start + d * cols, start + (d + 1) * cols)
         tiles = jnp.where(even, height_b[block], height_a[block])
@@ -1015,7 +1039,7 @@
     settled, leaving = particles(picks, *beside, own_parts)
     own, shared = deposits(settled, slots, weights, owners)
     near = exchanged(shared, "cols", True)
-    parcel = jnp.concatenate([shared, *near, leaving.reshape(-1, LANES)], axis=0)
+    parcel = parcel_of(shared, near, leaving)
     parcels = exchanged(parcel, "height", True)
     rhs, mid, part, ends = right_side_of(own, shared, near, cells, scaling, lines)
     first, second, dots = products_of(parcels, rhs, mid, part, ends, scaling, faces, heights * groups)

time: 50.3 us -> 50.2 us (level)
  no operation moved by 1% of the time
where the time goes in v8:
time: 50.2 us; the launch traced here: 50 us
  Pallas kernels  17.2 us (34%)
  starting transfers between devices  13.2 us (26%)
  blocking collectives  11 us (22%)
  waiting for transfers between devices  6.79 us (14%)
  local copies, waits for them, and re-layouts  1 us (2%)
  between operations  0.78 us (2%)
    all_to_all x1, blocking collectives, on_device(): dots = lax.all_to_all(dots, ('height', 'cols'), 0, 0, tiled=True)  11 us
    pallas_call x1, Pallas kernels, particles(): pl.pallas_call(functools.partial(particles_kernel, rows=rows, cols=cols),...  9.99 us
    ppermute x6, starting transfers between devices, exchanged(): lax.ppermute(value, ('height', 'cols'), matching(heights, groups, axis, o...  7.31 us
    ppermute x6, waiting for transfers between devices, exchanged(): lax.ppermute(value, ('height', 'cols'), matching(heights, groups, axis, o...  5.82 us
    pallas_call x1, Pallas kernels, own_sums(): pl.pallas_call(functools.partial(own_kernel, rows=rows, cols=cols), out_s...  3.26 us
    ppermute x2, starting transfers between devices, on_device(): lax.ppermute(value, ('height', 'cols'), matching(heights, groups, 'cols',...  3.12 us
    ppermute x2, starting transfers between devices, on_device(): lax.ppermute(value, ('height', 'cols'), matching(heights, groups, 'height...  2.76 us
    pallas_call x1, Pallas kernels, results_of(): pl.pallas_call(results_kernel, out_shape=(particle, particle, field, fiel...  1.15 us
  transfers between devices with their start and end apart: 10, of which 5 were waited for; matrix products, arithmetic and copies ran while one was open for 0% of the time, Pallas kernels for 30%

profile of v8, /device:TPU:0, one launch (start us, length us, event | category | flops | bytes accessed | tf_op | source)
XLA Modules:
  0.0 50.0 jit_solution(16853603575725997844)
XLA Ops:
  0.6 0.0 copy-start.4
  0.6 0.0 copy-start.3
  0.7 0.0 copy-start.5
  0.7 0.0 copy-start
  0.7 0.0 copy-start.1
  0.7 0.0 copy-start.2
  0.7 0.0 copy-start.7
  0.7 0.0 copy-start.6
  0.7 0.0 copy-start.8
  0.7 0.6 %copy-done.4 = s32[9,2,8]{0,2,1:T(8,128)S(1)} copy-done((s32[9,2,8]{0,2,1:T(8,128)S(1)}, s32[9,2,8]{0,2,1:T(8,128)}, u32[]{:S(2)}) %copy-start.4) | copy-done | bytes 600
  1.3 0.1 copy-done.3
  1.4 0.0 copy-done.5
  1.4 0.2 copy-done
  1.6 0.1 copy-done.1
  1.7 0.0 copy-done.2
  1.7 0.0 copy-done.7
  1.7 0.0 copy-done.6
  1.7 0.0 copy-done.8
  1.7 0.2 pack.1
  1.9 0.5 collective-permute-start
  2.4 2.6 %collective-permute-start.1 = (f32[64,128]{1,0:T(8,128)S(1)}, f32[64,128]{1,0:T(8,128)S(1)}, u32[]{:S(2)}, u32[]{:S(2)}) collective-permute-start(f32[64,128]{1,0:T(8,128)S(1)} %get-tuple-element.44), channel_id=1, source_target_pairs={{0,3},{1,2},{2,1},{3,0},{4,7},{5,6},{6,5},{7,4},{8,11},{9,10},{10,... | collective-permute-start | bytes 98312 | tf_op jit(solution)/shard_map/ppermute | solution.py:1025
  5.0 0.7 %marks.1 = (f32[8,8,128]{2,1,0:T(8,128)S(1)}, f32[8,128]{1,0:T(8,128)S(1)}, f32[8,8,128]{2,1,0:T(8,128)S(1)}, f32[16,128]{1,0:T(8,128)S(1)}, f32[1,128]{1,0:T(1,128)S(1)}) custom-call(s32[1,128]{1,0:T(1,128)S(1)} %get-tuple-element.38.ints_ref, f32[2,2,64,512]{3,2,1,0:T(8,128)S(1)} %get-tuple-element.39.cells_ref), custom_call_target="tpu_custom_call" | custom-call | flops 1000000000 | bytes 4096 | tf_op jit(solution)/shard_map/marks/pallas_call | solution.py:476
  5.7 0.0 collective-permute-done.line_a
  5.7 1.0 %collective-permute-done.1.line_b = f32[64,128]{1,0:T(8,128)S(1)} collective-permute-done((f32[64,128]{1,0:T(8,128)S(1)}, f32[64,128]{1,0:T(8,128)S(1)}, u32[]{:S(2)}, u32[]{:S(2)}) %collective-permute-start.1) | collective-permute-done | bytes 32800 | tf_op jit(solution)/shard_map/ppermute | solution.py:1025
  6.7 1.7 %collective-permute-start.2 = (f32[152,128]{1,0:T(8,128)S(1)}, f32[152,128]{1,0:T(8,128)S(1)}, u32[]{:S(2)}, u32[]{:S(2)}) collective-permute-start(f32[152,128]{1,0:T(8,128)S(1)} %merge.1.own_ref), channel_id=1, source_target_pairs={{0,4},{1,5},{2,6},{3,7},{4,0},{5,1},{6,2},{7,3},{8,12},{9,13},{10,... | collective-permute-start | bytes 233480 | tf_op jit(solution)/shard_map/ppermute | solution.py:522
  8.4 0.2 collective-permute-start.3
  8.5 3.3 %own_sums.1 = (f32[2,12,8,128]{3,2,1,0:T(8,128)S(1)}, bf16[2,3,128,128]{3,2,1,0:T(8,128)(2,1)S(1)}, bf16[2,12,16,128]{3,2,1,0:T(8,128)(2,1)S(1)}, f32[2,5,16,256]{3,2,1,0:T(8,128)S(1)}) custom-call(f32[152,128]{1,0:T(8,128)S(1)} %merge.1.own_ref), custom_call_target="tpu_custom_call" | custom-call | flops 4000000000 | bytes 4096 | tf_op jit(solution)/shard_map/own_sums/pallas_call | solution.py:270
  11.8 0.3 faces.1
  12.1 0.2 collective-permute-done.2.first_ref
  12.3 0.0 collective-permute-done.3.second_ref
  12.3 2.8 %collective-permute-start.8 = (f32[200,512]{1,0:T(8,128)S(1)}, f32[200,512]{1,0:T(8,128)S(1)}, u32[]{:S(2)}, u32[]{:S(2)}) collective-permute-start(f32[200,512]{1,0:T(8,128)S(1)} %get-tuple-element.67), channel_id=1, source_target_pairs={{0,4},{1,5},{2,6},{3,7},{4,0},{5,1},{6,2},{7,3},{8,12},{9,13},{10,... | collective-permute-start | bytes 1228808 | tf_op jit(solution)/shard_map/ppermute | solution.py:1036
  15.1 0.0 collective-permute-start.9
  15.1 10.0 %particles.1 = (f32[2,8,8,128]{3,2,1,0:T(8,128)S(1)}, f32[6,8,128]{2,1,0:T(8,128)S(1)}) custom-call(f32[8,8,128]{2,1,0:T(8,128)S(1)} %get-tuple-element.42.picks_ref, f32[152,128]{1,0:T(8,128)S(1)} %collective-permute-done.2.first_ref, f32[152,128]{1,0:T(8,128)S(1)} %collective-permute-done.3.second_ref, f32[2,12,8,128]{3,2,1,0:T(8,128)S(1)} %get-tuple-element.52.own_ref, ...), custom_call_target="tpu_custom_call" | custom-call | flops 10000000000 | bytes 4096 | tf_op jit(solution)/shard_map/particles/pallas_call | solution.py:388
  25.1 0.4 deposits.1
  25.5 0.6 %collective-permute-start.4 = (f32[24,128]{1,0:T(8,128)S(1)}, f32[24,128]{1,0:T(8,128)S(1)}, u32[]{:S(2)}, u32[]{:S(2)}) collective-permute-start(f32[24,128]{1,0:T(8,128)S(1)} %get-tuple-element.59.shared_ref), channel_id=1, source_target_pairs={{0,1},{1,0},{2,3},{3,2},{4,5},{5,4},{6,7},{7,6},{8,9},{9,8},{10,11... | collective-permute-start | bytes 36872 | tf_op jit(solution)/shard_map/ppermute | solution.py:522
  26.0 1.2 %collective-permute-start.5 = (f32[24,128]{1,0:T(8,128)S(1)}, f32[24,128]{1,0:T(8,128)S(1)}, u32[]{:S(2)}, u32[]{:S(2)}) collective-permute-start(f32[24,128]{1,0:T(8,128)S(1)} %get-tuple-element.59.shared_ref), channel_id=1, source_target_pairs={{0,3},{1,2},{2,1},{3,0},{4,7},{5,6},{6,5},{7,4},{8,11},{9,10},{10,... | collective-permute-start | bytes 36872 | tf_op jit(solution)/shard_map/ppermute | solution.py:522
  27.2 0.0 collective-permute-done.4.side_a
  27.2 1.9 %collective-permute-done.5.side_b = f32[24,128]{1,0:T(8,128)S(1)} collective-permute-done((f32[24,128]{1,0:T(8,128)S(1)}, f32[24,128]{1,0:T(8,128)S(1)}, u32[]{:S(2)}, u32[]{:S(2)}) %collective-permute-start.5) | collective-permute-done | bytes 12320 | tf_op jit(solution)/shard_map/ppermute | solution.py:522
  29.2 3.7 %collective-permute-start.6 = (f32[104,128]{1,0:T(8,128)S(1)}, f32[104,128]{1,0:T(8,128)S(1)}, u32[]{:S(2)}, u32[]{:S(2)}) collective-permute-start(f32[104,128]{1,0:T(8,128)S(1)} %parcel.1), channel_id=1, source_target_pairs={{0,28},{1,29},{2,30},{3,31},{4,8},{5,9},{6,10},{7,11},{8,4},{9,5},... | collective-permute-start | bytes 159752 | tf_op jit(solution)/shard_map/ppermute | solution.py:522
  32.9 0.0 collective-permute-start.7
  32.9 0.4 right_side.1
  33.3 2.8 %collective-permute-done.6.height_b = f32[104,128]{1,0:T(8,128)S(1)} collective-permute-done((f32[104,128]{1,0:T(8,128)S(1)}, f32[104,128]{1,0:T(8,128)S(1)}, u32[]{:S(2)}, u32[]{:S(2)}) %collective-permute-start.6) | collective-permute-done | bytes 53280 | tf_op jit(solution)/shard_map/ppermute | solution.py:522
  36.1 0.9 %collective-permute-done.7.height_a = f32[104,128]{1,0:T(8,128)S(1)} collective-permute-done((f32[104,128]{1,0:T(8,128)S(1)}, f32[104,128]{1,0:T(8,128)S(1)}, u32[]{:S(2)}, u32[]{:S(2)}) %collective-permute-start.7) | collective-permute-done | bytes 53280 | tf_op jit(solution)/shard_map/ppermute | solution.py:522
  37.0 0.0 collective-permute-done.8.face_a
  37.0 0.0 collective-permute-done.9.face_b
  37.0 0.8 %products.1 = (f32[2,64,512]{2,1,0:T(8,128)S(1)}, f32[2,64,512]{2,1,0:T(8,128)S(1)}, f32[32,128]{1,0:T(8,128)S(1)}) custom-call(f32[104,128]{1,0:T(8,128)S(1)} %collective-permute-done.6.height_b, f32[104,128]{1,0:T(8,128)S(1)} %collective-permute-done.7.height_a, f32[2,64,512]{2,1,0:T(8,128)S(1)} %get-tuple-element.63.rhs_ref, ...), custom_call_target="tpu_custom_call" | custom-call | tf_op jit(solution)/shard_map/products/pallas_call | solution.py:929
  37.8 11.0 %all_to_all.11 = f32[32,1,128]{2,1,0:T(1,128)S(1)} all-to-all(f32[32,1,128]{2,1,0:T(1,128)S(1)} %bitcast.6), channel_id=1, replica_groups=mesh['height'=8,'cols'=4] {'height','cols'}, dimensions={0} | all-to-all | bytes 32768 | tf_op jit(solution)/shard_map/all_to_all | solution.py:1046
  48.8 1.2 %results.1 = (f32[3,2,8,128]{3,2,1,0:T(8,128)}, f32[3,2,8,128]{3,2,1,0:T(8,128)}, f32[2,64,512]{2,1,0:T(8,128)}, f32[2,64,512]{2,1,0:T(8,128)}) custom-call(f32[8,128]{1,0:T(8,128)S(1)} %get-tuple-element.40.keeps_ref, f32[8,8,128]{2,1,0:T(8,128)S(1)} %get-tuple-element.41.places_ref, f32[32,128]{1,0:T(8,128)S(1)} %bitcast.5, ...), custom_call_target="tpu_custom_call" | custom-call | tf_op jit(solution)/shard_map/results/pallas_call | solution.py:1000
  (3 shorter events, 0.0 us)
Async XLA Ops:
  0.6 0.7 %copy-start.4 = (s32[9,2,8]{0,2,1:T(8,128)S(1)}, s32[9,2,8]{0,2,1:T(8,128)}, u32[]{:S(2)}) copy-start(s32[9,2,8]{0,2,1:T(8,128)} %param.11) | copy-start | bytes 1732
  0.6 0.7 %copy-start.3 = (f32[3,2,8,128]{3,2,1,0:T(8,128)S(1)}, f32[3,2,8,128]{3,2,1,0:T(8,128)}, u32[]{:S(2)}) copy-start(f32[3,2,8,128]{3,2,1,0:T(8,128)} %velocities_ref.1) | copy-start | bytes 73732
  0.7 0.7 %copy-start.5 = (s32[2,8,128]{2,1,0:T(8,128)S(1)}, s32[2,8,128]{2,1,0:T(8,128)}, u32[]{:S(2)}) copy-start(s32[2,8,128]{2,1,0:T(8,128)} %slots_in.1) | copy-start | bytes 24580
  0.7 1.0 %copy-start = (f32[2,64,512]{2,1,0:T(8,128)S(1)}, f32[2,64,512]{2,1,0:T(8,128)}, u32[]{:S(2)}) copy-start(f32[2,64,512]{2,1,0:T(8,128)} %gas_ref.1) | copy-start | bytes 786436
  0.7 1.0 %copy-start.1 = (f32[2,64,512]{2,1,0:T(8,128)S(1)}, f32[2,64,512]{2,1,0:T(8,128)}, u32[]{:S(2)}) copy-start(f32[2,64,512]{2,1,0:T(8,128)} %diagonal_ref.1) | copy-start | bytes 786436
  0.7 1.0 %copy-start.2 = (f32[3,2,8,128]{3,2,1,0:T(8,128)S(1)}, f32[3,2,8,128]{3,2,1,0:T(8,128)}, u32[]{:S(2)}) copy-start(f32[3,2,8,128]{3,2,1,0:T(8,128)} %positions_ref.1) | copy-start | bytes 73732
  0.7 1.0 %copy-start.7 = (s32[2,8]{1,0:T(2,128)S(1)}, s32[2,8]{1,0:T(2,128)}, u32[]{:S(2)}) copy-start(s32[2,8]{1,0:T(2,128)} %owners_ref.1) | copy-start | bytes 196
  0.7 1.0 %copy-start.6 = (s32[2,8]{1,0:T(2,128)S(1)}, s32[2,8]{1,0:T(2,128)}, u32[]{:S(2)}) copy-start(s32[2,8]{1,0:T(2,128)} %exits_ref.1) | copy-start | bytes 196
  0.7 1.0 %copy-start.8 = (s32[1,8]{1,0:T(1,128)S(1)}, s32[1,8]{1,0:T(1,128)}, u32[]{:S(2)}) copy-start(s32[1,8]{1,0:T(1,128)} %inlets_ref.1) | copy-start | bytes 100
  1.9 3.8 %collective-permute-start = (f32[64,128]{1,0:T(8,128)S(1)}, f32[64,128]{1,0:T(8,128)S(1)}, u32[]{:S(2)}, u32[]{:S(2)}) collective-permute-start(f32[64,128]{1,0:T(8,128)S(1)} %get-tuple-element.43), channel_id=1, source_target_pairs={{0,1},{1,0},{2,3},{3,2},{4,5},{5,4},{6,7},{7,6},{8,9},{9,8},{10,11... | collective-permute-start | bytes 98312 | tf_op jit(solution)/shard_map/ppermute | solution.py:1025
  2.4 4.3 %collective-permute-start.1 = (f32[64,128]{1,0:T(8,128)S(1)}, f32[64,128]{1,0:T(8,128)S(1)}, u32[]{:S(2)}, u32[]{:S(2)}) collective-permute-start(f32[64,128]{1,0:T(8,128)S(1)} %get-tuple-element.44), channel_id=1, source_target_pairs={{0,3},{1,2},{2,1},{3,0},{4,7},{5,6},{6,5},{7,4},{8,11},{9,10},{10,... | collective-permute-start | bytes 98312 | tf_op jit(solution)/shard_map/ppermute | solution.py:1025
  6.7 5.6 %collective-permute-start.2 = (f32[152,128]{1,0:T(8,128)S(1)}, f32[152,128]{1,0:T(8,128)S(1)}, u32[]{:S(2)}, u32[]{:S(2)}) collective-permute-start(f32[152,128]{1,0:T(8,128)S(1)} %merge.1.own_ref), channel_id=1, source_target_pairs={{0,4},{1,5},{2,6},{3,7},{4,0},{5,1},{6,2},{7,3},{8,12},{9,13},{10,... | collective-permute-start | bytes 233480 | tf_op jit(solution)/shard_map/ppermute | solution.py:522
  8.4 3.9 %collective-permute-start.3 = (f32[152,128]{1,0:T(8,128)S(1)}, f32[152,128]{1,0:T(8,128)S(1)}, u32[]{:S(2)}, u32[]{:S(2)}) collective-permute-start(f32[152,128]{1,0:T(8,128)S(1)} %merge.1.own_ref), channel_id=1, source_target_pairs={{0,1},{1,0},{2,3},{3,2},{4,8},{5,9},{6,10},{7,11},{8,4},{9,5},{10,... | collective-permute-start | bytes 233480 | tf_op jit(solution)/shard_map/ppermute | solution.py:522
  12.3 24.7 %collective-permute-start.8 = (f32[200,512]{1,0:T(8,128)S(1)}, f32[200,512]{1,0:T(8,128)S(1)}, u32[]{:S(2)}, u32[]{:S(2)}) collective-permute-start(f32[200,512]{1,0:T(8,128)S(1)} %get-tuple-element.67), channel_id=1, source_target_pairs={{0,4},{1,5},{2,6},{3,7},{4,0},{5,1},{6,2},{7,3},{8,12},{9,13},{10,... | collective-permute-start | bytes 1228808 | tf_op jit(solution)/shard_map/ppermute | solution.py:1036
  15.1 22.0 %collective-permute-start.9 = (f32[200,512]{1,0:T(8,128)S(1)}, f32[200,512]{1,0:T(8,128)S(1)}, u32[]{:S(2)}, u32[]{:S(2)}) collective-permute-start(f32[200,512]{1,0:T(8,128)S(1)} %get-tuple-element.68), channel_id=1, source_target_pairs={{0,1},{1,0},{2,3},{3,2},{4,8},{5,9},{6,10},{7,11},{8,4},{9,5},{10,... | collective-permute-start | bytes 1228808 | tf_op jit(solution)/shard_map/ppermute | solution.py:1036
  25.5 1.8 %collective-permute-start.4 = (f32[24,128]{1,0:T(8,128)S(1)}, f32[24,128]{1,0:T(8,128)S(1)}, u32[]{:S(2)}, u32[]{:S(2)}) collective-permute-start(f32[24,128]{1,0:T(8,128)S(1)} %get-tuple-element.59.shared_ref), channel_id=1, source_target_pairs={{0,1},{1,0},{2,3},{3,2},{4,5},{5,4},{6,7},{7,6},{8,9},{9,8},{10,11... | collective-permute-start | bytes 36872 | tf_op jit(solution)/shard_map/ppermute | solution.py:522
  26.0 3.1 %collective-permute-start.5 = (f32[24,128]{1,0:T(8,128)S(1)}, f32[24,128]{1,0:T(8,128)S(1)}, u32[]{:S(2)}, u32[]{:S(2)}) collective-permute-start(f32[24,128]{1,0:T(8,128)S(1)} %get-tuple-element.59.shared_ref), channel_id=1, source_target_pairs={{0,3},{1,2},{2,1},{3,0},{4,7},{5,6},{6,5},{7,4},{8,11},{9,10},{10,... | collective-permute-start | bytes 36872 | tf_op jit(solution)/shard_map/ppermute | solution.py:522
  29.2 6.9 %collective-permute-start.6 = (f32[104,128]{1,0:T(8,128)S(1)}, f32[104,128]{1,0:T(8,128)S(1)}, u32[]{:S(2)}, u32[]{:S(2)}) collective-permute-start(f32[104,128]{1,0:T(8,128)S(1)} %parcel.1), channel_id=1, source_target_pairs={{0,28},{1,29},{2,30},{3,31},{4,8},{5,9},{6,10},{7,11},{8,4},{9,5},... | collective-permute-start | bytes 159752 | tf_op jit(solution)/shard_map/ppermute | solution.py:522
  32.9 4.1 %collective-permute-start.7 = (f32[104,128]{1,0:T(8,128)S(1)}, f32[104,128]{1,0:T(8,128)S(1)}, u32[]{:S(2)}, u32[]{:S(2)}) collective-permute-start(f32[104,128]{1,0:T(8,128)S(1)} %parcel.1), channel_id=1, source_target_pairs={{0,4},{1,5},{2,6},{3,7},{4,0},{5,1},{6,2},{7,3},{8,12},{9,13},{10,... | collective-permute-start | bytes 159752 | tf_op jit(solution)/shard_map/ppermute | solution.py:522

commit v9 on v7

--- a/solution.py
+++ b/solution.py
@@ -315,7 +315,7 @@
         pulled[DEPTH + r] = own_pulled[r]
 
     def substeps(*refs):
-        nears, founds = emptied(refs)
+        nears, founds = refs[:NEARS], refs[NEARS:]
         sources = dict(turned=lambda row: turned.at[row], pulled=lambda row: pulled.at[row], nears=nears, founds=founds)
         columns = list(range(1, wide - 1, 2))
 

time: 50.3 us -> 50.2 us (level)
  no operation moved by 1% of the time
where the time goes in v9:
time: 50.2 us; the launch traced here: 50 us
  Pallas kernels  17.1 us (34%)
  starting transfers between devices  13.2 us (26%)
  blocking collectives  10.8 us (22%)
  waiting for transfers between devices  7.05 us (14%)
  local copies, waits for them, and re-layouts  1 us (2%)
  between operations  0.78 us (2%)
    all_to_all x1, blocking collectives, on_device(): dots = lax.all_to_all(dots, ('height', 'cols'), 0, 0, tiled=True)  10.8 us
    pallas_call x1, Pallas kernels, particles(): pl.pallas_call(functools.partial(particles_kernel, rows=rows, cols=cols),...  9.92 us
    ppermute x6, starting transfers between devices, exchanged(): lax.ppermute(value, ('height', 'cols'), matching(heights, groups, axis, o...  7.3 us
    ppermute x6, waiting for transfers between devices, exchanged(): lax.ppermute(value, ('height', 'cols'), matching(heights, groups, axis, o...  6.09 us
    pallas_call x1, Pallas kernels, own_sums(): pl.pallas_call(functools.partial(own_kernel, rows=rows, cols=cols), out_s...  3.26 us
    ppermute x2, starting transfers between devices, on_device(): lax.ppermute(value, ('height', 'cols'), matching(heights, groups, 'cols',...  3.12 us
    ppermute x2, starting transfers between devices, on_device(): lax.ppermute(value, ('height', 'cols'), matching(heights, groups, 'height...  2.76 us
    pallas_call x1, Pallas kernels, results_of(): pl.pallas_call(results_kernel, out_shape=(particle, particle, field, fiel...  1.15 us
  transfers between devices with their start and end apart: 10, of which 5 were waited for; matrix products, arithmetic and copies ran while one was open for 0% of the time, Pallas kernels for 30%

profile of v9, /device:TPU:0, one launch (start us, length us, event | category | flops | bytes accessed | tf_op | source)
XLA Modules:
  0.0 50.0 jit_solution(10801468149645123343)
XLA Ops:
  0.6 0.0 copy-start.4
  0.6 0.0 copy-start.3
  0.7 0.0 copy-start.5
  0.7 0.0 copy-start
  0.7 0.0 copy-start.1
  0.7 0.0 copy-start.2
  0.7 0.0 copy-start.7
  0.7 0.0 copy-start.6
  0.7 0.0 copy-start.8
  0.7 0.6 %copy-done.4 = s32[9,2,8]{0,2,1:T(8,128)S(1)} copy-done((s32[9,2,8]{0,2,1:T(8,128)S(1)}, s32[9,2,8]{0,2,1:T(8,128)}, u32[]{:S(2)}) %copy-start.4) | copy-done | bytes 600
  1.3 0.1 copy-done.3
  1.4 0.0 copy-done.5
  1.4 0.2 copy-done
  1.6 0.1 copy-done.1
  1.7 0.0 copy-done.2
  1.7 0.0 copy-done.7
  1.7 0.0 copy-done.6
  1.7 0.0 copy-done.8
  1.7 0.2 pack.1
  1.9 0.5 collective-permute-start
  2.4 2.6 %collective-permute-start.1 = (f32[64,128]{1,0:T(8,128)S(1)}, f32[64,128]{1,0:T(8,128)S(1)}, u32[]{:S(2)}, u32[]{:S(2)}) collective-permute-start(f32[64,128]{1,0:T(8,128)S(1)} %get-tuple-element.44), channel_id=1, source_target_pairs={{0,3},{1,2},{2,1},{3,0},{4,7},{5,6},{6,5},{7,4},{8,11},{9,10},{10,... | collective-permute-start | bytes 98312 | tf_op jit(solution)/shard_map/ppermute | solution.py:1001
  5.0 0.7 %marks.1 = (f32[8,8,128]{2,1,0:T(8,128)S(1)}, f32[8,128]{1,0:T(8,128)S(1)}, f32[8,8,128]{2,1,0:T(8,128)S(1)}, f32[16,128]{1,0:T(8,128)S(1)}, f32[1,128]{1,0:T(1,128)S(1)}) custom-call(s32[1,128]{1,0:T(1,128)S(1)} %get-tuple-element.38.ints_ref, f32[2,2,64,512]{3,2,1,0:T(8,128)S(1)} %get-tuple-element.39.cells_ref), custom_call_target="tpu_custom_call" | custom-call | flops 1000000000 | bytes 4096 | tf_op jit(solution)/shard_map/marks/pallas_call | solution.py:476
  5.7 0.0 collective-permute-done.line_a
  5.7 1.0 %collective-permute-done.1.line_b = f32[64,128]{1,0:T(8,128)S(1)} collective-permute-done((f32[64,128]{1,0:T(8,128)S(1)}, f32[64,128]{1,0:T(8,128)S(1)}, u32[]{:S(2)}, u32[]{:S(2)}) %collective-permute-start.1) | collective-permute-done | bytes 32800 | tf_op jit(solution)/shard_map/ppermute | solution.py:1001
  6.7 1.7 %collective-permute-start.2 = (f32[152,128]{1,0:T(8,128)S(1)}, f32[152,128]{1,0:T(8,128)S(1)}, u32[]{:S(2)}, u32[]{:S(2)}) collective-permute-start(f32[152,128]{1,0:T(8,128)S(1)} %merge.1.own_ref), channel_id=1, source_target_pairs={{0,4},{1,5},{2,6},{3,7},{4,0},{5,1},{6,2},{7,3},{8,12},{9,13},{10,... | collective-permute-start | bytes 233480 | tf_op jit(solution)/shard_map/ppermute | solution.py:522
  8.4 0.2 collective-permute-start.3
  8.5 3.3 %own_sums.1 = (f32[2,12,8,128]{3,2,1,0:T(8,128)S(1)}, bf16[2,3,128,128]{3,2,1,0:T(8,128)(2,1)S(1)}, bf16[2,12,16,128]{3,2,1,0:T(8,128)(2,1)S(1)}, f32[2,5,16,256]{3,2,1,0:T(8,128)S(1)}) custom-call(f32[152,128]{1,0:T(8,128)S(1)} %merge.1.own_ref), custom_call_target="tpu_custom_call" | custom-call | flops 4000000000 | bytes 4096 | tf_op jit(solution)/shard_map/own_sums/pallas_call | solution.py:270
  11.8 0.3 faces.1
  12.1 0.2 collective-permute-done.2.first_ref
  12.3 0.0 collective-permute-done.3.second_ref
  12.3 2.8 %collective-permute-start.8 = (f32[200,512]{1,0:T(8,128)S(1)}, f32[200,512]{1,0:T(8,128)S(1)}, u32[]{:S(2)}, u32[]{:S(2)}) collective-permute-start(f32[200,512]{1,0:T(8,128)S(1)} %get-tuple-element.67), channel_id=1, source_target_pairs={{0,4},{1,5},{2,6},{3,7},{4,0},{5,1},{6,2},{7,3},{8,12},{9,13},{10,... | collective-permute-start | bytes 1228808 | tf_op jit(solution)/shard_map/ppermute | solution.py:1012
  15.1 0.0 collective-permute-start.9
  15.1 9.9 %particles.1 = (f32[2,8,8,128]{3,2,1,0:T(8,128)S(1)}, f32[6,8,128]{2,1,0:T(8,128)S(1)}) custom-call(f32[8,8,128]{2,1,0:T(8,128)S(1)} %get-tuple-element.42.picks_ref, f32[152,128]{1,0:T(8,128)S(1)} %collective-permute-done.2.first_ref, f32[152,128]{1,0:T(8,128)S(1)} %collective-permute-done.3.second_ref, f32[2,12,8,128]{3,2,1,0:T(8,128)S(1)} %get-tuple-element.52.own_ref, ...), custom_call_target="tpu_custom_call" | custom-call | flops 10000000000 | bytes 4096 | tf_op jit(solution)/shard_map/particles/pallas_call | solution.py:388
  25.0 0.4 deposits.1
  25.4 0.6 %collective-permute-start.4 = (f32[24,128]{1,0:T(8,128)S(1)}, f32[24,128]{1,0:T(8,128)S(1)}, u32[]{:S(2)}, u32[]{:S(2)}) collective-permute-start(f32[24,128]{1,0:T(8,128)S(1)} %get-tuple-element.59.shared_ref), channel_id=1, source_target_pairs={{0,1},{1,0},{2,3},{3,2},{4,5},{5,4},{6,7},{7,6},{8,9},{9,8},{10,11... | collective-permute-start | bytes 36872 | tf_op jit(solution)/shard_map/ppermute | solution.py:522
  26.0 1.2 %collective-permute-start.5 = (f32[24,128]{1,0:T(8,128)S(1)}, f32[24,128]{1,0:T(8,128)S(1)}, u32[]{:S(2)}, u32[]{:S(2)}) collective-permute-start(f32[24,128]{1,0:T(8,128)S(1)} %get-tuple-element.59.shared_ref), channel_id=1, source_target_pairs={{0,3},{1,2},{2,1},{3,0},{4,7},{5,6},{6,5},{7,4},{8,11},{9,10},{10,... | collective-permute-start | bytes 36872 | tf_op jit(solution)/shard_map/ppermute | solution.py:522
  27.2 0.0 collective-permute-done.4.side_a
  27.2 1.9 %collective-permute-done.5.side_b = f32[24,128]{1,0:T(8,128)S(1)} collective-permute-done((f32[24,128]{1,0:T(8,128)S(1)}, f32[24,128]{1,0:T(8,128)S(1)}, u32[]{:S(2)}, u32[]{:S(2)}) %collective-permute-start.5) | collective-permute-done | bytes 12320 | tf_op jit(solution)/shard_map/ppermute | solution.py:522
  29.1 3.7 %collective-permute-start.6 = (f32[120,128]{1,0:T(8,128)S(1)}, f32[120,128]{1,0:T(8,128)S(1)}, u32[]{:S(2)}, u32[]{:S(2)}) collective-permute-start(f32[120,128]{1,0:T(8,128)S(1)} %pad_maximum_fusion), channel_id=1, source_target_pairs={{0,28},{1,29},{2,30},{3,31},{4,8},{5,9},{6,10},{7,11},{8,4},{9,5},... | collective-permute-start | bytes 184328 | tf_op jit(solution)/shard_map/ppermute | solution.py:522
  32.8 0.0 collective-permute-start.7
  32.8 0.4 right_side.1
  33.2 2.9 %collective-permute-done.6.height_b = f32[120,128]{1,0:T(8,128)S(1)} collective-permute-done((f32[120,128]{1,0:T(8,128)S(1)}, f32[120,128]{1,0:T(8,128)S(1)}, u32[]{:S(2)}, u32[]{:S(2)}) %collective-permute-start.6) | collective-permute-done | bytes 61472 | tf_op jit(solution)/shard_map/ppermute | solution.py:522
  36.1 1.1 %collective-permute-done.7.height_a = f32[120,128]{1,0:T(8,128)S(1)} collective-permute-done((f32[120,128]{1,0:T(8,128)S(1)}, f32[120,128]{1,0:T(8,128)S(1)}, u32[]{:S(2)}, u32[]{:S(2)}) %collective-permute-start.7) | collective-permute-done | bytes 61472 | tf_op jit(solution)/shard_map/ppermute | solution.py:522
  37.2 0.0 collective-permute-done.8.face_a
  37.2 0.0 collective-permute-done.9.face_b
  37.2 0.8 %products.1 = (f32[2,64,512]{2,1,0:T(8,128)S(1)}, f32[2,64,512]{2,1,0:T(8,128)S(1)}, f32[32,128]{1,0:T(8,128)S(1)}) custom-call(f32[120,128]{1,0:T(8,128)S(1)} %collective-permute-done.6.height_b, f32[120,128]{1,0:T(8,128)S(1)} %collective-permute-done.7.height_a, f32[2,64,512]{2,1,0:T(8,128)S(1)} %get-tuple-element.63.rhs_ref, ...), custom_call_target="tpu_custom_call" | custom-call | tf_op jit(solution)/shard_map/products/pallas_call | solution.py:905
  38.0 10.8 %all_to_all.11 = f32[32,1,128]{2,1,0:T(1,128)S(1)} all-to-all(f32[32,1,128]{2,1,0:T(1,128)S(1)} %bitcast.8), channel_id=1, replica_groups=mesh['height'=8,'cols'=4] {'height','cols'}, dimensions={0} | all-to-all | bytes 32768 | tf_op jit(solution)/shard_map/all_to_all | solution.py:1022
  48.8 1.2 %results.1 = (f32[3,2,8,128]{3,2,1,0:T(8,128)}, f32[3,2,8,128]{3,2,1,0:T(8,128)}, f32[2,64,512]{2,1,0:T(8,128)}, f32[2,64,512]{2,1,0:T(8,128)}) custom-call(f32[8,128]{1,0:T(8,128)S(1)} %get-tuple-element.40.keeps_ref, f32[8,8,128]{2,1,0:T(8,128)S(1)} %get-tuple-element.41.places_ref, f32[32,128]{1,0:T(8,128)S(1)} %bitcast.6, ...), custom_call_target="tpu_custom_call" | custom-call | tf_op jit(solution)/shard_map/results/pallas_call | solution.py:976
  (3 shorter events, 0.0 us)
Async XLA Ops:
  0.6 0.7 %copy-start.4 = (s32[9,2,8]{0,2,1:T(8,128)S(1)}, s32[9,2,8]{0,2,1:T(8,128)}, u32[]{:S(2)}) copy-start(s32[9,2,8]{0,2,1:T(8,128)} %param.11) | copy-start | bytes 1732
  0.6 0.7 %copy-start.3 = (f32[3,2,8,128]{3,2,1,0:T(8,128)S(1)}, f32[3,2,8,128]{3,2,1,0:T(8,128)}, u32[]{:S(2)}) copy-start(f32[3,2,8,128]{3,2,1,0:T(8,128)} %velocities_ref.1) | copy-start | bytes 73732
  0.7 0.7 %copy-start.5 = (s32[2,8,128]{2,1,0:T(8,128)S(1)}, s32[2,8,128]{2,1,0:T(8,128)}, u32[]{:S(2)}) copy-start(s32[2,8,128]{2,1,0:T(8,128)} %slots_in.1) | copy-start | bytes 24580
  0.7 1.0 %copy-start = (f32[2,64,512]{2,1,0:T(8,128)S(1)}, f32[2,64,512]{2,1,0:T(8,128)}, u32[]{:S(2)}) copy-start(f32[2,64,512]{2,1,0:T(8,128)} %gas_ref.1) | copy-start | bytes 786436
  0.7 1.0 %copy-start.1 = (f32[2,64,512]{2,1,0:T(8,128)S(1)}, f32[2,64,512]{2,1,0:T(8,128)}, u32[]{:S(2)}) copy-start(f32[2,64,512]{2,1,0:T(8,128)} %diagonal_ref.1) | copy-start | bytes 786436
  0.7 1.0 %copy-start.2 = (f32[3,2,8,128]{3,2,1,0:T(8,128)S(1)}, f32[3,2,8,128]{3,2,1,0:T(8,128)}, u32[]{:S(2)}) copy-start(f32[3,2,8,128]{3,2,1,0:T(8,128)} %positions_ref.1) | copy-start | bytes 73732
  0.7 1.0 %copy-start.7 = (s32[2,8]{1,0:T(2,128)S(1)}, s32[2,8]{1,0:T(2,128)}, u32[]{:S(2)}) copy-start(s32[2,8]{1,0:T(2,128)} %owners_ref.1) | copy-start | bytes 196
  0.7 1.0 %copy-start.6 = (s32[2,8]{1,0:T(2,128)S(1)}, s32[2,8]{1,0:T(2,128)}, u32[]{:S(2)}) copy-start(s32[2,8]{1,0:T(2,128)} %exits_ref.1) | copy-start | bytes 196
  0.7 1.0 %copy-start.8 = (s32[1,8]{1,0:T(1,128)S(1)}, s32[1,8]{1,0:T(1,128)}, u32[]{:S(2)}) copy-start(s32[1,8]{1,0:T(1,128)} %inlets_ref.1) | copy-start | bytes 100
  1.9 3.8 %collective-permute-start = (f32[64,128]{1,0:T(8,128)S(1)}, f32[64,128]{1,0:T(8,128)S(1)}, u32[]{:S(2)}, u32[]{:S(2)}) collective-permute-start(f32[64,128]{1,0:T(8,128)S(1)} %get-tuple-element.43), channel_id=1, source_target_pairs={{0,1},{1,0},{2,3},{3,2},{4,5},{5,4},{6,7},{7,6},{8,9},{9,8},{10,11... | collective-permute-start | bytes 98312 | tf_op jit(solution)/shard_map/ppermute | solution.py:1001
  2.4 4.3 %collective-permute-start.1 = (f32[64,128]{1,0:T(8,128)S(1)}, f32[64,128]{1,0:T(8,128)S(1)}, u32[]{:S(2)}, u32[]{:S(2)}) collective-permute-start(f32[64,128]{1,0:T(8,128)S(1)} %get-tuple-element.44), channel_id=1, source_target_pairs={{0,3},{1,2},{2,1},{3,0},{4,7},{5,6},{6,5},{7,4},{8,11},{9,10},{10,... | collective-permute-start | bytes 98312 | tf_op jit(solution)/shard_map/ppermute | solution.py:1001
  6.7 5.6 %collective-permute-start.2 = (f32[152,128]{1,0:T(8,128)S(1)}, f32[152,128]{1,0:T(8,128)S(1)}, u32[]{:S(2)}, u32[]{:S(2)}) collective-permute-start(f32[152,128]{1,0:T(8,128)S(1)} %merge.1.own_ref), channel_id=1, source_target_pairs={{0,4},{1,5},{2,6},{3,7},{4,0},{5,1},{6,2},{7,3},{8,12},{9,13},{10,... | collective-permute-start | bytes 233480 | tf_op jit(solution)/shard_map/ppermute | solution.py:522
  8.4 3.9 %collective-permute-start.3 = (f32[152,128]{1,0:T(8,128)S(1)}, f32[152,128]{1,0:T(8,128)S(1)}, u32[]{:S(2)}, u32[]{:S(2)}) collective-permute-start(f32[152,128]{1,0:T(8,128)S(1)} %merge.1.own_ref), channel_id=1, source_target_pairs={{0,1},{1,0},{2,3},{3,2},{4,8},{5,9},{6,10},{7,11},{8,4},{9,5},{10,... | collective-permute-start | bytes 233480 | tf_op jit(solution)/shard_map/ppermute | solution.py:522
  12.3 24.9 %collective-permute-start.8 = (f32[200,512]{1,0:T(8,128)S(1)}, f32[200,512]{1,0:T(8,128)S(1)}, u32[]{:S(2)}, u32[]{:S(2)}) collective-permute-start(f32[200,512]{1,0:T(8,128)S(1)} %get-tuple-element.67), channel_id=1, source_target_pairs={{0,4},{1,5},{2,6},{3,7},{4,0},{5,1},{6,2},{7,3},{8,12},{9,13},{10,... | collective-permute-start | bytes 1228808 | tf_op jit(solution)/shard_map/ppermute | solution.py:1012
  15.1 22.1 %collective-permute-start.9 = (f32[200,512]{1,0:T(8,128)S(1)}, f32[200,512]{1,0:T(8,128)S(1)}, u32[]{:S(2)}, u32[]{:S(2)}) collective-permute-start(f32[200,512]{1,0:T(8,128)S(1)} %get-tuple-element.68), channel_id=1, source_target_pairs={{0,1},{1,0},{2,3},{3,2},{4,8},{5,9},{6,10},{7,11},{8,4},{9,5},{10,... | collective-permute-start | bytes 1228808 | tf_op jit(solution)/shard_map/ppermute | solution.py:1012
  25.4 1.8 %collective-permute-start.4 = (f32[24,128]{1,0:T(8,128)S(1)}, f32[24,128]{1,0:T(8,128)S(1)}, u32[]{:S(2)}, u32[]{:S(2)}) collective-permute-start(f32[24,128]{1,0:T(8,128)S(1)} %get-tuple-element.59.shared_ref), channel_id=1, source_target_pairs={{0,1},{1,0},{2,3},{3,2},{4,5},{5,4},{6,7},{7,6},{8,9},{9,8},{10,11... | collective-permute-start | bytes 36872 | tf_op jit(solution)/shard_map/ppermute | solution.py:522
  26.0 3.1 %collective-permute-start.5 = (f32[24,128]{1,0:T(8,128)S(1)}, f32[24,128]{1,0:T(8,128)S(1)}, u32[]{:S(2)}, u32[]{:S(2)}) collective-permute-start(f32[24,128]{1,0:T(8,128)S(1)} %get-tuple-element.59.shared_ref), channel_id=1, source_target_pairs={{0,3},{1,2},{2,1},{3,0},{4,7},{5,6},{6,5},{7,4},{8,11},{9,10},{10,... | collective-permute-start | bytes 36872 | tf_op jit(solution)/shard_map/ppermute | solution.py:522
  29.1 7.0 %collective-permute-start.6 = (f32[120,128]{1,0:T(8,128)S(1)}, f32[120,128]{1,0:T(8,128)S(1)}, u32[]{:S(2)}, u32[]{:S(2)}) collective-permute-start(f32[120,128]{1,0:T(8,128)S(1)} %pad_maximum_fusion), channel_id=1, source_target_pairs={{0,28},{1,29},{2,30},{3,31},{4,8},{5,9},{6,10},{7,11},{8,4},{9,5},... | collective-permute-start | bytes 184328 | tf_op jit(solution)/shard_map/ppermute | solution.py:522
  32.8 4.4 %collective-permute-start.7 = (f32[120,128]{1,0:T(8,128)S(1)}, f32[120,128]{1,0:T(8,128)S(1)}, u32[]{:S(2)}, u32[]{:S(2)}) collective-permute-start(f32[120,128]{1,0:T(8,128)S(1)} %pad_maximum_fusion), channel_id=1, source_target_pairs={{0,4},{1,5},{2,6},{3,7},{4,0},{5,1},{6,2},{7,3},{8,12},{9,13},{10,... | collective-permute-start | bytes 184328 | tf_op jit(solution)/shard_map/ppermute | solution.py:522
